TPU v7x, 128 devices: a whole 4x4x4 slice. The times are simulated.
128 devices in a mesh: row: 16 (over x, y_hi, core), col: 8 (over y_lo, z).
Axes of the slice: x: 4, y: 4 (y_hi: 2, y_lo: 2; y = y_hi * 2 + y_lo), z: 4, core: 2. Of those that a mesh axis runs over, the one named last changes fastest.
Arguments:
- pair: bfloat16 [768, 768, 128], P('row', 'col'), may hold values from -6 to 6
- residue_mask: int32 [768], replicated, may hold values 0 or 1
- left_weight: bfloat16 [128, 256], replicated, may hold values from -0.5 to 0.5
- right_weight: bfloat16 [128, 256], replicated, may hold values from -0.5 to 0.5
- gate_weight: bfloat16 [128, 128], replicated, may hold values from -0.5 to 0.5
- out_weight: bfloat16 [128, 128], replicated, may hold values from -0.5 to 0.5
- attn_weight: bfloat16 [128, 128], replicated, may hold values from -0.5 to 0.5
- bias_weight: bfloat16 [128], replicated
- attn_out_weight: bfloat16 [32, 128], replicated, may hold values from -1 to 1
Outputs:
- updated: bfloat16 [768, 768, 128], P('row', 'col')
All inputs are finite; a program needn't handle non-finite values.
Results may differ from a plain program's by a relative error of at most 0.035.
Values may be sent and summed in bfloat16 or wider, within the bound.
No kernel may reach another device: no remote copies, remote signals or barrier semaphores. Data moves between devices by JAX's collectives and lax.ppermute only.
A program may use at most 128 MiB of HBM per device.

v0:
```python
import math

import jax
import jax.numpy as jnp
from jax import lax
from jax.sharding import PartitionSpec as P


def layer_norm(values):
    center = values - jnp.mean(values, axis=-1, keepdims=True)
    spread = jnp.mean(center * center, axis=-1, keepdims=True)
    return center * lax.rsqrt(spread + 1e-05)


def gated_side(normed, weight, row_mask, col_mask, width):
    proj = jnp.dot(normed, weight, preferred_element_type=jnp.float32)
    value = jax.nn.sigmoid(proj[..., width:]) * proj[..., :width]
    return (value * row_mask[:, None, None] * col_mask[None, :, None]).astype(jnp.bfloat16)


def body(
    pair,
    residue_mask,
    left_weight,
    right_weight,
    gate_weight,
    out_weight,
    attn_weight,
    bias_weight,
    attn_out_weight,
):
    rows, cols, width = pair.shape
    head = attn_out_weight.shape[0]
    row_pos = lax.axis_index("row")
    col_pos = lax.axis_index("col")
    mvec = residue_mask.astype(jnp.float32)
    row_mask = lax.dynamic_slice_in_dim(mvec, row_pos * rows, rows)
    col_mask = lax.dynamic_slice_in_dim(mvec, col_pos * cols, cols)
    pair_f = pair.astype(jnp.float32)
    normed = layer_norm(pair_f).astype(jnp.bfloat16)
    left = gated_side(normed, left_weight, row_mask, col_mask, width)
    right = gated_side(normed, right_weight, row_mask, col_mask, width)
    gate = jax.nn.sigmoid(jnp.dot(normed, gate_weight, preferred_element_type=jnp.float32))
    right_all = lax.all_gather(right, "row", axis=0, tiled=True)
    summed = lax.psum_scatter(
        jnp.einsum("ikc,jkc->jic", left, right_all, preferred_element_type=jnp.float32),
        "col",
        scatter_dimension=0,
        tiled=True,
    )
    tri_sum = jnp.transpose(summed, (1, 0, 2))
    tri_normed = layer_norm(tri_sum).astype(jnp.bfloat16)
    first = pair_f + gate * jnp.dot(tri_normed, out_weight, preferred_element_type=jnp.float32)
    normed2 = layer_norm(first).astype(jnp.bfloat16)
    proj = jnp.dot(normed2, attn_weight, preferred_element_type=jnp.float32)
    query = proj[..., :head].astype(jnp.bfloat16)
    key_value = proj[..., head : 3 * head].astype(jnp.bfloat16)
    agate = proj[..., 3 * head :]
    bias_tile = jnp.dot(normed2, bias_weight, preferred_element_type=jnp.float32).astype(
        jnp.bfloat16
    )
    bias_cols = lax.all_gather(bias_tile, "col", axis=1, tiled=True)
    bias_all = lax.all_gather(bias_cols, "row", axis=0, tiled=True)
    bias_mine = lax.dynamic_slice_in_dim(bias_all, col_pos * cols, cols, 0)
    extra = bias_mine.astype(jnp.float32) + 1000000000.0 * (mvec[None, :] - 1.0)
    scale = 1.0 / math.sqrt(head)
    piece = lax.all_gather(key_value, "col", axis=1, tiled=True)
    top_score = jnp.full((rows, cols), -1e30, jnp.float32)
    key_part = piece[..., :head]
    value_part = piece[..., head:]
    scores = jnp.einsum("ijd,ild->ijl", query, key_part, preferred_element_type=jnp.float32) * scale
    scores = scores + extra[None, :, :]
    new_top = jnp.maximum(top_score, jnp.max(scores, axis=-1))
    expw = jnp.exp(scores - new_top[..., None])
    total = jnp.sum(expw, axis=-1)
    accum = jnp.einsum(
        "ijl,ild->ijd", expw.astype(jnp.bfloat16), value_part, preferred_element_type=jnp.float32
    )
    top_score, total, accum = (new_top, total, accum)
    attended = accum / total[..., None]
    gated = (jax.nn.sigmoid(agate) * attended).astype(jnp.bfloat16)
    return (first + jnp.dot(gated, attn_out_weight, preferred_element_type=jnp.float32)).astype(
        jnp.bfloat16
    )


def solution(mesh):
    return jax.shard_map(
        body,
        mesh=mesh,
        in_specs=(P("row", "col", None), P(), P(), P(), P(), P(), P(), P(), P()),
        out_specs=P("row", "col", None),
        check_vma=False,
    )
```

profile of v0, /device:TPU:1, one launch (start us, length us, event | category | flops | bytes accessed | tf_op | source)
XLA Modules:
  0.0 633.1 jit_solution(7487252900955826026)
XLA Ops:
  6.5 0.8 convert_element_type.40
  7.3 0.1 dynamic_slice.10
  7.4 0.1 dynamic_slice.9
  7.5 1.8 convert_reduce_fusion
  9.3 2.7 fusion.13
  12.0 0.0 copy-start.4
  12.0 3.0 fusion.54
  15.0 3.0 fusion.52
  18.0 2.7 fusion.17
  20.7 0.0 all-gather.5.cloned.1.call-update
  20.8 0.0 reduce-scatter.2.cloned.1.call-start
  20.8 2.0 copy.72
  22.8 121.6 %all-gather.5.cloned.1.call-done = bf16[768,96,128]{2,1,0:T(8,128)(2,1)} async-done(((bf16[48,96,128]{2,1,0:T(8,128)(2,1)}), bf16[768,96,128]{2,1,0:T(8,128)(2,1)}) %all-gather.5.cloned.1.call-update) | async-done | bytes 18874384 | tf_op jit(solution)/shard_map/all_gather | solution.py:44
  144.4 29.6 %copy.71 = bf16[768,96,128]{1,0,2:T(8,128)(2,1)} copy(bf16[768,96,128]{2,1,0:T(8,128)(2,1)} %all-gather.5.cloned.1.call-done) | data formatting | bytes 37748736 | tf_op jit(solution)/shard_map/all_gather | solution.py:44
  174.0 20.0 %convolution_bitcast_fusion = f32[768,48,128]{0,1,2:T(8,128)} fusion(bf16[768,96,128]{1,0,2:T(8,128)(2,1)} %copy.71, bf16[48,96,128]{1,0,2:T(8,128)(2,1)S(1)} %copy.72), kind=kOutput, calls=%fused_computation.9 | convolution fusion | flops 905969664 | bytes 38928384 | tf_op jit(solution)/shard_map/ikc,jkc->jic/dot_general | solution.py:46
  194.1 18.9 %copy.73 = f32[768,48,128]{2,1,0:T(8,128)} copy(f32[768,48,128]{0,1,2:T(8,128)} %convolution_bitcast_fusion) | data formatting | bytes 37748736 | tf_op jit(solution)/shard_map/ikc,jkc->jic/transpose | solution.py:46
  213.0 0.0 reduce-scatter.2.cloned.1.call-update
  213.0 0.0 all-gather.9.cloned.1.call-start
  213.1 0.7 copy-done.5
  213.8 3.0 fusion.56
  216.8 185.1 %reduce-scatter.2.cloned.1.call-done = f32[96,48,128]{2,1,0:T(8,128)} async-done(((f32[768,48,128]{2,1,0:T(8,128)}), f32[96,48,128]{2,1,0:T(8,128)}) %reduce-scatter.2.cloned.1.call-update) | async-done | bytes 2359312 | tf_op jit(solution)/shard_map/reduce_scatter | solution.py:45
  401.8 2.3 bitcast_reduce_fusion
  404.2 0.1 copy.74
  404.3 0.1 copy.75
  404.4 2.7 multiply_reduce_fusion.1
  407.1 0.0 copy-start.9
  407.1 0.1 copy.76
  407.2 0.1 copy.77
  407.3 3.2 multiply_convert_fusion.1
  410.5 2.8 fusion.72
  413.3 0.0 copy-start.8
  413.4 1.7 multiply_reduce_fusion
  415.1 2.0 fusion.60
  417.0 21.9 %all-gather = bf16[8,96,48]{1,2,0:T(8,128)(2,1)S(1)} all-gather(bf16[1,96,48]{1,2,0:T(8,128)(2,1)S(1)} %convert_bitcast_fusion), channel_id=1, replica_groups=mesh['row'=16,'col'=8] {'col'}, dimensions={0}, use_global_device_ids=true | all-gather | bytes 82944 | tf_op jit(solution)/shard_map/all_gather | solution.py:62
  438.9 0.8 reshape.47
  439.7 0.0 all-gather.9.cloned.1.call-update
  439.7 0.2 all-gather.7.cloned.1.call-start
  440.0 4.0 fusion.73
  443.9 1.4 slice.44
  445.3 0.0 all-gather.7.cloned.1.call-update
  445.4 3.7 slice.42
  449.1 2.3 copy.88
  451.4 39.2 %all-gather.9.cloned.1.call-done = bf16[768,768]{1,0:T(8,128)(2,1)} async-done(((bf16[48,768]{1,0:T(8,128)(2,1)}), bf16[768,768]{1,0:T(8,128)(2,1)}) %all-gather.9.cloned.1.call-update) | async-done | bytes 1179664 | tf_op jit(solution)/shard_map/all_gather | solution.py:63
  490.7 0.9 convert_add_fusion.1
  491.6 100.9 %all-gather.7.cloned.1.call-done = bf16[48,768,64]{2,1,0:T(8,128)(2,1)} async-done(((bf16[48,96,64]{2,1,0:T(8,128)(2,1)}), bf16[48,768,64]{2,1,0:T(8,128)(2,1)}) %all-gather.7.cloned.1.call-update) | async-done | bytes 4718608 | tf_op jit(solution)/shard_map/all_gather | solution.py:67
  592.5 11.8 %fusion = (f32[48,96]{1,0:T(8,128)S(1)}, f32[48,96,768]{2,1,0:T(8,128)}) fusion(f32[96,768]{1,0:T(8,128)S(1)} %convert_add_fusion.1, bf16[48,768,64]{2,1,0:T(8,128)(2,1)} %all-gather.7.cloned.1.call-done, bf16[48,96,128]{2,1,0:T(8,128)(2,1)S(1)} %get-tuple-element.9), kind=kOutput, calls=%fused_computation.2 | convolution fusion | flops 237104640 | bytes 20367360 | tf_op jit(solution)/shard_map/ijd,ild->ijl/dot_general | solution.py:71
  604.4 7.1 %fusion.1 = f32[48,96]{1,0:T(8,128)S(1)} fusion(f32[48,96,768]{2,1,0:T(8,128)} %get-tuple-element.12, f32[48,96]{1,0:T(8,128)S(1)} %broadcast_maximum_fusion, f32[96,768]{1,0:T(8,128)S(1)} %convert_add_fusion.1), kind=kLoop, calls=%fused_computation.3 | loop fusion | flops 14151168 | bytes 14487552 | tf_op jit(solution)/shard_map/reduce_sum | solution.py:75
  611.5 15.0 %add_convert_fusion = bf16[48,96,128]{2,1,0:T(8,128)(2,1)} fusion(f32[48,96,128]{2,1,0:T(8,128)} %copy-done.3, bf16[48,768,64]{2,1,0:T(8,128)(2,1)} %all-gather.7.cloned.1.call-done, f32[48,96,768]{2,1,0:T(8,128)} %get-tuple-element.12, f32[48,96]{1,0:T(8,128)S(1)} %broadcast_maximum_fusion, f32[96,768]{1,0:T(8,128)S(1)} %convert_add_fusion.1, ...), kind=kOutput, calls=%fused_computation.38 | convolution fusion | flops 280461312 | bytes 23343104 | tf_op jit(solution)/shard_map/dot_general | solution.py:82
  (29 shorter events, 0.2 us)
Async XLA Ops:
  6.5 5.4 copy-start
  6.5 5.5 copy-start.2
  6.5 137.9 %all-gather.5.cloned.1.call-start = ((), (), s32[]{:S(2)}) async-start(), calls=%async_computation.1 | async-start | bytes 20054016 | tf_op jit(solution)/shard_map/all_gather | solution.py:44
  12.0 3.0 copy-start.4
  20.8 381.1 %reduce-scatter.2.cloned.1.call-start = ((), (), s32[]{:S(2)}) async-start(), calls=%async_computation.2 | async-start | bytes 21233664 | tf_op jit(solution)/shard_map/reduce_scatter | solution.py:45
  213.0 0.8 copy-start.5
  213.0 277.6 %all-gather.9.cloned.1.call-start = ((), (), s32[]{:S(2)}) async-start(), calls=%async_computation.4 | async-start | bytes 1253376 | tf_op jit(solution)/shard_map/all_gather | solution.py:63
  407.1 3.4 copy-start.9
  413.3 3.7 copy-start.3
  413.3 1.7 copy-start.8
  413.3 26.6 %copy-start.6 = (bf16[128,128]{1,0:T(8,128)(2,1)S(1)}, bf16[128,128]{1,0:T(8,128)(2,1)}, u32[]{:S(2)}) copy-start(bf16[128,128]{1,0:T(8,128)(2,1)} %param.15) | copy-start | bytes 98308
  439.7 152.8 %all-gather.7.cloned.1.call-start = ((), (), s32[]{:S(2)}) async-start(), calls=%async_computation.3 | async-start | bytes 10616832 | tf_op jit(solution)/shard_map/all_gather | solution.py:67
  443.9 1.4 copy-start.7
  604.4 7.2 %copy-start.10 = (bf16[32,128]{1,0:T(8,128)(2,1)S(1)}, bf16[32,128]{1,0:T(8,128)(2,1)}, u32[]{:S(2)}) copy-start(bf16[32,128]{1,0:T(8,128)(2,1)} %param.17) | copy-start | bytes 24580
  611.5 15.0 %copy-start.1 = (bf16[128,256]{1,0:T(8,128)(2,1)S(1)}, bf16[128,256]{1,0:T(8,128)(2,1)}, u32[]{:S(2)}) copy-start(bf16[128,256]{1,0:T(8,128)(2,1)} %param.12) | copy-start | bytes 196612
Sparse Core Ops, SparseCore 0:
  20.9 123.5 all-gather.4
  213.2 188.6 reduce-scatter.1
  439.8 50.7 all-gather.8
  492.2 100.3 all-gather.6
where the time goes:
time: 635 us; the launch traced here: 633 us
  waiting for transfers between devices  447 us (70%)
  matrix products  64.6 us (10%)
  local copies, waits for them, and re-layouts  59.9 us (9%)
  other arithmetic  26.1 us (4%)
  blocking collectives  21.9 us (3%)
  between operations  13.4 us (2%)
    reduce_scatter x1, waiting for transfers between devices, body(): lax.psum_scatter(jnp.einsum('ikc,jkc->jic', left, right_all, preferred_el...  185 us
    all_gather x1, waiting for transfers between devices, body(): right_all = lax.all_gather(right, 'row', axis=0, tiled=True)  122 us
    all_gather x1, waiting for transfers between devices, body(): piece = lax.all_gather(key_value, 'col', axis=1, tiled=True)  101 us
    all_gather x1, waiting for transfers between devices, body(): bias_all = lax.all_gather(bias_cols, 'row', axis=0, tiled=True)  39.2 us
    all_gather x1, local copies, waits for them, and re-layouts, body(): right_all = lax.all_gather(right, 'row', axis=0, tiled=True)  29.6 us
    all_gather x1, blocking collectives, body(): bias_cols = lax.all_gather(bias_tile, 'col', axis=1, tiled=True)  21.9 us
    dot_general x1, matrix products, body(): jnp.einsum('ikc,jkc->jic', left, right_all, preferred_element_type=jnp.fl...  20 us
    transpose x1, local copies, waits for them, and re-layouts, body(): jnp.einsum('ikc,jkc->jic', left, right_all, preferred_element_type=jnp.fl...  18.9 us
  transfers between devices with their start and end apart: 4, of which 4 were waited for; matrix products, arithmetic and copies ran while one was open for 3% of the time, Pallas kernels for 0%

commit v1 on v0

v1 whole, which is shorter than its diff:
```python
import functools
import math

import jax
import jax.numpy as jnp
from jax import lax
from jax.experimental import pallas as pl
from jax.experimental.pallas import tpu as pltpu
from jax.sharding import Mesh
from jax.sharding import PartitionSpec as P

F32 = jnp.float32
BF16 = jnp.bfloat16
LOG2E = math.log2(math.e)
ALL = ("x", "yh", "core", "yl", "z")
COL = ("yl", "z")
VMEM = pl.BlockSpec(memory_space=pltpu.VMEM)


def sigmoid(values):
    return 0.5 * jnp.tanh(0.5 * values) + 0.5


def layer_norm_rows(values):
    center = values - jnp.mean(values, axis=-1, keepdims=True)
    spread = jnp.mean(center * center, axis=-1, keepdims=True)
    return center * lax.rsqrt(spread + 1e-05)


def swap_blocks(parts):
    lane = lax.broadcasted_iota(jnp.int32, parts[0].shape, 1)
    odd = (lane // 32) % 2 == 1
    high = lane >= 64
    v0, v1, v2, v3 = parts
    a0 = jnp.where(odd, pltpu.roll(v1, 32, 1), v0)
    a1 = jnp.where(odd, v1, pltpu.roll(v0, 96, 1))
    a2 = jnp.where(odd, pltpu.roll(v3, 32, 1), v2)
    a3 = jnp.where(odd, v3, pltpu.roll(v2, 96, 1))
    return (
        jnp.where(high, pltpu.roll(a2, 64, 1), a0),
        jnp.where(high, pltpu.roll(a3, 64, 1), a1),
        jnp.where(high, a2, pltpu.roll(a0, 64, 1)),
        jnp.where(high, a3, pltpu.roll(a1, 64, 1)),
    )


def project_kernel(pair_ref, mask_ref, sides_ref, gate_w_ref, wire_ref, gate_ref, slab_ref):
    lane = lax.broadcasted_iota(jnp.int32, (128, 128), 1)

    def step(ii, carry):
        values = jnp.concatenate([pair_ref[s * 8 + ii] for s in range(6)], axis=0).astype(F32)
        normed = layer_norm_rows(values).astype(BF16)
        gate = jnp.dot(normed, gate_w_ref[...], preferred_element_type=F32)
        gate_ref[ii] = sigmoid(gate).astype(BF16)
        piece = lambda s, kc: normed[s * 96 + kc * 32 : s * 96 + kc * 32 + 32]
        for kc in range(3):
            rows = jnp.concatenate([piece(s, kc) for s in range(4)], axis=0)
            proj = lax.dot_general(
                sides_ref[...], rows, (((1,), (1,)), ((), ())), preferred_element_type=F32
            )
            left = sigmoid(proj[128:256]) * proj[0:128]
            right = sigmoid(proj[384:512]) * proj[256:384]
            slab_ref[pl.ds(pl.multiple_of((kc * 8 + ii) * 128, 128), 128), :] = left
            slab_ref[pl.ds(pl.multiple_of((24 + kc * 8 + ii) * 128, 128), 128), :] = right
        for kc in range(3):
            rows = jnp.concatenate([piece(s, kc) for s in (4, 5, 4, 5)], axis=0)
            proj = lax.dot_general(
                sides_ref[...], rows, (((1,), (1,)), ((), ())), preferred_element_type=F32
            )
            value = jnp.where(lane < 64, proj[0:128], proj[256:384])
            gating = jnp.where(lane < 64, proj[128:256], proj[384:512])
            slab_ref[pl.ds(pl.multiple_of((48 + kc * 8 + ii) * 128, 128), 128), :] = (
                sigmoid(gating) * value
            )
        return carry

    lax.fori_loop(0, 8, step, 0)

    def emit(ch, carry):
        wire_ref[ch] = (slab_ref[pl.ds(ch, 72, stride=128), :] * mask_ref[...]).astype(BF16)
        return carry

    lax.fori_loop(0, 128, emit, 0, unroll=4)


def triangle_kernel(wire_ref, out_ref, left_ref, right_ref, sums_ref):
    def unpack(c_pair, carry):
        for half in range(2):
            r = c_pair * 2 + half
            for yl in range(2):
                parts = [wire_ref[r * 8 + yl * 4 + z].astype(F32) for z in range(4)]
                w = swap_blocks(parts)
                for kc in range(3):
                    cols = pl.ds((yl * 3 + kc) * 128, 128)
                    at = lambda k, base: w[k][base + kc * 8 : base + kc * 8 + 8]
                    left = jnp.concatenate(
                        [at(s, 0) for s in range(4)] + [at(0, 48), at(1, 48)], axis=0
                    ).astype(BF16)
                    right = jnp.concatenate(
                        [at(s, 24) for s in range(4)] + [at(2, 48), at(3, 48)], axis=0
                    ).astype(BF16)
                    left_ref[pl.ds(pl.multiple_of(r * 48, 16), 48), cols] = left
                    for g3 in range(3):
                        g = half * 3 + g3
                        base = ((c_pair // 4) * 3 + g // 2) * 128 + (c_pair % 4) * 32 + (g % 2) * 16
                        right_ref[pl.ds(pl.multiple_of(base, 16), 16), cols] = right[
                            g3 * 16 : g3 * 16 + 16
                        ]
        return carry

    lax.fori_loop(0, 8, unpack, 0)
    for n in range(3):
        sums_ref[:, n * 256 : (n + 1) * 256] = lax.dot_general(
            left_ref[...],
            right_ref[n * 256 : (n + 1) * 256, :],
            (((1,), (1,)), ((), ())),
            preferred_element_type=F32,
        )

    def pack(r, carry):
        base = pl.multiple_of(r * 48, 16)
        rows = [sums_ref[pl.ds(pl.multiple_of(base + s * 8, 8), 8), :] for s in range(6)]
        for yl in range(2):
            tile = lambda s, jc: rows[s][:, (yl * 3 + jc) * 128 : (yl * 3 + jc + 1) * 128]
            outs = [swap_blocks([tile(s, jc) for s in range(4)]) for jc in range(3)]
            outs.append(swap_blocks([tile(4, 0), tile(5, 0), tile(4, 1), tile(5, 1)]))
            outs.append(swap_blocks([tile(4, 2), tile(5, 2), tile(4, 2), tile(5, 2)]))
            for z in range(4):
                out_ref[r * 8 + yl * 4 + z] = jnp.concatenate([o[z] for o in outs], axis=0).astype(
                    BF16
                )
        return carry

    lax.fori_loop(0, 16, pack, 0)


def first_kernel(
    wire_ref, pair_ref, gate_ref, out_w_ref, attn_w_ref, bias_w_ref, first_ref, send_ref, norm_ref, bias_ref
):
    def add(ch, total):
        return total + wire_ref[ch].astype(F32)

    zero = jnp.zeros((40, 128), F32)
    mean = lax.fori_loop(0, 128, add, zero, unroll=8) * (1.0 / 128)

    def add_square(ch, total):
        center = wire_ref[ch].astype(F32) - mean
        return total + center * center

    spread = lax.fori_loop(0, 128, add_square, zero, unroll=8) * (1.0 / 128)
    scale = lax.rsqrt(spread + 1e-05)

    def write(ch, carry):
        norm_ref[pl.ds(pl.multiple_of(ch * 40, 8), 40), :] = (
            wire_ref[ch].astype(F32) - mean
        ) * scale
        return carry

    lax.fori_loop(0, 128, write, 0, unroll=8)

    lane = lax.broadcasted_iota(jnp.int32, (1, 128), 1)
    query_scale = jnp.where(lane < 32, LOG2E / math.sqrt(32), 1.0)

    def step(ii, carry):
        slabs = []
        for base in (0, 8, 16, 24, 32):
            tn = norm_ref[pl.ds(base + ii, 128, stride=40), :]
            slabs.append(
                jnp.dot(tn.T.astype(BF16), out_w_ref[...], preferred_element_type=F32)
            )
        chunks = []
        for s in range(6):
            for jc in range(3):
                if s < 4:
                    slab, at = jc, s
                elif jc < 2:
                    slab, at = 3, jc * 2 + s - 4
                else:
                    slab, at = 4, s - 4
                chunks.append(slabs[slab][at * 32 : at * 32 + 32])
        update = jnp.concatenate(chunks, axis=0)
        values = jnp.concatenate([pair_ref[s * 8 + ii] for s in range(6)], axis=0).astype(F32)
        first = values + gate_ref[ii].astype(F32) * update
        first_ref[ii] = first
        normed = layer_norm_rows(first).astype(BF16)
        proj = jnp.dot(normed, attn_w_ref[...], preferred_element_type=F32)
        send_ref[ii, 0:576, :] = (proj * query_scale).astype(BF16)
        for s in range(6):
            row = jnp.concatenate(
                [normed[s * 96 : s * 96 + 96], normed[s * 96 : s * 96 + 32]], axis=0
            )
            bias = lax.dot_general(
                bias_w_ref[...], row, (((1,), (1,)), ((), ())), preferred_element_type=F32
            )
            bias_ref[pl.ds(s * 8 + ii, 1), :] = bias[0:1]
        return carry

    lax.fori_loop(0, 8, step, 0)
    bias = bias_ref[...].astype(BF16)
    for ii in range(8):
        send_ref[ii, 576:624, :] = bias


def bias_kernel(held_ref, out_ref):
    lane = lax.broadcasted_iota(jnp.int32, (48, 128), 1)
    tiles = []
    for yl in range(2):
        b = [held_ref[yl * 4 + z].astype(F32) for z in range(4)]
        r1, r2, r3 = pltpu.roll(b[1], 96, 1), pltpu.roll(b[2], 64, 1), pltpu.roll(b[3], 32, 1)
        tiles.append(jnp.where(lane < 96, b[0], r1))
        tiles.append(jnp.where(lane < 64, r1, r2))
        tiles.append(jnp.where(lane < 32, r2, r3))
    whole = jnp.concatenate(tiles, axis=1).astype(BF16)
    for copy in range(8):
        out_ref[copy] = whole


def attend_kernel(held_ref, bias_ref, mask_ref, spread_ref, out_ref, extra_ref, packed_ref):
    def fill(r, carry):
        extra_ref[pl.ds(pl.multiple_of(r * 48, 16), 48), :] = (
            bias_ref[r].astype(F32) * LOG2E + mask_ref[...]
        )
        return carry

    lax.fori_loop(0, 16, fill, 0)
    lane = lax.broadcasted_iota(jnp.int32, (24, 128), 1)

    def step(s, carry):
        rows = jnp.concatenate(
            [held_ref[c, pl.ds(pl.multiple_of(s * 96, 32), 96), :] for c in range(8)], axis=0
        )
        moved = jnp.dot(rows, spread_ref[...], preferred_element_type=F32)
        key = moved[:, 0:128].astype(BF16)
        value = jnp.concatenate([moved[:, 128:256].astype(BF16), jnp.ones((768, 128), BF16)], axis=1)
        for t in range(4):
            scores = lax.dot_general(
                rows[t * 192 : (t + 1) * 192],
                key,
                (((1,), (1,)), ((), ())),
                preferred_element_type=F32,
            )
            scores = scores + extra_ref[t * 192 : (t + 1) * 192, :]
            top = jnp.max(scores, axis=-1, keepdims=True)
            weights = jnp.exp2(scores - top).astype(BF16)
            summed = jnp.dot(weights, value, preferred_element_type=F32)
            gated = sigmoid(moved[t * 192 : (t + 1) * 192, 256:384]) * (
                summed[:, 0:128] / summed[:, 128:256]
            )
            for h in range(2):
                c = t * 2 + h
                g = [gated[h * 96 + k * 24 : h * 96 + k * 24 + 24] for k in range(4)]
                low = jnp.where(lane < 32, g[0], g[1])
                high = jnp.where(lane < 96, g[2], g[3])
                packed_ref[pl.ds(pl.multiple_of(c * 144 + s * 24, 8), 24), :] = jnp.where(
                    lane < 64, low, high
                )
        return carry

    lax.fori_loop(0, 6, step, 0)
    for c in range(8):
        out_ref[c] = packed_ref[c * 144 : (c + 1) * 144, :].astype(BF16)


def update_kernel(held_ref, first_ref, weight_ref, out_ref):
    def step(ii, carry):
        add = jnp.dot(held_ref[ii], weight_ref[...], preferred_element_type=F32)
        for s in range(6):
            rows = jnp.concatenate(
                [add[s * 24 : s * 24 + 24, g * 128 : (g + 1) * 128] for g in range(4)], axis=0
            )
            out_ref[s * 8 + ii] = (first_ref[ii, s * 96 : (s + 1) * 96, :] + rows).astype(BF16)
        return carry

    lax.fori_loop(0, 8, step, 0)


def call(kernel, outs, n_in, scratch=()):
    return pl.pallas_call(
        kernel,
        out_shape=outs,
        in_specs=[VMEM] * n_in,
        out_specs=jax.tree.map(lambda _: VMEM, outs),
        scratch_shapes=list(scratch),
        compiler_params=pltpu.CompilerParams(vmem_limit_bytes=48 * 1024 * 1024),
    )


def shape(dims, dtype=BF16):
    return jax.ShapeDtypeStruct(dims, dtype)


def exchange(values, axes):
    return lax.all_to_all(values, axes, 0, 0, tiled=True)


def body(
    pair,
    residue_mask,
    left_weight,
    right_weight,
    gate_weight,
    out_weight,
    attn_weight,
    bias_weight,
    attn_out_weight,
):
    row_pos = lax.axis_index(("x", "yh", "core"))
    col_pos = lax.axis_index(COL)
    mvec = residue_mask.astype(F32)
    row_mask = lax.dynamic_slice_in_dim(mvec, row_pos * 48, 48)
    col_mask = lax.dynamic_slice_in_dim(mvec, col_pos * 96, 96)
    main = (
        row_mask[:32].reshape(4, 8).T[None, :, :, None] * col_mask.reshape(3, 1, 1, 32)
    ).reshape(24, 128)
    rest_rows = jnp.concatenate([row_mask[32:].reshape(2, 8)] * 2, axis=0)
    rest = (rest_rows.T[None, :, :, None] * col_mask.reshape(3, 1, 1, 32)).reshape(24, 128)
    mask_wire = jnp.concatenate([main, main, rest], axis=0)

    sides = jnp.concatenate([left_weight, right_weight], axis=1).T
    wire, gate = call(
        project_kernel,
        (shape((128, 72, 128)), shape((8, 576, 128))),
        4,
        [pltpu.VMEM((72 * 128, 128), F32)],
    )(pair, mask_wire, sides, gate_weight)
    wire = exchange(wire, ALL)
    sums = call(
        triangle_kernel,
        shape((128, 40, 128)),
        1,
        [pltpu.VMEM((768, 768), BF16), pltpu.VMEM((768, 768), BF16), pltpu.VMEM((768, 768), F32)],
    )(wire)
    sums = exchange(sums, ALL)

    lane = jnp.arange(128)
    bias_w = jnp.concatenate([bias_weight[None, :], jnp.zeros((15, 128), BF16)], axis=0)
    first, send = call(
        first_kernel,
        (shape((8, 576, 128), F32), shape((8, 624, 128))),
        6,
        [pltpu.VMEM((128 * 40, 128), F32), pltpu.VMEM((48, 128), F32)],
    )(sums, pair, gate, out_weight, attn_weight, bias_w)
    held = exchange(send, COL)

    bias = call(bias_kernel, shape((8, 48, 768)), 1)(held[:, 576:624, :])
    bias = exchange(bias, ("x", "yh"))
    other = lax.ppermute(bias, "core", [(0, 1), (1, 0)])
    core = lax.axis_index("core")
    bias = jnp.where(
        core == 0, jnp.stack([bias, other], axis=1), jnp.stack([other, bias], axis=1)
    ).reshape(16, 48, 768)

    row = jnp.arange(128)[:, None]
    key_move = (row == lane[None, :] + 32) & (lane[None, :] < 32)
    value_move = row == lane[None, :] % 32 + 64
    gate_move = row == lane[None, :] % 32 + 96
    spread = jnp.concatenate([key_move, value_move, gate_move], axis=1).astype(BF16)
    mask_add = (1e9 * LOG2E) * (mvec[None, :] - 1.0)
    gated = call(
        attend_kernel,
        shape((8, 144, 128)),
        4,
        [pltpu.VMEM((768, 768), F32), pltpu.VMEM((8 * 144, 128), F32)],
    )(held, bias, mask_add, spread)
    gated = exchange(gated, COL)

    out_w = jnp.concatenate(
        [jnp.pad(attn_out_weight, ((g * 32, 96 - g * 32), (0, 0))) for g in range(4)], axis=1
    )
    return call(update_kernel, shape((48, 96, 128)), 3)(gated, first, out_w)


def solution(mesh):
    parts = Mesh(mesh.devices.reshape(4, 2, 2, 2, 4), ALL)
    spec = P(("x", "yh", "core"), COL, None)
    return jax.shard_map(
        body,
        mesh=parts,
        in_specs=(spec, P(), P(), P(), P(), P(), P(), P(), P()),
        out_specs=spec,
        check_vma=False,
    )
```

time: 635 us -> 166 us (0.26)
  waiting for transfers between devices: 447 us -> 38.9 us
  matrix products: 64.6 us -> 0 us
  local copies, waits for them, and re-layouts: 59.9 us -> 8.81 us
  blocking collectives: 21.9 us -> 63.6 us
  Pallas kernels: 0 us -> 36.7 us
  other arithmetic: 26.1 us -> 1.09 us
  starting transfers between devices: 0.31 us -> 15.7 us
  between operations: 13.4 us -> 0.22 us
    all_gather x3 -> x0, waiting for transfers between devices: 262 us -> none  [the longest x1 122 us: body(): right_all = lax.all_gather(right, 'row', axis=0, tiled=True)]
    reduce_scatter x1 -> x0, waiting for transfers between devices: 185 us -> none  [body(): lax.psum_scatter(jnp.einsum('ikc,jkc->jic', left, right_all, preferred_el...]
    dot_general x9 -> x0, matrix products: 64.6 us -> none  [the longest x1 20 us: body(): jnp.einsum('ikc,jkc->jic', left, right_all, preferred_element_type=jnp.fl...]
    all_to_all x0 -> x2, blocking collectives: none -> 63.6 us  [exchange(): return lax.all_to_all(values, axes, 0, 0, tiled=True)]
    all_to_all x0 -> x3, waiting for transfers between devices: none -> 37.4 us  [exchange(): return lax.all_to_all(values, axes, 0, 0, tiled=True)]
    pallas_call x0 -> x6, Pallas kernels: none -> 36.7 us  [the longest x1 9.24 us: body(): call(attend_kernel, shape((8, 144, 128)), 4, [pltpu.VMEM((768, 768), F32)...]
    all_gather x2 -> x0, local copies, waits for them, and re-layouts: 29.6 us -> none  [the longest x1 29.6 us: body(): right_all = lax.all_gather(right, 'row', axis=0, tiled=True)]
    all_gather x1 -> x0, blocking collectives: 21.9 us -> none  [body(): bias_cols = lax.all_gather(bias_tile, 'col', axis=1, tiled=True)]
  transfers between devices with their start and end apart: 4 -> 4, of which waited for: 4 -> 4; matrix products, arithmetic and copies ran while one was open for 3% -> 0% of each run, Pallas kernels for 0% -> 0%
where the time goes in v1:
time: 166 us; the launch traced here: 165 us
  blocking collectives  63.6 us (38%)
  waiting for transfers between devices  38.9 us (23%)
  Pallas kernels  36.7 us (22%)
  starting transfers between devices  15.7 us (9%)
  local copies, waits for them, and re-layouts  8.81 us (5%)
    all_to_all x2, blocking collectives, exchange(): return lax.all_to_all(values, axes, 0, 0, tiled=True)  63.6 us
    all_to_all x3, waiting for transfers between devices, exchange(): return lax.all_to_all(values, axes, 0, 0, tiled=True)  37.4 us
    all_to_all x3, starting transfers between devices, exchange(): return lax.all_to_all(values, axes, 0, 0, tiled=True)  11.9 us
    pallas_call x1, Pallas kernels, body(): call(attend_kernel, shape((8, 144, 128)), 4, [pltpu.VMEM((768, 768), F32)...  9.24 us
    pallas_call x1, Pallas kernels, body(): call(project_kernel, (shape((128, 72, 128)), shape((8, 576, 128))), 4, [p...  8.38 us
    pallas_call x1, Pallas kernels, body(): call(triangle_kernel, shape((128, 40, 128)), 1, [pltpu.VMEM((768, 768), B...  7.9 us
    unnamed x24, local copies, waits for them, and re-layouts  7.89 us
    pallas_call x1, Pallas kernels, body(): call(first_kernel, (shape((8, 576, 128), F32), shape((8, 624, 128))), 6,...  7.8 us
  transfers between devices with their start and end apart: 4, of which 4 were waited for; matrix products, arithmetic and copies ran while one was open for 0% of the time, Pallas kernels for 0%

profile of v1, /device:TPU:1, one launch (start us, length us, event | category | flops | bytes accessed | tf_op | source)
XLA Modules:
  0.0 164.9 jit_solution(14536200632468601029)
XLA Ops:
  0.0 0.7 convert_element_type.14
  0.7 0.1 dynamic_slice.6
  0.8 0.1 slice.26
  0.8 0.1 reshape.73
  0.9 0.1 copy.11
  1.0 0.1 reshape.72
  1.1 0.1 copy.10
  1.2 0.1 dynamic_slice.7
  1.3 0.1 mul.63
  1.3 0.1 broadcast_multiply_fusion.1
  1.4 0.1 mul.66
  1.5 0.1 mul.69
  1.6 1.0 copy.12
  2.6 1.0 copy.13
  3.6 0.0 copy-start
  3.6 1.3 copy-done
  4.8 0.0 copy-start.7
  4.8 0.8 copy-done.7
  5.6 8.4 %shard_map.91 = (bf16[128,72,128]{2,1,0:T(8,128)(2,1)S(1)}, bf16[8,576,128]{2,1,0:T(8,128)(2,1)S(1)}) custom-call(bf16[48,96,128]{2,1,0:T(8,128)(2,1)S(1)} %copy-done, f32[72,128]{1,0:T(8,128)S(1)} %pad_maximum_fusion.mask_ref, bf16[512,128]{1,0:T(8,128)(2,1)S(1)} %maximum_bitcast_fusion.sides_ref, bf16[128,128]{1,0:T(8,128)(2,1)S(1)} %copy-done.7), custom_call_target="tpu_custom_call" | custom-call | tf_op jit(solution)/shard_map/pallas_call | solution.py:320
  14.0 0.0 copy-start.3
  14.0 1.0 copy-done.3
  15.0 44.2 %all_to_all.25.wire_ref = bf16[128,72,128]{2,1,0:T(8,128)(2,1)S(1)} all-to-all(bf16[128,72,128]{2,1,0:T(8,128)(2,1)S(1)} %get-tuple-element.9), channel_id=1, replica_groups=mesh['x'=4,'yh'=2,'core'=2,'yl'=2,'z'=4] {'x','yh','core','yl','z'}, dimensions={0} | all-to-all | bytes 4718592 | tf_op jit(solution)/shard_map/all_to_all | solution.py:293
  59.2 7.9 %shard_map.92 = bf16[128,40,128]{2,1,0:T(8,128)(2,1)} custom-call(bf16[128,72,128]{2,1,0:T(8,128)(2,1)S(1)} %all_to_all.25.wire_ref), custom_call_target="tpu_custom_call" | custom-call | tf_op jit(solution)/shard_map/pallas_call | solution.py:327
  67.1 4.9 %all-to-all-start.1 = ((bf16[128,40,128]{2,1,0:T(8,128)(2,1)}), bf16[128,40,128]{2,1,0:T(8,128)(2,1)S(1)}, u32[]{:S(2)}, u32[]{:S(2)}) async-start(bf16[128,40,128]{2,1,0:T(8,128)(2,1)} %shard_map.92), calls=%async_computation.1 | async-start | bytes 2621440 | tf_op jit(solution)/shard_map/all_to_all | solution.py:293
  72.1 0.0 copy-done.10
  72.1 22.3 %all-to-all-done.1.wire_ref = bf16[128,40,128]{2,1,0:T(8,128)(2,1)S(1)} async-done(((bf16[128,40,128]{2,1,0:T(8,128)(2,1)}), bf16[128,40,128]{2,1,0:T(8,128)(2,1)S(1)}, u32[]{:S(2)}, u32[]{:S(2)}) %all-to-all-start.1) | async-done | bytes 1310752 | tf_op jit(solution)/shard_map/all_to_all | solution.py:293
  94.4 0.0 copy-done.1
  94.4 0.0 copy-done.5
  94.4 0.0 copy-done.6
  94.4 0.0 copy-start.4
  94.4 1.3 copy-done.4
  95.7 7.8 %shard_map.93 = (f32[8,576,128]{2,1,0:T(8,128)}, bf16[8,624,128]{2,1,0:T(8,128)(2,1)S(1)}) custom-call(bf16[128,40,128]{2,1,0:T(8,128)(2,1)S(1)} %all-to-all-done.1.wire_ref, bf16[48,96,128]{2,1,0:T(8,128)(2,1)S(1)} %copy-done.1, bf16[8,576,128]{2,1,0:T(8,128)(2,1)S(1)} %copy-done.4, bf16[128,128]{1,0:T(8,128)(2,1)S(1)} %copy-done.5, ...), custom_call_target="tpu_custom_call" | custom-call | tf_op jit(solution)/shard_map/pallas_call | solution.py:337
  103.5 19.3 %all_to_all.26.held_ref = bf16[8,624,128]{2,1,0:T(8,128)(2,1)S(1)} all-to-all(bf16[8,624,128]{2,1,0:T(8,128)(2,1)S(1)} %get-tuple-element.11), channel_id=1, replica_groups=mesh['x'=4,'yh'=2,'core'=2,'yl'=2,'z'=4] {'yl','z'}, dimensions={0} | all-to-all | bytes 2555904 | tf_op jit(solution)/shard_map/all_to_all | solution.py:293
  122.8 0.9 shard_map.94
  123.7 3.5 %all-to-all-start.3 = ((bf16[8,48,768]{2,1,0:T(8,128)(2,1)}), bf16[8,48,768]{2,1,0:T(8,128)(2,1)S(1)}, u32[]{:S(2)}, u32[]{:S(2)}) async-start(bf16[8,48,768]{2,1,0:T(8,128)(2,1)} %shard_map.94), calls=%async_computation.3 | async-start | bytes 1179648 | tf_op jit(solution)/shard_map/all_to_all | solution.py:293
  127.3 0.0 copy-done.8
  127.3 8.9 %all-to-all-done.3 = bf16[8,48,768]{2,1,0:T(8,128)(2,1)S(1)} async-done(((bf16[8,48,768]{2,1,0:T(8,128)(2,1)}), bf16[8,48,768]{2,1,0:T(8,128)(2,1)S(1)}, u32[]{:S(2)}, u32[]{:S(2)}) %all-to-all-start.3) | async-done | bytes 589856 | tf_op jit(solution)/shard_map/all_to_all | solution.py:293
  136.3 3.8 %collective-permute-start = (bf16[8,48,768]{2,1,0:T(8,128)(2,1)S(1)}, bf16[8,48,768]{2,1,0:T(8,128)(2,1)S(1)}, u32[]{:S(2)}, u32[]{:S(2)}) collective-permute-start(bf16[8,48,768]{2,1,0:T(8,128)(2,1)S(1)} %all-to-all-done.3), channel_id=1, source_target_pairs={{0,8},{8,0},{1,9},{9,1},{2,10},{10,2},{3,11},{11,3},{4,12},{12,4},... | collective-permute-start | bytes 1769480 | tf_op jit(solution)/shard_map/ppermute | solution.py:347
  140.1 1.5 collective-permute-done
  141.6 0.2 maximum_select_fusion
  141.8 0.1 copy.14
  141.9 0.0 copy-start.9
  141.9 9.2 %shard_map.95 = bf16[8,144,128]{2,1,0:T(8,128)(2,1)} custom-call(bf16[8,624,128]{2,1,0:T(8,128)(2,1)S(1)} %all_to_all.26.held_ref, bf16[16,48,768]{2,1,0:T(8,128)(2,1)S(1)} %bitcast.10, f32[1,768]{1,0:T(1,128)S(1)} %mul.72.mask_ref, bf16[128,384]{1,0:T(8,128)(2,1)S(1)} %add_convert_fusion.spread_ref), custom_call_target="tpu_custom_call" | custom-call | tf_op jit(solution)/shard_map/pallas_call | solution.py:359
  151.2 3.4 %all-to-all-start.4 = ((bf16[8,144,128]{2,1,0:T(8,128)(2,1)}), bf16[8,144,128]{2,1,0:T(8,128)(2,1)S(1)}, u32[]{:S(2)}, u32[]{:S(2)}) async-start(bf16[8,144,128]{2,1,0:T(8,128)(2,1)} %shard_map.95), calls=%async_computation.4 | async-start | bytes 589824 | tf_op jit(solution)/shard_map/all_to_all | solution.py:293
  154.6 0.0 copy-done.9
  154.6 6.2 %all-to-all-done.4.held_ref = bf16[8,144,128]{2,1,0:T(8,128)(2,1)S(1)} async-done(((bf16[8,144,128]{2,1,0:T(8,128)(2,1)}), bf16[8,144,128]{2,1,0:T(8,128)(2,1)S(1)}, u32[]{:S(2)}, u32[]{:S(2)}) %all-to-all-start.4) | async-done | bytes 294944 | tf_op jit(solution)/shard_map/all_to_all | solution.py:293
  160.8 1.7 %copy-done.2 = f32[8,576,128]{2,1,0:T(8,128)S(1)} copy-done((f32[8,576,128]{2,1,0:T(8,128)S(1)}, f32[8,576,128]{2,1,0:T(8,128)}, u32[]{:S(2)}) %copy-start.2) | copy-done | bytes 2359320
  162.5 2.4 %shard_map.96 = bf16[48,96,128]{2,1,0:T(8,128)(2,1)} custom-call(bf16[8,144,128]{2,1,0:T(8,128)(2,1)S(1)} %all-to-all-done.4.held_ref, f32[8,576,128]{2,1,0:T(8,128)S(1)} %copy-done.2, bf16[128,512]{1,0:T(8,128)(2,1)S(1)} %fusion.7.weight_ref), custom_call_target="tpu_custom_call" | custom-call | tf_op jit(solution)/shard_map/pallas_call | solution.py:370
  (21 shorter events, 0.2 us)
Async XLA Ops:
  3.6 1.3 copy-start
  4.8 0.8 copy-start.7
  14.0 1.0 copy-start.3
  67.1 5.0 %copy-start.10 = (bf16[128]{0:T(256)(128)(2,1)S(1)}, bf16[128]{0:T(256)(128)(2,1)}, u32[]{:S(2)}) copy-start(bf16[128]{0:T(256)(128)(2,1)} %param.16) | copy-start | bytes 772
  67.1 27.2 %copy-start.1 = (bf16[48,96,128]{2,1,0:T(8,128)(2,1)S(1)}, bf16[48,96,128]{2,1,0:T(8,128)(2,1)}, u32[]{:S(2)}) copy-start(bf16[48,96,128]{2,1,0:T(8,128)(2,1)} %pair_ref.3) | copy-start | bytes 3538948
  67.1 27.2 %copy-start.5 = (bf16[128,128]{1,0:T(8,128)(2,1)S(1)}, bf16[128,128]{1,0:T(8,128)(2,1)}, u32[]{:S(2)}) copy-start(bf16[128,128]{1,0:T(8,128)(2,1)} %out_w_ref.1) | copy-start | bytes 98308
  67.1 27.2 %copy-start.6 = (bf16[128,128]{1,0:T(8,128)(2,1)S(1)}, bf16[128,128]{1,0:T(8,128)(2,1)}, u32[]{:S(2)}) copy-start(bf16[128,128]{1,0:T(8,128)(2,1)} %attn_w_ref.1) | copy-start | bytes 98308
  67.1 27.2 %all-to-all-start.1 = ((bf16[128,40,128]{2,1,0:T(8,128)(2,1)}), bf16[128,40,128]{2,1,0:T(8,128)(2,1)S(1)}, u32[]{:S(2)}, u32[]{:S(2)}) async-start(bf16[128,40,128]{2,1,0:T(8,128)(2,1)} %shard_map.92), calls=%async_computation.1 | async-start | bytes 2621440 | tf_op jit(solution)/shard_map/all_to_all | solution.py:293
  94.4 1.3 copy-start.4
  122.8 4.5 %copy-start.8 = (s32[768]{0:T(1024)S(1)}, s32[768]{0:T(1024)}, u32[]{:S(2)}) copy-start(s32[768]{0:T(1024)} %param.10) | copy-start | bytes 9220
  123.7 12.5 %all-to-all-start.3 = ((bf16[8,48,768]{2,1,0:T(8,128)(2,1)}), bf16[8,48,768]{2,1,0:T(8,128)(2,1)S(1)}, u32[]{:S(2)}, u32[]{:S(2)}) async-start(bf16[8,48,768]{2,1,0:T(8,128)(2,1)} %shard_map.94), calls=%async_computation.3 | async-start | bytes 1179648 | tf_op jit(solution)/shard_map/all_to_all | solution.py:293
  136.3 5.4 %collective-permute-start = (bf16[8,48,768]{2,1,0:T(8,128)(2,1)S(1)}, bf16[8,48,768]{2,1,0:T(8,128)(2,1)S(1)}, u32[]{:S(2)}, u32[]{:S(2)}) collective-permute-start(bf16[8,48,768]{2,1,0:T(8,128)(2,1)S(1)} %all-to-all-done.3), channel_id=1, source_target_pairs={{0,8},{8,0},{1,9},{9,1},{2,10},{10,2},{3,11},{11,3},{4,12},{12,4},... | collective-permute-start | bytes 1769480 | tf_op jit(solution)/shard_map/ppermute | solution.py:347
  141.9 12.7 %copy-start.9 = (bf16[32,128]{1,0:T(8,128)(2,1)S(1)}, bf16[32,128]{1,0:T(8,128)(2,1)}, u32[]{:S(2)}) copy-start(bf16[32,128]{1,0:T(8,128)(2,1)} %param.17) | copy-start | bytes 24580
  151.2 9.7 %all-to-all-start.4 = ((bf16[8,144,128]{2,1,0:T(8,128)(2,1)}), bf16[8,144,128]{2,1,0:T(8,128)(2,1)S(1)}, u32[]{:S(2)}, u32[]{:S(2)}) async-start(bf16[8,144,128]{2,1,0:T(8,128)(2,1)} %shard_map.95), calls=%async_computation.4 | async-start | bytes 589824 | tf_op jit(solution)/shard_map/all_to_all | solution.py:293
  160.8 1.7 %copy-start.2 = (f32[8,576,128]{2,1,0:T(8,128)S(1)}, f32[8,576,128]{2,1,0:T(8,128)}, u32[]{:S(2)}) copy-start(f32[8,576,128]{2,1,0:T(8,128)} %get-tuple-element.12.first_ref) | copy-start | bytes 7077892

commit v2 on v1

v2 whole, which is shorter than its diff:
```python
import math

import jax
import jax.numpy as jnp
import numpy as np
from jax import lax
from jax.experimental import pallas as pl
from jax.experimental.pallas import tpu as pltpu
from jax.sharding import Mesh
from jax.sharding import PartitionSpec as P

F32 = jnp.float32
BF16 = jnp.bfloat16
LOG2E = math.log2(math.e)
PITCH = 136
UNROLL_PROJECT = 2
LIMIT_PROJECT = 60
LIMIT_TRIANGLE = 20
LIMIT_FIRST = 20
LIMIT_UPDATE = 20
UNROLL_UNPACK = 2
UNROLL_PACK = 2
UNROLL_FIRST = 2
UNROLL_ATTEND = 2
UNROLL_UPDATE = 4
ALL = ("x", "yh", "core", "yl", "z")
COL = ("yl", "z")
VMEM = pl.BlockSpec(memory_space=pltpu.VMEM)
HBM = pl.BlockSpec(memory_space=pltpu.HBM)


def swap_matrix():
    at = np.arange(512)
    target = at % 128 // 32 * 128 + at // 128 * 32 + at % 32
    return (target[:, None] == at[None, :]).astype(np.float32)


def move_matrix():
    row, lane = np.arange(128)[:, None], np.arange(128)[None, :]
    key = (row == lane + 32) & (lane < 32)
    return np.concatenate([key, row == lane % 32 + 64, row == lane % 32 + 96], axis=1).astype(
        np.float32
    )


SWAP = swap_matrix()
MOVE = move_matrix()


def sigmoid(values):
    return 0.5 * jnp.tanh(0.5 * values) + 0.5


def layer_norm_rows(values):
    center = values - jnp.mean(values, axis=-1, keepdims=True)
    spread = jnp.mean(center * center, axis=-1, keepdims=True)
    return center * lax.rsqrt(spread + 1e-05)


def swap_blocks(parts):
    lane = lax.broadcasted_iota(jnp.int32, parts[0].shape, 1)
    odd = jnp.bitwise_and(lane, 32) != 0
    high = lane >= 64
    v0, v1, v2, v3 = parts
    a0 = jnp.where(odd, pltpu.roll(v1, 32, 1), v0)
    a1 = jnp.where(odd, v1, pltpu.roll(v0, 96, 1))
    a2 = jnp.where(odd, pltpu.roll(v3, 32, 1), v2)
    a3 = jnp.where(odd, v3, pltpu.roll(v2, 96, 1))
    return (
        jnp.where(high, pltpu.roll(a2, 64, 1), a0),
        jnp.where(high, pltpu.roll(a3, 64, 1), a1),
        jnp.where(high, a2, pltpu.roll(a0, 64, 1)),
        jnp.where(high, a3, pltpu.roll(a1, 64, 1)),
    )


def project_kernel(
    pair_hbm, mask_ref, left_hbm, right_hbm, gate_hbm, wire_ref, gate_out, held_ref, slab_ref,
    left_ref, right_ref, gate_w_ref, sides_ref, col_ref, gated_ref, sems, w_sems, out_sems,
):
    loads = [
        pltpu.make_async_copy(
            pair_hbm.at[:, 2 * q : 2 * q + 2], held_ref.at[:, 2 * q : 2 * q + 2], sems.at[q]
        )
        for q in range(4)
    ]
    weights = [
        pltpu.make_async_copy(left_hbm, left_ref, w_sems.at[0]),
        pltpu.make_async_copy(right_hbm, right_ref, w_sems.at[1]),
        pltpu.make_async_copy(gate_hbm, gate_w_ref, w_sems.at[2]),
    ]
    for copy in weights + loads:
        copy.start()
    row_base = lax.axis_index(("x", "yh", "core")) * 48
    col_base = lax.axis_index(COL) * 96

    def mask_row(k, carry):
        col_ref[pl.ds(k, 1), :] = jnp.full((1, 128), mask_ref[col_base + k].astype(F32))
        return carry

    lax.fori_loop(0, 96, mask_row, 0, unroll=8)
    for copy in weights:
        copy.wait()
    sides_ref[0:256, :] = left_ref[...].T
    sides_ref[256:512, :] = right_ref[...].T
    lane = lax.broadcasted_iota(jnp.int32, (128, 128), 1)

    def step(ii, carry):
        values = jnp.concatenate([held_ref[s, ii] for s in range(6)], axis=0).astype(F32)
        normed = layer_norm_rows(values)
        gate = jnp.dot(normed.astype(BF16), gate_w_ref[...], preferred_element_type=F32)
        gated_ref[ii] = sigmoid(gate).astype(BF16)
        pltpu.make_async_copy(gated_ref.at[ii], gate_out.at[ii], out_sems.at[ii]).start()
        kept = [
            (
                normed[s * 96 : s * 96 + 96]
                * (col_ref[...] * mask_ref[row_base + s * 8 + ii].astype(F32))
            ).astype(BF16)
            for s in range(6)
        ]
        piece = lambda s, kc: kept[s][kc * 32 : kc * 32 + 32]
        store = lambda row: pl.ds(pl.multiple_of(row * PITCH, 8), 128)
        for kc in range(3):
            rows = jnp.concatenate([piece(s, kc) for s in range(4)], axis=0)
            proj = lax.dot_general(
                sides_ref[...], rows, (((1,), (1,)), ((), ())), preferred_element_type=F32
            )
            slab_ref[store(kc * 8 + ii), :] = sigmoid(proj[128:256]) * proj[0:128]
            slab_ref[store(24 + kc * 8 + ii), :] = sigmoid(proj[384:512]) * proj[256:384]
        for kc in range(3):
            rows = jnp.concatenate([piece(s, kc) for s in (4, 5, 4, 5)], axis=0)
            proj = lax.dot_general(
                sides_ref[...], rows, (((1,), (1,)), ((), ())), preferred_element_type=F32
            )
            value = jnp.where(lane < 64, proj[0:128], proj[256:384])
            gating = jnp.where(lane < 64, proj[128:256], proj[384:512])
            slab_ref[store(48 + kc * 8 + ii), :] = sigmoid(gating) * value
        return carry

    for q in range(4):
        loads[q].wait()
        lax.fori_loop(2 * q, 2 * q + 2, step, 0, unroll=UNROLL_PROJECT)

    def emit(ch, carry):
        wire_ref[ch] = slab_ref[pl.ds(ch, 72, stride=PITCH), :].astype(BF16)
        return carry

    lax.fori_loop(0, 128, emit, 0, unroll=4)
    for ii in range(8):
        pltpu.make_async_copy(gated_ref.at[ii], gate_out.at[ii], out_sems.at[ii]).wait()


def triangle_kernel(wire_ref, perm_ref, out_ref, left_ref, right_ref, sums_ref):
    def unpack(c_pair, carry):
        groups = [(half, yl) for half in range(2) for yl in range(2)]
        source = lambda half, yl, z: wire_ref[(c_pair * 2 + half) * 8 + yl * 4 + z]
        rows = jnp.concatenate(
            [
                jnp.concatenate([source(half, yl, z) for z in range(4)], axis=1)
                for half, yl in groups
            ],
            axis=0,
        )
        swapped = jnp.dot(rows, perm_ref[...], preferred_element_type=F32)
        for n, (half, yl) in enumerate(groups):
            at = lambda k, base: swapped[
                n * 72 + base + kc * 8 : n * 72 + base + kc * 8 + 8, k * 128 : k * 128 + 128
            ]
            for kc in range(3):
                cols = pl.ds((yl * 3 + kc) * 128, 128)
                left = jnp.concatenate(
                    [at(s, 0) for s in range(4)] + [at(0, 48), at(1, 48)], axis=0
                ).astype(BF16)
                right = jnp.concatenate(
                    [at(s, 24) for s in range(4)] + [at(2, 48), at(3, 48)], axis=0
                ).astype(BF16)
                row = pl.multiple_of((c_pair * 2 + half) * 48, 16)
                left_ref[pl.ds(row, 48), cols] = left
                for g3 in range(3):
                    g = half * 3 + g3
                    base = ((c_pair // 4) * 3 + g // 2) * 128 + (c_pair % 4) * 32 + (g % 2) * 16
                    right_ref[pl.ds(pl.multiple_of(base, 16), 16), cols] = right[
                        g3 * 16 : g3 * 16 + 16
                    ]
        return carry

    lax.fori_loop(0, 8, unpack, 0, unroll=UNROLL_UNPACK)
    for n in range(3):
        sums_ref[:, n * 256 : (n + 1) * 256] = lax.dot_general(
            left_ref[...],
            right_ref[n * 256 : (n + 1) * 256, :],
            (((1,), (1,)), ((), ())),
            preferred_element_type=F32,
        )

    def pack(r, carry):
        base = pl.multiple_of(r * 48, 16)
        order = (
            [(s, 0) for s in range(4)],
            [(s, 1) for s in range(4)],
            [(s, 2) for s in range(4)],
            [(4, 0), (5, 0), (4, 1), (5, 1)],
            [(4, 2), (5, 2), (4, 2), (5, 2)],
        )
        for yl in range(2):
            tile = lambda s, jc: sums_ref[
                pl.ds(pl.multiple_of(base + s * 8, 8), 8),
                (yl * 3 + jc) * 128 : (yl * 3 + jc + 1) * 128,
            ]
            parts = [
                jnp.concatenate([tile(*entry[a]) for entry in order], axis=0) for a in range(4)
            ]
            outs = swap_blocks(parts)
            for z in range(4):
                out_ref[r * 8 + yl * 4 + z] = outs[z].astype(BF16)
        return carry

    lax.fori_loop(0, 16, pack, 0, unroll=UNROLL_PACK)


def first_kernel(
    wire_ref, pair_hbm, gate_hbm, out_w_ref, attn_w_ref, bias_w_ref, mask_ref,
    first_out, send_ref, held_ref, gate_ref, first_ref, norm_ref, bias_ref, sems, out_sems,
):
    loads = [
        pltpu.make_async_copy(pair_hbm, held_ref, sems.at[0]),
        pltpu.make_async_copy(gate_hbm, gate_ref, sems.at[1]),
    ]
    for copy in loads:
        copy.start()

    def add(ch, total):
        return total + wire_ref[ch].astype(F32)

    zero = jnp.zeros((40, 128), F32)
    mean = lax.fori_loop(0, 128, add, zero, unroll=8) * (1.0 / 128)

    def add_square(ch, total):
        center = wire_ref[ch].astype(F32) - mean
        return total + center * center

    spread = lax.fori_loop(0, 128, add_square, zero, unroll=8) * (1.0 / 128)
    scale = lax.rsqrt(spread + 1e-05)

    def write(ch, carry):
        norm_ref[pl.ds(pl.multiple_of(ch * 40, 8), 40), :] = (
            wire_ref[ch].astype(F32) - mean
        ) * scale
        return carry

    lax.fori_loop(0, 128, write, 0, unroll=8)
    lane = lax.broadcasted_iota(jnp.int32, (1, 128), 1)
    query_scale = jnp.where(lane < 32, LOG2E / math.sqrt(32), 1.0)
    bias_w = jnp.broadcast_to(bias_w_ref[...], (16, 128))

    def step(ii, carry):
        slabs = []
        for base in (0, 8, 16, 24, 32):
            tn = norm_ref[pl.ds(base + ii, 128, stride=40), :]
            slabs.append(
                jnp.dot(tn.T.astype(BF16), out_w_ref[...], preferred_element_type=F32)
            )
        chunks = []
        for s in range(6):
            for jc in range(3):
                if s < 4:
                    slab, at = jc, s
                elif jc < 2:
                    slab, at = 3, jc * 2 + s - 4
                else:
                    slab, at = 4, s - 4
                chunks.append(slabs[slab][at * 32 : at * 32 + 32])
        update = jnp.concatenate(chunks, axis=0)
        values = jnp.concatenate([held_ref[s, ii] for s in range(6)], axis=0).astype(F32)
        first = values + gate_ref[ii].astype(F32) * update
        first_ref[ii] = first
        pltpu.make_async_copy(first_ref.at[ii], first_out.at[ii], out_sems.at[ii]).start()
        normed = layer_norm_rows(first).astype(BF16)
        proj = jnp.dot(normed, attn_w_ref[...], preferred_element_type=F32)
        send_ref[ii, 0:576, :] = (proj * query_scale).astype(BF16)
        for s in range(6):
            row = jnp.concatenate(
                [normed[s * 96 : s * 96 + 96], normed[s * 96 : s * 96 + 32]], axis=0
            )
            bias = lax.dot_general(
                bias_w, row, (((1,), (1,)), ((), ())), preferred_element_type=F32
            )
            bias_ref[pl.ds(s * 8 + ii, 1), :] = bias[0:1]
        return carry

    for copy in loads:
        copy.wait()
    lax.fori_loop(0, 8, step, 0, unroll=UNROLL_FIRST)
    bias = jnp.where(mask_ref[...] > 0, bias_ref[...] * LOG2E, -1e9 * LOG2E).astype(BF16)
    for ii in range(8):
        send_ref[ii, 576:624, :] = bias
    for ii in range(8):
        pltpu.make_async_copy(first_ref.at[ii], first_out.at[ii], out_sems.at[ii]).wait()


def bias_kernel(held_ref, out_ref):
    lane = lax.broadcasted_iota(jnp.int32, (48, 128), 1)
    tiles = []
    for yl in range(2):
        b = [held_ref[yl * 4 + z, 576:624, :].astype(F32) for z in range(4)]
        r1, r2, r3 = pltpu.roll(b[1], 96, 1), pltpu.roll(b[2], 64, 1), pltpu.roll(b[3], 32, 1)
        tiles.append(jnp.where(lane < 96, b[0], r1))
        tiles.append(jnp.where(lane < 64, r1, r2))
        tiles.append(jnp.where(lane < 32, r2, r3))
    whole = jnp.concatenate(tiles, axis=1).astype(BF16)
    for copy in range(8):
        out_ref[copy] = whole


def attend_kernel(held_ref, mine_ref, other_ref, move_ref, out_ref, extra_ref, packed_ref):
    core = lax.axis_index("core")

    def fill(chip, carry):
        for ref, at in ((mine_ref, core), (other_ref, 1 - core)):
            rows = pl.ds(pl.multiple_of(chip * 96 + at * 48, 16), 48)
            extra_ref[rows, :] = ref[chip].astype(F32)
        return carry

    lax.fori_loop(0, 8, fill, 0)
    lane = lax.broadcasted_iota(jnp.int32, (24, 128), 1)

    def step(s, carry):
        rows = jnp.concatenate(
            [held_ref[c, pl.ds(pl.multiple_of(s * 96, 32), 96), :] for c in range(8)], axis=0
        )
        moved = jnp.dot(rows, move_ref[...], preferred_element_type=F32)
        key = moved[:, 0:128].astype(BF16)
        value = jnp.concatenate([moved[:, 128:256].astype(BF16), jnp.ones((768, 128), BF16)], axis=1)
        for t in range(4):
            scores = lax.dot_general(
                rows[t * 192 : (t + 1) * 192],
                key,
                (((1,), (1,)), ((), ())),
                preferred_element_type=F32,
            )
            scores = scores + extra_ref[t * 192 : (t + 1) * 192, :]
            top = jnp.max(scores, axis=-1, keepdims=True)
            weights = jnp.exp2(scores - top).astype(BF16)
            summed = jnp.dot(weights, value, preferred_element_type=F32)
            gated = sigmoid(moved[t * 192 : (t + 1) * 192, 256:384]) * (
                summed[:, 0:128] / summed[:, 128:256]
            )
            for h in range(2):
                c = t * 2 + h
                g = [gated[h * 96 + k * 24 : h * 96 + k * 24 + 24] for k in range(4)]
                low = jnp.where(lane < 32, g[0], g[1])
                high = jnp.where(lane < 96, g[2], g[3])
                packed_ref[pl.ds(pl.multiple_of(c * 144 + s * 24, 8), 24), :] = jnp.where(
                    lane < 64, low, high
                )
        return carry

    lax.fori_loop(0, 6, step, 0, unroll=UNROLL_ATTEND)
    for c in range(8):
        out_ref[c] = packed_ref[c * 144 : (c + 1) * 144, :].astype(BF16)


def update_kernel(
    held_ref, first_hbm, weight_ref, out_hbm, first_ref, wide_ref, done_ref, sems, out_sems
):
    def load(ii):
        return pltpu.make_async_copy(first_hbm.at[ii], first_ref.at[ii], sems.at[ii])

    def store(ii):
        return pltpu.make_async_copy(done_ref.at[:, ii], out_hbm.at[:, ii], out_sems.at[ii])

    for ii in range(8):
        load(ii).start()
    wide_ref[...] = jnp.zeros((128, 512), BF16)
    for g in range(4):
        wide_ref[g * 32 : g * 32 + 32, g * 128 : g * 128 + 128] = weight_ref[...]

    def step(ii, carry):
        load(ii).wait()
        add = jnp.dot(held_ref[ii], wide_ref[...], preferred_element_type=F32)
        for s in range(6):
            rows = jnp.concatenate(
                [add[s * 24 : s * 24 + 24, g * 128 : (g + 1) * 128] for g in range(4)], axis=0
            )
            done_ref[s, ii] = (first_ref[ii, s * 96 : (s + 1) * 96, :] + rows).astype(BF16)
        store(ii).start()
        return carry

    lax.fori_loop(0, 8, step, 0, unroll=UNROLL_UPDATE)
    for ii in range(8):
        store(ii).wait()


def call(kernel, outs, in_specs, out_specs, scratch, limit=20):
    return pl.pallas_call(
        kernel,
        out_shape=outs,
        in_specs=in_specs,
        out_specs=out_specs,
        scratch_shapes=scratch,
        compiler_params=pltpu.CompilerParams(vmem_limit_bytes=limit * 1024 * 1024),
    )


def shape(dims, dtype=BF16):
    return jax.ShapeDtypeStruct(dims, dtype)


def exchange(values, axes):
    return lax.all_to_all(values, axes, 0, 0, tiled=True)


def body(
    pair,
    residue_mask,
    left_weight,
    right_weight,
    gate_weight,
    out_weight,
    attn_weight,
    bias_weight,
    attn_out_weight,
):
    pair = pair.reshape(6, 8, 96, 128)
    wire, gate = call(
        project_kernel,
        (shape((128, 72, 128)), shape((8, 576, 128))),
        [HBM, pl.BlockSpec(memory_space=pltpu.SMEM), HBM, HBM, HBM],
        (VMEM, HBM),
        [
            pltpu.VMEM((6, 8, 96, 128), BF16),
            pltpu.VMEM((72 * PITCH, 128), F32),
            pltpu.VMEM((128, 256), BF16),
            pltpu.VMEM((128, 256), BF16),
            pltpu.VMEM((128, 128), BF16),
            pltpu.VMEM((512, 128), BF16),
            pltpu.VMEM((96, 128), F32),
            pltpu.VMEM((8, 576, 128), BF16),
            pltpu.SemaphoreType.DMA((4,)),
            pltpu.SemaphoreType.DMA((3,)),
            pltpu.SemaphoreType.DMA((8,)),
        ],
        LIMIT_PROJECT,
    )(pair, residue_mask, left_weight, right_weight, gate_weight)
    wire = exchange(wire, ALL)
    sums = call(
        triangle_kernel,
        shape((128, 40, 128)),
        [VMEM, VMEM],
        VMEM,
        [pltpu.VMEM((768, 768), BF16), pltpu.VMEM((768, 768), BF16), pltpu.VMEM((768, 768), F32)],
        LIMIT_TRIANGLE,
    )(wire, jnp.asarray(SWAP, BF16))
    sums = exchange(sums, ALL)

    col_mask = lax.dynamic_slice_in_dim(residue_mask, lax.axis_index(COL) * 96, 96)
    col_mask = jnp.pad(col_mask, (0, 32))[None, :]
    first, send = call(
        first_kernel,
        (shape((8, 576, 128), F32), shape((8, 624, 128))),
        [VMEM, HBM, HBM] + [VMEM] * 4,
        (HBM, VMEM),
        [
            pltpu.VMEM((6, 8, 96, 128), BF16),
            pltpu.VMEM((8, 576, 128), BF16),
            pltpu.VMEM((8, 576, 128), F32),
            pltpu.VMEM((128 * 40, 128), F32),
            pltpu.VMEM((48, 128), F32),
            pltpu.SemaphoreType.DMA((2,)),
            pltpu.SemaphoreType.DMA((8,)),
        ],
        LIMIT_FIRST,
    )(sums, pair, gate, out_weight, attn_weight, bias_weight[None, :], col_mask)
    held = exchange(send, COL)
    bias = call(bias_kernel, shape((8, 48, 768)), [VMEM], VMEM, [])(held)
    bias = exchange(bias, ("x", "yh"))
    other = lax.ppermute(bias, "core", [(0, 1), (1, 0)])
    gated = call(
        attend_kernel,
        shape((8, 144, 128)),
        [VMEM] * 4,
        VMEM,
        [pltpu.VMEM((768, 768), F32), pltpu.VMEM((8 * 144, 128), F32)],
    )(held, bias, other, jnp.asarray(MOVE, BF16))
    gated = exchange(gated, COL)
    updated = call(
        update_kernel,
        shape((6, 8, 96, 128)),
        [VMEM, HBM, VMEM],
        HBM,
        [
            pltpu.VMEM((8, 576, 128), F32),
            pltpu.VMEM((128, 512), BF16),
            pltpu.VMEM((6, 8, 96, 128), BF16),
            pltpu.SemaphoreType.DMA((8,)),
            pltpu.SemaphoreType.DMA((8,)),
        ],
        LIMIT_UPDATE,
    )(gated, first, attn_out_weight)
    return updated.reshape(48, 96, 128)


def solution(mesh):
    parts = Mesh(mesh.devices.reshape(4, 2, 2, 2, 4), ALL)
    spec = P(("x", "yh", "core"), COL, None)
    return jax.shard_map(
        body,
        mesh=parts,
        in_specs=(spec, P(), P(), P(), P(), P(), P(), P(), P()),
        out_specs=spec,
        check_vma=False,
    )
```

time: 166 us -> 152 us (0.916)
  blocking collectives: 63.6 us -> 87.1 us
  waiting for transfers between devices: 38.9 us -> 23.1 us
  starting transfers between devices: 15.7 us -> 8.37 us
  local copies, waits for them, and re-layouts: 8.81 us -> 2.06 us
  Pallas kernels: 36.7 us -> 30.9 us
    all_to_all x2 -> x4, blocking collectives: 63.6 us -> 87.1 us  [exchange(): return lax.all_to_all(values, axes, 0, 0, tiled=True)]
    all_to_all x3 -> x1, waiting for transfers between devices: 37.4 us -> 21.5 us  [exchange(): return lax.all_to_all(values, axes, 0, 0, tiled=True)]
    all_to_all x3 -> x1, starting transfers between devices: 11.9 us -> 4.93 us  [exchange(): return lax.all_to_all(values, axes, 0, 0, tiled=True)]
    unnamed x24 -> x16, local copies, waits for them, and re-layouts: 7.89 us -> 1.29 us
    pallas_call x6, Pallas kernels: 36.7 us -> 30.9 us  [the longest x1 7.86 us: body(): call(project_kernel, (shape((128, 72, 128)), shape((8, 576, 128))), [HBM,...]
  transfers between devices with their start and end apart: 4 -> 2, of which waited for: 4 -> 2; matrix products, arithmetic and copies ran while one was open for 0% -> 1% of each run, Pallas kernels for 0% -> 0%
where the time goes in v2:
time: 152 us
  blocking collectives  87.1 us (57%)
  Pallas kernels  30.9 us (20%)
  waiting for transfers between devices  23.1 us (15%)
  starting transfers between devices  8.37 us (6%)
  local copies, waits for them, and re-layouts  2.06 us (1%)
    all_to_all x4, blocking collectives, exchange(): return lax.all_to_all(values, axes, 0, 0, tiled=True)  87.1 us
    all_to_all x1, waiting for transfers between devices, exchange(): return lax.all_to_all(values, axes, 0, 0, tiled=True)  21.5 us
    pallas_call x1, Pallas kernels, body(): call(project_kernel, (shape((128, 72, 128)), shape((8, 576, 128))), [HBM,...  7.86 us
    pallas_call x1, Pallas kernels, body(): call(attend_kernel, shape((8, 144, 128)), [VMEM] * 4, VMEM, [pltpu.VMEM((...  7.32 us
    pallas_call x1, Pallas kernels, body(): call(first_kernel, (shape((8, 576, 128), F32), shape((8, 624, 128))), [VM...  7.22 us
    pallas_call x1, Pallas kernels, body(): call(triangle_kernel, shape((128, 40, 128)), [VMEM, VMEM], VMEM, [pltpu.V...  5.65 us
    all_to_all x1, starting transfers between devices, exchange(): return lax.all_to_all(values, axes, 0, 0, tiled=True)  4.93 us
    ppermute x1, starting transfers between devices, body(): other = lax.ppermute(bias, 'core', [(0, 1), (1, 0)])  3.44 us
  transfers between devices with their start and end apart: 2, of which 2 were waited for; matrix products, arithmetic and copies ran while one was open for 1% of the time, Pallas kernels for 0%

profile of v2, /device:TPU:1, one launch (start us, length us, event | category | flops | bytes accessed | tf_op | source)
XLA Modules:
  0.0 151.6 jit_solution(9336191421731433977)
XLA Ops:
  0.0 7.9 %shard_map.109 = (bf16[128,72,128]{2,1,0:T(8,128)(2,1)}, bf16[8,576,128]{2,1,0:T(8,128)(2,1)}) custom-call(bf16[6,8,96,128]{3,2,1,0:T(8,128)(2,1)} %bitcast.5, s32[768]{0:T(1024)} %mask_ref.1, bf16[128,256]{1,0:T(8,128)(2,1)} %left_hbm.1, bf16[128,256]{1,0:T(8,128)(2,1)} %right_hbm.1, bf16[128,128]{1,0:T(8,128)(2,1)} %gate_hbm.1), custom_call_target="tpu_custom_call" | custom-call | tf_op jit(solution)/shard_map/pallas_call | solution.py:425
  7.9 0.0 copy-start.2
  7.9 44.4 %all_to_all.25.wire_ref = bf16[128,72,128]{2,1,0:T(8,128)(2,1)S(1)} all-to-all(bf16[128,72,128]{2,1,0:T(8,128)(2,1)} %get-tuple-element.9), channel_id=1, replica_groups=mesh['x'=4,'yh'=2,'core'=2,'yl'=2,'z'=4] {'x','yh','core','yl','z'}, dimensions={0} | all-to-all | bytes 4718592 | tf_op jit(solution)/shard_map/all_to_all | solution.py:410
  52.3 0.0 copy-done.2
  52.3 5.6 %shard_map.110 = bf16[128,40,128]{2,1,0:T(8,128)(2,1)} custom-call(bf16[128,72,128]{2,1,0:T(8,128)(2,1)S(1)} %all_to_all.25.wire_ref, bf16[512,512]{1,0:T(8,128)(2,1)S(1)} %copy-done.2), custom_call_target="tpu_custom_call" | custom-call | tf_op jit(solution)/shard_map/pallas_call | solution.py:446
  58.0 0.0 copy-start
  58.0 0.0 copy-start.4
  58.0 0.0 copy-start.5
  58.0 0.0 copy-start.7
  58.0 4.9 %all-to-all-start.1 = ((bf16[128,40,128]{2,1,0:T(8,128)(2,1)}), bf16[128,40,128]{2,1,0:T(8,128)(2,1)S(1)}, u32[]{:S(2)}, u32[]{:S(2)}) async-start(bf16[128,40,128]{2,1,0:T(8,128)(2,1)} %shard_map.110), calls=%async_computation.1 | async-start | bytes 2621440 | tf_op jit(solution)/shard_map/all_to_all | solution.py:410
  62.9 0.8 dynamic_slice.3
  63.7 21.5 %all-to-all-done.1.wire_ref = bf16[128,40,128]{2,1,0:T(8,128)(2,1)S(1)} async-done(((bf16[128,40,128]{2,1,0:T(8,128)(2,1)}), bf16[128,40,128]{2,1,0:T(8,128)(2,1)S(1)}, u32[]{:S(2)}, u32[]{:S(2)}) %all-to-all-start.1) | async-done | bytes 1310752 | tf_op jit(solution)/shard_map/all_to_all | solution.py:410
  85.2 0.0 copy-done
  85.2 0.0 copy-done.4
  85.2 0.0 copy-done.5
  85.2 0.0 copy-done.7
  85.2 0.0 copy-start.1
  85.2 1.3 copy-done.1
  86.5 7.2 %shard_map.111 = (f32[8,576,128]{2,1,0:T(8,128)S(1)}, bf16[8,624,128]{2,1,0:T(8,128)(2,1)S(1)}) custom-call(bf16[128,40,128]{2,1,0:T(8,128)(2,1)S(1)} %all-to-all-done.1.wire_ref, bf16[6,8,96,128]{3,2,1,0:T(8,128)(2,1)S(1)} %bitcast.6, bf16[8,576,128]{2,1,0:T(8,128)(2,1)S(1)} %copy-done.1, bf16[128,128]{1,0:T(8,128)(2,1)S(1)} %copy-done.4, ...), custom_call_target="tpu_custom_call" | custom-call | tf_op jit(solution)/shard_map/pallas_call | solution.py:458
  93.7 19.4 %all_to_all.26.held_ref = bf16[8,624,128]{2,1,0:T(8,128)(2,1)S(1)} all-to-all(bf16[8,624,128]{2,1,0:T(8,128)(2,1)S(1)} %get-tuple-element.11), channel_id=1, replica_groups=mesh['x'=4,'yh'=2,'core'=2,'yl'=2,'z'=4] {'yl','z'}, dimensions={0} | all-to-all | bytes 2555904 | tf_op jit(solution)/shard_map/all_to_all | solution.py:410
  113.1 0.0 copy-start.3
  113.1 0.1 shard_map.112
  113.2 12.9 %all_to_all.27.mine_ref = bf16[8,48,768]{2,1,0:T(8,128)(2,1)S(1)} all-to-all(bf16[8,48,768]{2,1,0:T(8,128)(2,1)S(1)} %shard_map.112), channel_id=1, replica_groups=mesh['x'=4,'yh'=2,'core'=2,'yl'=2,'z'=4] {'x','yh'}, dimensions={0} | all-to-all | bytes 1179648 | tf_op jit(solution)/shard_map/all_to_all | solution.py:410
  126.1 0.0 copy-start.6
  126.1 3.4 %collective-permute-start = (bf16[8,48,768]{2,1,0:T(8,128)(2,1)S(1)}, bf16[8,48,768]{2,1,0:T(8,128)(2,1)S(1)}, u32[]{:S(2)}, u32[]{:S(2)}) collective-permute-start(bf16[8,48,768]{2,1,0:T(8,128)(2,1)S(1)} %all_to_all.27.mine_ref), channel_id=1, source_target_pairs={{0,8},{8,0},{1,9},{9,1},{2,10},{10,2},{3,11},{11,3},{4,12},{12,4},... | collective-permute-start | bytes 1769480 | tf_op jit(solution)/shard_map/ppermute | solution.py:477
  129.5 1.6 %collective-permute-done.other_ref = bf16[8,48,768]{2,1,0:T(8,128)(2,1)S(1)} collective-permute-done((bf16[8,48,768]{2,1,0:T(8,128)(2,1)S(1)}, bf16[8,48,768]{2,1,0:T(8,128)(2,1)S(1)}, u32[]{:S(2)}, u32[]{:S(2)}) %collective-permute-start) | collective-permute-done | bytes 589856 | tf_op jit(solution)/shard_map/ppermute | solution.py:477
  131.2 0.0 copy-done.3
  131.2 7.3 %shard_map.113 = bf16[8,144,128]{2,1,0:T(8,128)(2,1)S(1)} custom-call(bf16[8,624,128]{2,1,0:T(8,128)(2,1)S(1)} %all_to_all.26.held_ref, bf16[8,48,768]{2,1,0:T(8,128)(2,1)S(1)} %all_to_all.27.mine_ref, bf16[8,48,768]{2,1,0:T(8,128)(2,1)S(1)} %collective-permute-done.other_ref, bf16[128,384]{1,0:T(8,128)(2,1)S(1)} %copy-done.3), custom_call_target="tpu_custom_call" | custom-call | tf_op jit(solution)/shard_map/pallas_call | solution.py:478
  138.5 10.4 %all_to_all.28.held_ref = bf16[8,144,128]{2,1,0:T(8,128)(2,1)S(1)} all-to-all(bf16[8,144,128]{2,1,0:T(8,128)(2,1)S(1)} %shard_map.113), channel_id=1, replica_groups=mesh['x'=4,'yh'=2,'core'=2,'yl'=2,'z'=4] {'yl','z'}, dimensions={0} | all-to-all | bytes 589824 | tf_op jit(solution)/shard_map/all_to_all | solution.py:410
  148.9 0.0 copy-done.6
  148.9 2.7 %shard_map.114 = bf16[6,8,96,128]{3,2,1,0:T(8,128)(2,1)} custom-call(bf16[8,144,128]{2,1,0:T(8,128)(2,1)S(1)} %all_to_all.28.held_ref, f32[8,576,128]{2,1,0:T(8,128)S(1)} %get-tuple-element.12.first_hbm, bf16[32,128]{1,0:T(8,128)(2,1)S(1)} %copy-done.6), custom_call_target="tpu_custom_call" | custom-call | tf_op jit(solution)/shard_map/pallas_call | solution.py:486
  (1 shorter events, 0.0 us)
Async XLA Ops:
  7.9 44.5 %copy-start.2 = (bf16[512,512]{1,0:T(8,128)(2,1)S(1)}, bf16[512,512]{1,0:T(8,128)(2,1)}, u32[]{:S(2)}) copy-start(bf16[512,512]{1,0:T(8,128)(2,1)} %constant.21.clone.perm_ref) | copy-start | bytes 1572868
  58.0 27.2 %copy-start = (bf16[48,96,128]{2,1,0:T(8,128)(2,1)S(1)}, bf16[48,96,128]{2,1,0:T(8,128)(2,1)}, u32[]{:S(2)}) copy-start(bf16[48,96,128]{2,1,0:T(8,128)(2,1)} %param.11) | copy-start | bytes 3538948
  58.0 27.2 %copy-start.4 = (bf16[128,128]{1,0:T(8,128)(2,1)S(1)}, bf16[128,128]{1,0:T(8,128)(2,1)}, u32[]{:S(2)}) copy-start(bf16[128,128]{1,0:T(8,128)(2,1)} %out_w_ref.1) | copy-start | bytes 98308
  58.0 27.2 %copy-start.5 = (bf16[128,128]{1,0:T(8,128)(2,1)S(1)}, bf16[128,128]{1,0:T(8,128)(2,1)}, u32[]{:S(2)}) copy-start(bf16[128,128]{1,0:T(8,128)(2,1)} %attn_w_ref.1) | copy-start | bytes 98308
  58.0 27.2 %copy-start.7 = (bf16[128]{0:T(256)(128)(2,1)S(1)}, bf16[128]{0:T(256)(128)(2,1)}, u32[]{:S(2)}) copy-start(bf16[128]{0:T(256)(128)(2,1)} %param.18) | copy-start | bytes 772
  58.0 27.2 %all-to-all-start.1 = ((bf16[128,40,128]{2,1,0:T(8,128)(2,1)}), bf16[128,40,128]{2,1,0:T(8,128)(2,1)S(1)}, u32[]{:S(2)}, u32[]{:S(2)}) async-start(bf16[128,40,128]{2,1,0:T(8,128)(2,1)} %shard_map.110), calls=%async_computation.1 | async-start | bytes 2621440 | tf_op jit(solution)/shard_map/all_to_all | solution.py:410
  85.2 1.3 copy-start.1
  113.1 18.1 %copy-start.3 = (bf16[128,384]{1,0:T(8,128)(2,1)S(1)}, bf16[128,384]{1,0:T(8,128)(2,1)}, u32[]{:S(2)}) copy-start(bf16[128,384]{1,0:T(8,128)(2,1)} %constant.22.clone.move_ref) | copy-start | bytes 294916
  126.1 22.8 %copy-start.6 = (bf16[32,128]{1,0:T(8,128)(2,1)S(1)}, bf16[32,128]{1,0:T(8,128)(2,1)}, u32[]{:S(2)}) copy-start(bf16[32,128]{1,0:T(8,128)(2,1)} %weight_ref.1) | copy-start | bytes 24580
  126.1 5.1 %collective-permute-start = (bf16[8,48,768]{2,1,0:T(8,128)(2,1)S(1)}, bf16[8,48,768]{2,1,0:T(8,128)(2,1)S(1)}, u32[]{:S(2)}, u32[]{:S(2)}) collective-permute-start(bf16[8,48,768]{2,1,0:T(8,128)(2,1)S(1)} %all_to_all.27.mine_ref), channel_id=1, source_target_pairs={{0,8},{8,0},{1,9},{9,1},{2,10},{10,2},{3,11},{11,3},{4,12},{12,4},... | collective-permute-start | bytes 1769480 | tf_op jit(solution)/shard_map/ppermute | solution.py:477

commit v3 on v2

v3 whole, which is shorter than its diff:
```python
import math

import jax
import jax.numpy as jnp
import numpy as np
from jax import lax
from jax.experimental import pallas as pl
from jax.experimental.pallas import tpu as pltpu
from jax.sharding import Mesh
from jax.sharding import PartitionSpec as P

F32 = jnp.float32
BF16 = jnp.bfloat16
LOG2E = math.log2(math.e)
PITCH = 136
UNROLL_PROJECT = 2
WORK_MINE = 30
WORK_SCORE = 30
LIMIT_OTHER = 20
LIMIT_PROJECT = 60
LIMIT_TRIANGLE = 20
LIMIT_FIRST = 20
LIMIT_UPDATE = 20
UNROLL_UNPACK = 4
UNROLL_PACK = 2
UNROLL_FIRST = 2
UNROLL_ATTEND = 6
UNROLL_UPDATE = 4
ALL = ("x", "yh", "core", "yl", "z")
COL = ("yl", "z")
VMEM = pl.BlockSpec(memory_space=pltpu.VMEM)
HBM = pl.BlockSpec(memory_space=pltpu.HBM)


def swap_matrix():
    at = np.arange(512)
    target = at % 128 // 32 * 128 + at // 128 * 32 + at % 32
    return (target[:, None] == at[None, :]).astype(np.float32)


def move_matrix():
    row, lane = np.arange(128)[:, None], np.arange(128)[None, :]
    key = (row == lane + 32) & (lane < 32)
    return np.concatenate([key, row == lane % 32 + 64, row == lane % 32 + 96], axis=1).astype(
        np.float32
    )


SWAP = swap_matrix()
MOVE = move_matrix()


def sigmoid(values):
    return 0.5 * jnp.tanh(0.5 * values) + 0.5


def layer_norm_rows(values):
    center = values - jnp.mean(values, axis=-1, keepdims=True)
    spread = jnp.mean(center * center, axis=-1, keepdims=True)
    return center * lax.rsqrt(spread + 1e-05)


def swap_blocks(parts):
    lane = lax.broadcasted_iota(jnp.int32, parts[0].shape, 1)
    odd = jnp.bitwise_and(lane, 32) != 0
    high = lane >= 64
    v0, v1, v2, v3 = parts
    a0 = jnp.where(odd, pltpu.roll(v1, 32, 1), v0)
    a1 = jnp.where(odd, v1, pltpu.roll(v0, 96, 1))
    a2 = jnp.where(odd, pltpu.roll(v3, 32, 1), v2)
    a3 = jnp.where(odd, v3, pltpu.roll(v2, 96, 1))
    return (
        jnp.where(high, pltpu.roll(a2, 64, 1), a0),
        jnp.where(high, pltpu.roll(a3, 64, 1), a1),
        jnp.where(high, a2, pltpu.roll(a0, 64, 1)),
        jnp.where(high, a3, pltpu.roll(a1, 64, 1)),
    )


def project_kernel(
    pair_hbm, mask_ref, left_hbm, right_hbm, wire_out, held_ref, slab_ref,
    left_ref, right_ref, sides_ref, col_ref, wire_ref, sems, w_sems, out_sems,
):
    loads = [
        pltpu.make_async_copy(
            pair_hbm.at[:, 2 * q : 2 * q + 2], held_ref.at[:, 2 * q : 2 * q + 2], sems.at[q]
        )
        for q in range(4)
    ]
    weights = [
        pltpu.make_async_copy(left_hbm, left_ref, w_sems.at[0]),
        pltpu.make_async_copy(right_hbm, right_ref, w_sems.at[1]),
    ]
    for copy in weights + loads:
        copy.start()
    row_base = lax.axis_index(("x", "yh", "core")) * 48
    col_base = lax.axis_index(COL) * 96

    def mask_row(k, carry):
        col_ref[pl.ds(k, 1), :] = jnp.full((1, 128), mask_ref[col_base + k].astype(F32))
        return carry

    lax.fori_loop(0, 96, mask_row, 0, unroll=8)
    for copy in weights:
        copy.wait()
    sides_ref[0:256, :] = left_ref[...].T
    sides_ref[256:512, :] = right_ref[...].T
    lane = lax.broadcasted_iota(jnp.int32, (128, 128), 1)

    def step(ii, carry):
        values = jnp.concatenate([held_ref[s, ii] for s in range(6)], axis=0).astype(F32)
        normed = layer_norm_rows(values)
        kept = [
            (
                normed[s * 96 : s * 96 + 96]
                * (col_ref[...] * mask_ref[row_base + s * 8 + ii].astype(F32))
            ).astype(BF16)
            for s in range(6)
        ]
        piece = lambda s, kc: kept[s][kc * 32 : kc * 32 + 32]
        store = lambda row: pl.ds(pl.multiple_of(row * PITCH, 8), 128)
        blocks = [(kc, s) for kc in range(3) for s in range(4)]
        blocks += [(kc, s) for kc in range(3) for s in (4, 5, 4, 5)]
        rows = jnp.concatenate([piece(s, kc) for kc, s in blocks], axis=0)
        for n in range(6):
            if n % 2 == 0:
                pair_of = lax.dot_general(
                    sides_ref[...],
                    rows[n * 128 : n * 128 + 256],
                    (((1,), (1,)), ((), ())),
                    preferred_element_type=F32,
                )
            proj = pair_of[:, n % 2 * 128 : n % 2 * 128 + 128]
            if n < 3:
                slab_ref[store(n * 8 + ii), :] = sigmoid(proj[128:256]) * proj[0:128]
                slab_ref[store(24 + n * 8 + ii), :] = sigmoid(proj[384:512]) * proj[256:384]
            else:
                value = jnp.where(lane < 64, proj[0:128], proj[256:384])
                gating = jnp.where(lane < 64, proj[128:256], proj[384:512])
                slab_ref[store(24 + n * 8 + ii), :] = sigmoid(gating) * value
        return carry

    for q in range(4):
        loads[q].wait()
        lax.fori_loop(2 * q, 2 * q + 2, step, 0, unroll=UNROLL_PROJECT)

    def emit(ch, carry):
        wire_ref[ch] = slab_ref[pl.ds(ch, 72, stride=PITCH), :].astype(BF16)
        return carry

    stores = [
        pltpu.make_async_copy(
            wire_ref.at[32 * q : 32 * q + 32], wire_out.at[32 * q : 32 * q + 32], out_sems.at[q]
        )
        for q in range(4)
    ]
    for q in range(4):
        lax.fori_loop(32 * q, 32 * q + 32, emit, 0, unroll=4)
        stores[q].start()
    for copy in stores:
        copy.wait()


def triangle_kernel(wire_ref, perm_ref, out_ref, left_ref, right_ref, sums_ref):
    def unpack(c_pair, carry):
        groups = [(half, yl) for half in range(2) for yl in range(2)]
        source = lambda half, yl, z: wire_ref[(c_pair * 2 + half) * 8 + yl * 4 + z]
        rows = jnp.concatenate(
            [
                jnp.concatenate([source(half, yl, z) for z in range(4)], axis=1)
                for half, yl in groups
            ],
            axis=0,
        )
        swapped = jnp.dot(rows, perm_ref[...], preferred_element_type=F32)
        for n, (half, yl) in enumerate(groups):
            at = lambda k, base: swapped[
                n * 72 + base + kc * 8 : n * 72 + base + kc * 8 + 8, k * 128 : k * 128 + 128
            ]
            for kc in range(3):
                cols = pl.ds((yl * 3 + kc) * 128, 128)
                left = jnp.concatenate(
                    [at(s, 0) for s in range(4)] + [at(0, 48), at(1, 48)], axis=0
                ).astype(BF16)
                right = jnp.concatenate(
                    [at(s, 24) for s in range(4)] + [at(2, 48), at(3, 48)], axis=0
                ).astype(BF16)
                row = pl.multiple_of((c_pair * 2 + half) * 48, 16)
                left_ref[pl.ds(row, 48), cols] = left
                for g3 in range(3):
                    g = half * 3 + g3
                    base = ((c_pair // 4) * 3 + g // 2) * 128 + (c_pair % 4) * 32 + (g % 2) * 16
                    right_ref[pl.ds(pl.multiple_of(base, 16), 16), cols] = right[
                        g3 * 16 : g3 * 16 + 16
                    ]
        return carry

    lax.fori_loop(0, 8, unpack, 0, unroll=UNROLL_UNPACK)
    for n in range(3):
        sums_ref[:, n * 256 : (n + 1) * 256] = lax.dot_general(
            left_ref[...],
            right_ref[n * 256 : (n + 1) * 256, :],
            (((1,), (1,)), ((), ())),
            preferred_element_type=F32,
        )

    def pack(r, carry):
        base = pl.multiple_of(r * 48, 16)
        order = (
            [(s, 0) for s in range(4)],
            [(s, 1) for s in range(4)],
            [(s, 2) for s in range(4)],
            [(4, 0), (5, 0), (4, 1), (5, 1)],
            [(4, 2), (5, 2), (4, 2), (5, 2)],
        )
        for yl in range(2):
            tile = lambda s, jc: sums_ref[
                pl.ds(pl.multiple_of(base + s * 8, 8), 8),
                (yl * 3 + jc) * 128 : (yl * 3 + jc + 1) * 128,
            ]
            parts = [
                jnp.concatenate([tile(*entry[a]) for entry in order], axis=0) for a in range(4)
            ]
            outs = swap_blocks(parts)
            for z in range(4):
                out_ref[r * 8 + yl * 4 + z] = outs[z].astype(BF16)
        return carry

    lax.fori_loop(0, 16, pack, 0, unroll=UNROLL_PACK)


def slab_chunks(base):
    if base < 3:
        return [(s, base) for s in range(4)]
    if base == 3:
        return [(4, 0), (5, 0), (4, 1), (5, 1)]
    return [(4, 2), (5, 2)]


def gate_kernel(pair_ref, gate_w_ref, out_ref):
    gate_w = gate_w_ref[...].T
    same = lax.broadcasted_iota(jnp.int32, (128, 128), 0) == lax.broadcasted_iota(
        jnp.int32, (128, 128), 1
    )
    unit = jnp.where(same, 1.0, 0.0).astype(BF16)

    def step(ii, carry):
        held = [pair_ref[s, ii] for s in range(6)]
        values = jnp.concatenate(held, axis=0).astype(F32)
        normed = layer_norm_rows(values).astype(BF16)
        for base in range(5):
            chunks = slab_chunks(base)
            chunks = chunks + chunks[: 4 - len(chunks)]
            rows = jnp.concatenate(
                [normed[s * 96 + jc * 32 : s * 96 + jc * 32 + 32] for s, jc in chunks], axis=0
            )
            plain = jnp.concatenate(
                [held[s][jc * 32 : jc * 32 + 32] for s, jc in chunks], axis=0
            )
            contract = (((1,), (1,)), ((), ()))
            gate = lax.dot_general(gate_w, rows, contract, preferred_element_type=F32)
            out_ref[base * 8 + ii] = sigmoid(gate).astype(BF16)
            turned = lax.dot_general(unit, plain, contract, preferred_element_type=F32)
            out_ref[40 + base * 8 + ii] = turned.astype(BF16)
        return carry

    lax.fori_loop(0, 8, step, 0)


def first_kernel(
    wire_ref, sides_ref, out_w_ref, attn_w_ref, bias_w_ref, mask_ref,
    send_ref, first_ref, norm_ref, bias_ref,
):
    def add(ch, total):
        return total + wire_ref[ch].astype(F32)

    zero = jnp.zeros((40, 128), F32)
    mean = lax.fori_loop(0, 128, add, zero, unroll=8) * (1.0 / 128)

    def add_square(ch, total):
        center = wire_ref[ch].astype(F32) - mean
        return total + center * center

    spread = lax.fori_loop(0, 128, add_square, zero, unroll=8) * (1.0 / 128)
    scale = lax.rsqrt(spread + 1e-05)

    def write(ch, carry):
        norm_ref[pl.ds(pl.multiple_of(ch * 40, 8), 40), :] = (
            wire_ref[ch].astype(F32) - mean
        ) * scale
        return carry

    lax.fori_loop(0, 128, write, 0, unroll=8)
    lane = lax.broadcasted_iota(jnp.int32, (1, 128), 1)
    query_scale = jnp.where(lane < 32, LOG2E / math.sqrt(32), 1.0)
    bias_w = jnp.broadcast_to(bias_w_ref[...], (16, 128))
    out_w = out_w_ref[...].T

    def step(ii, carry):
        rows = [base * 8 + ii for base in range(5)]
        side = lambda values: jnp.concatenate(values, axis=1)
        tri = side([norm_ref[pl.ds(row, 128, stride=40), :].astype(BF16) for row in rows])
        update = jnp.dot(out_w, tri, preferred_element_type=F32)
        first = side([sides_ref[40 + row].astype(F32) for row in rows]) + (
            side([sides_ref[row].astype(F32) for row in rows]) * update
        )
        center = first - jnp.mean(first, axis=0, keepdims=True)
        spread = jnp.mean(center * center, axis=0, keepdims=True)
        normed = center * lax.rsqrt(spread + 1e-05)
        bias = jnp.dot(bias_w, normed.astype(BF16), preferred_element_type=F32)
        turned = []
        for base, row in enumerate(rows):
            cols = slice(base * 128, base * 128 + 128)
            first_ref[row] = first[:, cols].astype(BF16)
            bias_ref[pl.ds(row, 1), :] = bias[0:1, cols]
            turned.append(normed[:, cols].T)
        turned = jnp.concatenate(turned, axis=0).astype(BF16)
        proj = jnp.dot(turned, attn_w_ref[...], preferred_element_type=F32)
        proj = (proj * query_scale).astype(BF16)
        for base in range(5):
            for n, (s, jc) in enumerate(slab_chunks(base)):
                at = base * 128 + n * 32
                send_ref[ii, s * 96 + jc * 32 : s * 96 + jc * 32 + 32, :] = proj[at : at + 32]
        return carry

    lax.fori_loop(0, 8, step, 0, unroll=UNROLL_FIRST)
    bias = jnp.where(mask_ref[...] > 0, bias_ref[...] * LOG2E, -1e9 * LOG2E)
    bias = jnp.concatenate([bias, jnp.zeros((8, 128), F32)], axis=0).astype(BF16)
    for ii in range(8):
        send_ref[ii, 576:624, :] = bias


def turn_kernel(slab_ref, first_ref):
    def step(ii, carry):
        for base in range(5):
            turned = slab_ref[base * 8 + ii].T
            for n, (s, jc) in enumerate(slab_chunks(base)):
                first_ref[ii, s * 96 + jc * 32 : s * 96 + jc * 32 + 32, :] = turned[
                    n * 32 : n * 32 + 32
                ]
        return carry

    lax.fori_loop(0, 8, step, 0)


def bias_kernel(held_ref, out_ref):
    both = swap_blocks(
        [
            jnp.concatenate(
                [held_ref[yl * 4 + z, 576:624, :].astype(F32)[0:40] for yl in range(2)], axis=0
            )
            for z in range(4)
        ]
    )
    tiles = []
    for yl in range(2):
        parts = [part[yl * 40 : yl * 40 + 40] for part in both]
        tiles.append([p[0:8] for p in parts] + [parts[0][24:32], parts[1][24:32]])
        tiles.append([p[8:16] for p in parts] + [parts[2][24:32], parts[3][24:32]])
        tiles.append([p[16:24] for p in parts] + [parts[0][32:40], parts[1][32:40]])
    whole = jnp.concatenate([jnp.concatenate(t, axis=0) for t in tiles], axis=1).astype(BF16)
    for copy in range(8):
        out_ref[copy] = whole


def split_kernel(held_ref, move_ref, out_ref):
    def step(s, carry):
        rows = jnp.concatenate(
            [held_ref[c, pl.ds(pl.multiple_of(s * 96, 32), 96), :] for c in range(8)], axis=0
        )
        turned = jnp.concatenate(
            [
                held_ref[yl * 4 + z, pl.ds(pl.multiple_of(s * 96 + jc * 32, 32), 32), :]
                for yl in range(2)
                for jc in range(3)
                for z in range(4)
            ],
            axis=0,
        )
        moved = jnp.dot(turned, move_ref[:, 0:256], preferred_element_type=F32).astype(BF16)
        out_ref[s, :, 0:256] = moved
        gate = jnp.dot(rows, move_ref[:, 256:384], preferred_element_type=F32)
        out_ref[s, :, 256:384] = sigmoid(gate).astype(BF16)
        return carry

    lax.fori_loop(0, 6, step, 0)


def attend_half(half, held_ref, keyed_ref, bias_ref, extra_ref, packed_ref):
    for c in range(8):
        extra_ref[c * 48 : c * 48 + 48, :] = bias_ref[c].astype(F32)
    place = lax.broadcasted_iota(jnp.int32, (24, 128), 1) // 32 - 2 * half

    def step(s, carry):
        value = jnp.concatenate([keyed_ref[s, :, 128:256], jnp.ones((768, 128), BF16)], axis=1)
        for t in range(2):
            at = [pl.ds(pl.multiple_of(s * 96 + half * 48, 16), 48)] * 4
            rows = jnp.concatenate([held_ref[t * 4 + c, at[c], :] for c in range(4)], axis=0)
            scores = lax.dot_general(
                rows, keyed_ref[s, :, 0:128], (((1,), (1,)), ((), ())), preferred_element_type=F32
            )
            scores = scores + extra_ref[t * 192 : t * 192 + 192, :]
            top = jnp.max(scores, axis=-1, keepdims=True)
            weights = jnp.exp2(scores - top).astype(BF16)
            summed = jnp.dot(weights, value, preferred_element_type=F32)
            for h in range(4):
                c = t * 4 + h
                part = summed[h * 48 : h * 48 + 48]
                gate = keyed_ref[s, pl.ds(pl.multiple_of(c * 96 + half * 48, 16), 48), 256:384]
                gated = gate.astype(F32) * (part[:, 0:128] / part[:, 128:256])
                packed_ref[pl.ds(pl.multiple_of(c * 144 + s * 24, 8), 24), :] = jnp.where(
                    place == 0, gated[0:24], jnp.where(place == 1, gated[24:48], 0.0)
                )
        return carry

    lax.fori_loop(0, 6, step, 0, unroll=UNROLL_ATTEND)


def attend_mine_kernel(held_ref, keyed_ref, bias_ref, out_ref, extra_ref, packed_ref):
    half = lax.axis_index("core")
    attend_half(half, held_ref, keyed_ref, bias_ref, extra_ref, packed_ref)
    for c in range(8):
        out_ref[c] = packed_ref[c * 144 : (c + 1) * 144, :].astype(BF16)


def attend_other_kernel(held_ref, keyed_ref, bias_ref, mine_ref, out_ref, extra_ref, packed_ref):
    half = 1 - lax.axis_index("core")
    attend_half(half, held_ref, keyed_ref, bias_ref, extra_ref, packed_ref)
    for c in range(8):
        out_ref[c] = (
            packed_ref[c * 144 : (c + 1) * 144, :] + mine_ref[c].astype(F32)
        ).astype(BF16)


def update_kernel(held_ref, first_ref, weight_ref, out_hbm, wide_ref, done_ref, out_sems):
    def store(ii):
        return pltpu.make_async_copy(done_ref.at[:, ii], out_hbm.at[:, ii], out_sems.at[ii])

    wide_ref[...] = jnp.zeros((128, 512), BF16)
    for g in range(4):
        wide_ref[g * 32 : g * 32 + 32, g * 128 : g * 128 + 128] = weight_ref[...]

    def step(ii, carry):
        add = jnp.dot(held_ref[ii], wide_ref[...], preferred_element_type=F32)
        for s in range(6):
            rows = jnp.concatenate(
                [add[s * 24 : s * 24 + 24, g * 128 : (g + 1) * 128] for g in range(4)], axis=0
            )
            first = first_ref[ii, s * 96 : (s + 1) * 96, :].astype(F32)
            done_ref[s, ii] = (first + rows).astype(BF16)
        store(ii).start()
        return carry

    lax.fori_loop(0, 8, step, 0, unroll=UNROLL_UPDATE)
    for ii in range(8):
        store(ii).wait()


def call(kernel, outs, in_specs, out_specs, scratch, limit=LIMIT_OTHER, work=0):
    cost = pl.CostEstimate(flops=work * 10**9, bytes_accessed=work * 10**6, transcendentals=0)
    return pl.pallas_call(
        kernel,
        out_shape=outs,
        in_specs=in_specs,
        out_specs=out_specs,
        scratch_shapes=scratch,
        cost_estimate=cost if work else None,
        compiler_params=pltpu.CompilerParams(vmem_limit_bytes=limit * 1024 * 1024),
    )


def shape(dims, dtype=BF16):
    return jax.ShapeDtypeStruct(dims, dtype)


def settle(values):
    return jnp.maximum(values, jnp.asarray(-3e38, values.dtype))


def exchange(values, axes):
    return lax.all_to_all(values, axes, 0, 0, tiled=True)


def body(
    pair,
    residue_mask,
    left_weight,
    right_weight,
    gate_weight,
    out_weight,
    attn_weight,
    bias_weight,
    attn_out_weight,
):
    pair = pair.reshape(6, 8, 96, 128)
    wire = call(
        project_kernel,
        shape((128, 72, 128)),
        [HBM, pl.BlockSpec(memory_space=pltpu.SMEM), HBM, HBM],
        HBM,
        [
            pltpu.VMEM((6, 8, 96, 128), BF16),
            pltpu.VMEM((72 * PITCH, 128), F32),
            pltpu.VMEM((128, 256), BF16),
            pltpu.VMEM((128, 256), BF16),
            pltpu.VMEM((512, 128), BF16),
            pltpu.VMEM((96, 128), F32),
            pltpu.VMEM((128, 72, 128), BF16),
            pltpu.SemaphoreType.DMA((4,)),
            pltpu.SemaphoreType.DMA((2,)),
            pltpu.SemaphoreType.DMA((4,)),
        ],
        LIMIT_PROJECT,
    )(pair, residue_mask, left_weight, right_weight)
    wire = exchange(wire, ALL)
    sums = call(
        triangle_kernel,
        shape((128, 40, 128)),
        [VMEM, VMEM],
        VMEM,
        [pltpu.VMEM((768, 768), BF16), pltpu.VMEM((768, 768), BF16), pltpu.VMEM((768, 768), F32)],
    )(wire, jnp.asarray(SWAP, BF16))
    sums = exchange(sums, ALL)
    sides = call(gate_kernel, shape((80, 128, 128)), [VMEM] * 2, VMEM, [], work=3)(
        pair, gate_weight
    )
    sides = settle(sides)

    col_mask = lax.dynamic_slice_in_dim(residue_mask, lax.axis_index(COL) * 96, 96).reshape(3, 32)
    chunk = lambda jc: jnp.tile(col_mask[jc], 4)
    split = jnp.concatenate([col_mask[0], col_mask[0], col_mask[1], col_mask[1]])
    mask = jnp.repeat(jnp.stack([chunk(0), chunk(1), chunk(2), split, chunk(2)]), 8, axis=0)
    send, first = call(
        first_kernel,
        (shape((8, 624, 128)), shape((40, 128, 128))),
        [VMEM] * 6,
        (VMEM, VMEM),
        [pltpu.VMEM((128 * 40, 128), F32), pltpu.VMEM((40, 128), F32)],
    )(sums, sides, out_weight, attn_weight, bias_weight[None, :], mask)
    held = exchange(send, COL)
    first, held = lax.optimization_barrier((first, held))
    bias = call(bias_kernel, shape((8, 48, 768)), [VMEM], VMEM, [])(held)
    bias = exchange(bias, ("x", "yh"))
    other = lax.ppermute(bias, "core", [(0, 1), (1, 0)])
    keyed = call(
        split_kernel, shape((6, 768, 384)), [VMEM] * 2, VMEM, [], work=WORK_SCORE
    )(held, jnp.asarray(MOVE, BF16))
    keyed = settle(keyed)
    scratch = [pltpu.VMEM((384, 768), F32), pltpu.VMEM((8 * 144, 128), F32)]
    mine = call(
        attend_mine_kernel, shape((8, 144, 128)), [VMEM] * 3, VMEM, scratch, work=WORK_MINE
    )(held, keyed, bias)
    gated = call(
        attend_other_kernel, shape((8, 144, 128)), [VMEM] * 4, VMEM, scratch, work=2
    )(held, keyed, other, mine)
    first = call(turn_kernel, shape((8, 576, 128)), [VMEM], VMEM, [], work=2)(first)
    first = settle(first)
    gated = exchange(gated, COL)
    updated = call(
        update_kernel,
        shape((6, 8, 96, 128)),
        [VMEM, VMEM, VMEM],
        HBM,
        [
            pltpu.VMEM((128, 512), BF16),
            pltpu.VMEM((6, 8, 96, 128), BF16),
            pltpu.SemaphoreType.DMA((8,)),
        ],
        LIMIT_UPDATE,
    )(gated, first, attn_out_weight)
    return updated.reshape(48, 96, 128)


def solution(mesh):
    parts = Mesh(mesh.devices.reshape(4, 2, 2, 2, 4), ALL)
    spec = P(("x", "yh", "core"), COL, None)
    return jax.shard_map(
        body,
        mesh=parts,
        in_specs=(spec, P(), P(), P(), P(), P(), P(), P(), P()),
        out_specs=spec,
        check_vma=False,
    )
```

time: 152 us -> 148 us (0.974)
  blocking collectives: 87.1 us -> 63.9 us
  starting transfers between devices: 8.37 us -> 16.8 us
  waiting for transfers between devices: 23.1 us -> 26.6 us
  Pallas kernels: 30.9 us -> 34 us
  other arithmetic: 0 us -> 2.57 us
    all_to_all x4 -> x2, blocking collectives: 87.1 us -> 63.9 us  [exchange(): return lax.all_to_all(values, axes, 0, 0, tiled=True)]
    all_to_all x1 -> x3, starting transfers between devices: 4.93 us -> 13 us  [exchange(): return lax.all_to_all(values, axes, 0, 0, tiled=True)]
    all_to_all x1 -> x3, waiting for transfers between devices: 21.5 us -> 26.6 us  [exchange(): return lax.all_to_all(values, axes, 0, 0, tiled=True)]
    pallas_call x4 -> x8, Pallas kernels: 25.1 us -> 27.7 us  [the longest x1 6.95 us: body(): call(project_kernel, shape((128, 72, 128)), [HBM, pl.BlockSpec(memory_spa...]
    max x0 -> x3, other arithmetic: none -> 2.49 us  [settle(): return jnp.maximum(values, jnp.asarray(-3e+38, values.dtype))]
    ppermute x1, waiting for transfers between devices: 1.63 us -> 0.01 us  [body(): other = lax.ppermute(bias, 'core', [(0, 1), (1, 0)])]
  transfers between devices with their start and end apart: 2 -> 4, of which waited for: 2 -> 3; matrix products, arithmetic and copies ran while one was open for 1% -> 3% of each run, Pallas kernels for 0% -> 7%
where the time goes in v3:
time: 148 us; the launch traced here: 147 us
  blocking collectives  63.9 us (43%)
  Pallas kernels  34 us (23%)
  waiting for transfers between devices  26.6 us (18%)
  starting transfers between devices  16.8 us (11%)
  local copies, waits for them, and re-layouts  3.18 us (2%)
  other arithmetic  2.57 us (2%)
    all_to_all x2, blocking collectives, exchange(): return lax.all_to_all(values, axes, 0, 0, tiled=True)  63.9 us
    all_to_all x3, waiting for transfers between devices, exchange(): return lax.all_to_all(values, axes, 0, 0, tiled=True)  26.6 us
    all_to_all x3, starting transfers between devices, exchange(): return lax.all_to_all(values, axes, 0, 0, tiled=True)  13 us
    pallas_call x1, Pallas kernels, body(): call(project_kernel, shape((128, 72, 128)), [HBM, pl.BlockSpec(memory_spa...  6.95 us
    pallas_call x1, Pallas kernels, body(): call(first_kernel, (shape((8, 624, 128)), shape((40, 128, 128))), [VMEM]...  5.88 us
    pallas_call x1, Pallas kernels, body(): call(triangle_kernel, shape((128, 40, 128)), [VMEM, VMEM], VMEM, [pltpu.V...  5.28 us
    pallas_call x1, Pallas kernels, body(): call(gate_kernel, shape((80, 128, 128)), [VMEM] * 2, VMEM, [], work=3)  4.91 us
    ppermute x1, starting transfers between devices, body(): other = lax.ppermute(bias, 'core', [(0, 1), (1, 0)])  3.75 us
  transfers between devices with their start and end apart: 4, of which 3 were waited for; matrix products, arithmetic and copies ran while one was open for 3% of the time, Pallas kernels for 7%

profile of v3, /device:TPU:1, one launch (start us, length us, event | category | flops | bytes accessed | tf_op | source)
XLA Modules:
  0.0 147.4 jit_solution(15038885127403322732)
XLA Ops:
  0.0 6.9 %shard_map.109 = bf16[128,72,128]{2,1,0:T(8,128)(2,1)} custom-call(bf16[6,8,96,128]{3,2,1,0:T(8,128)(2,1)} %bitcast.8, s32[768]{0:T(1024)} %mask_ref.1, bf16[128,256]{1,0:T(8,128)(2,1)} %left_hbm.1, bf16[128,256]{1,0:T(8,128)(2,1)} %right_hbm.1), custom_call_target="tpu_custom_call" | custom-call | tf_op jit(solution)/shard_map/pallas_call | solution.py:496
  7.0 0.0 copy-start.2
  7.0 44.4 %all_to_all.25.wire_ref = bf16[128,72,128]{2,1,0:T(8,128)(2,1)S(1)} all-to-all(bf16[128,72,128]{2,1,0:T(8,128)(2,1)} %shard_map.109), channel_id=1, replica_groups=mesh['x'=4,'yh'=2,'core'=2,'yl'=2,'z'=4] {'x','yh','core','yl','z'}, dimensions={0} | all-to-all | bytes 4718592 | tf_op jit(solution)/shard_map/all_to_all | solution.py:481
  51.4 0.0 copy-done.2
  51.4 5.3 %shard_map.110 = bf16[128,40,128]{2,1,0:T(8,128)(2,1)} custom-call(bf16[128,72,128]{2,1,0:T(8,128)(2,1)S(1)} %all_to_all.25.wire_ref, bf16[512,512]{1,0:T(8,128)(2,1)S(1)} %copy-done.2), custom_call_target="tpu_custom_call" | custom-call | tf_op jit(solution)/shard_map/pallas_call | solution.py:516
  56.7 0.0 copy-start.1
  56.7 5.9 %all-to-all-start.1 = ((bf16[128,40,128]{2,1,0:T(8,128)(2,1)}), bf16[128,40,128]{2,1,0:T(8,128)(2,1)}, u32[]{:S(2)}, u32[]{:S(2)}) async-start(bf16[128,40,128]{2,1,0:T(8,128)(2,1)} %shard_map.110), calls=%async_computation.1 | async-start | bytes 2621440 | tf_op jit(solution)/shard_map/all_to_all | solution.py:481
  62.6 0.8 dynamic_slice.3
  63.4 0.1 fusion
  63.5 0.1 stack_tile.10
  63.6 0.1 stack_tile.11
  63.6 0.1 stack_tile.12
  63.7 0.1 add_bitcast_fusion
  63.8 0.0 copy-done.1
  63.8 0.0 copy-done.9
  63.9 4.9 %shard_map.111 = bf16[80,128,128]{2,1,0:T(8,128)(2,1)S(1)} custom-call(bf16[6,8,96,128]{3,2,1,0:T(8,128)(2,1)S(1)} %bitcast.9, bf16[128,128]{1,0:T(8,128)(2,1)S(1)} %copy-done.9), custom_call_target="tpu_custom_call" | custom-call | flops 3000000000 | bytes 3000000 | tf_op jit(solution)/shard_map/pallas_call | solution.py:524
  68.8 0.0 copy-start.3
  68.8 0.0 copy-start.4
  68.8 0.0 copy-start.6
  68.8 0.2 broadcast_maximum_fusion.1.sides_ref
  69.0 15.6 %all-to-all-done.1.wire_ref = bf16[128,40,128]{2,1,0:T(8,128)(2,1)} async-done(((bf16[128,40,128]{2,1,0:T(8,128)(2,1)}), bf16[128,40,128]{2,1,0:T(8,128)(2,1)}, u32[]{:S(2)}, u32[]{:S(2)}) %all-to-all-start.1) | async-done | bytes 1310752 | tf_op jit(solution)/shard_map/all_to_all | solution.py:481
  84.6 0.0 copy-done.3
  84.6 0.0 copy-done.4
  84.6 0.0 copy-done.6
  84.6 5.9 %shard_map.112 = (bf16[8,624,128]{2,1,0:T(8,128)(2,1)S(1)}, bf16[40,128,128]{2,1,0:T(8,128)(2,1)S(1)}) custom-call(bf16[128,40,128]{2,1,0:T(8,128)(2,1)} %all-to-all-done.1.wire_ref, bf16[80,128,128]{2,1,0:T(8,128)(2,1)S(1)} %broadcast_maximum_fusion.1.sides_ref, bf16[128,128]{1,0:T(8,128)(2,1)S(1)} %copy-done.3, bf16[128,128]{1,0:T(8,128)(2,1)S(1)} %copy-done.4, ...), custom_call_target="tpu_custom_call" | custom-call | tf_op jit(solution)/shard_map/pallas_call | solution.py:533
  90.5 0.0 copy-start.7
  90.5 0.0 copy-start.10
  90.5 19.5 %all_to_all.26.held_ref = bf16[8,624,128]{2,1,0:T(8,128)(2,1)S(1)} all-to-all(bf16[8,624,128]{2,1,0:T(8,128)(2,1)S(1)} %get-tuple-element.10), channel_id=1, replica_groups=mesh['x'=4,'yh'=2,'core'=2,'yl'=2,'z'=4] {'yl','z'}, dimensions={0} | all-to-all | bytes 2555904 | tf_op jit(solution)/shard_map/all_to_all | solution.py:481
  110.0 0.0 copy-done.7
  110.0 1.0 shard_map.114
  111.0 3.5 %all-to-all-start.3 = ((bf16[8,48,768]{2,1,0:T(8,128)(2,1)}), bf16[8,48,768]{2,1,0:T(8,128)(2,1)S(1)}, u32[]{:S(2)}, u32[]{:S(2)}) async-start(bf16[8,48,768]{2,1,0:T(8,128)(2,1)} %shard_map.114), calls=%async_computation.3 | async-start | bytes 1179648 | tf_op jit(solution)/shard_map/all_to_all | solution.py:481
  114.6 0.0 copy-done.10
  114.6 0.0 copy-start.8
  114.6 1.9 %shard_map.113 = bf16[6,768,384]{2,1,0:T(8,128)(2,1)S(1)} custom-call(bf16[8,624,128]{2,1,0:T(8,128)(2,1)S(1)} %all_to_all.26.held_ref, bf16[128,384]{1,0:T(8,128)(2,1)S(1)} %copy-done.10), custom_call_target="tpu_custom_call" | custom-call | flops 30000001024 | bytes 30000000 | tf_op jit(solution)/shard_map/pallas_call | solution.py:545
  116.5 0.0 copy-done.8
  116.5 0.8 shard_map.117
  117.2 2.2 %broadcast_maximum_fusion.keyed_ref = bf16[6,768,384]{2,1,0:T(8,128)(2,1)} fusion(bf16[6,768,384]{2,1,0:T(8,128)(2,1)S(1)} %shard_map.113), kind=kLoop, calls=%fused_computation | loop fusion | flops 1769472 | bytes 7077888 | tf_op jit(solution)/shard_map/max | solution.py:477
  119.4 4.1 %all-to-all-done.3.bias_ref = bf16[8,48,768]{2,1,0:T(8,128)(2,1)S(1)} async-done(((bf16[8,48,768]{2,1,0:T(8,128)(2,1)}), bf16[8,48,768]{2,1,0:T(8,128)(2,1)S(1)}, u32[]{:S(2)}, u32[]{:S(2)}) %all-to-all-start.3) | async-done | bytes 589856 | tf_op jit(solution)/shard_map/all_to_all | solution.py:481
  123.5 3.8 %collective-permute-start = (bf16[8,48,768]{2,1,0:T(8,128)(2,1)S(1)}, bf16[8,48,768]{2,1,0:T(8,128)(2,1)S(1)}, u32[]{:S(2)}, u32[]{:S(2)}) collective-permute-start(bf16[8,48,768]{2,1,0:T(8,128)(2,1)S(1)} %all-to-all-done.3.bias_ref), channel_id=1, source_target_pairs={{0,8},{8,0},{1,9},{9,1},{2,10},{10,2},{3,11},{11,3},{4,12},{12,4},... | collective-permute-start | bytes 1769480 | tf_op jit(solution)/shard_map/ppermute | solution.py:544
  127.3 2.0 %copy-done = bf16[6,768,384]{2,1,0:T(8,128)(2,1)S(1)} copy-done((bf16[6,768,384]{2,1,0:T(8,128)(2,1)S(1)}, bf16[6,768,384]{2,1,0:T(8,128)(2,1)}, u32[]{:S(2)}) %copy-start) | copy-done | bytes 3538968
  129.3 2.6 %shard_map.115.mine_ref = bf16[8,144,128]{2,1,0:T(8,128)(2,1)S(1)} custom-call(bf16[8,624,128]{2,1,0:T(8,128)(2,1)S(1)} %all_to_all.26.held_ref, bf16[6,768,384]{2,1,0:T(8,128)(2,1)S(1)} %copy-done, bf16[8,48,768]{2,1,0:T(8,128)(2,1)S(1)} %all-to-all-done.3.bias_ref), custom_call_target="tpu_custom_call" | custom-call | flops 30000001024 | bytes 30000000 | tf_op jit(solution)/shard_map/pallas_call | solution.py:550
  131.9 0.0 collective-permute-done.bias_ref
  131.9 3.4 %shard_map.116 = bf16[8,144,128]{2,1,0:T(8,128)(2,1)} custom-call(bf16[8,624,128]{2,1,0:T(8,128)(2,1)S(1)} %all_to_all.26.held_ref, bf16[6,768,384]{2,1,0:T(8,128)(2,1)S(1)} %copy-done, bf16[8,48,768]{2,1,0:T(8,128)(2,1)S(1)} %collective-permute-done.bias_ref, bf16[8,144,128]{2,1,0:T(8,128)(2,1)S(1)} %shard_map.115.mine_ref), custom_call_target="tpu_custom_call" | custom-call | flops 2000000000 | bytes 2000000 | tf_op jit(solution)/shard_map/pallas_call | solution.py:553
  135.3 3.6 %all-to-all-start.4 = ((bf16[8,144,128]{2,1,0:T(8,128)(2,1)}), bf16[8,144,128]{2,1,0:T(8,128)(2,1)S(1)}, u32[]{:S(2)}, u32[]{:S(2)}) async-start(bf16[8,144,128]{2,1,0:T(8,128)(2,1)} %shard_map.116), calls=%async_computation.4 | async-start | bytes 589824 | tf_op jit(solution)/shard_map/all_to_all | solution.py:481
  138.9 0.1 broadcast_maximum_fusion.2.first_ref
  139.0 6.9 %all-to-all-done.4.held_ref = bf16[8,144,128]{2,1,0:T(8,128)(2,1)S(1)} async-done(((bf16[8,144,128]{2,1,0:T(8,128)(2,1)}), bf16[8,144,128]{2,1,0:T(8,128)(2,1)S(1)}, u32[]{:S(2)}, u32[]{:S(2)}) %all-to-all-start.4) | async-done | bytes 294944 | tf_op jit(solution)/shard_map/all_to_all | solution.py:481
  145.9 0.0 copy-done.5
  145.9 1.4 shard_map.118
  (8 shorter events, 0.0 us)
Async XLA Ops:
  7.0 44.5 %copy-start.2 = (bf16[512,512]{1,0:T(8,128)(2,1)S(1)}, bf16[512,512]{1,0:T(8,128)(2,1)}, u32[]{:S(2)}) copy-start(bf16[512,512]{1,0:T(8,128)(2,1)} %constant.25.clone.perm_ref) | copy-start | bytes 1572868
  56.7 7.1 %copy-start.1 = (bf16[48,96,128]{2,1,0:T(8,128)(2,1)S(1)}, bf16[48,96,128]{2,1,0:T(8,128)(2,1)}, u32[]{:S(2)}) copy-start(bf16[48,96,128]{2,1,0:T(8,128)(2,1)} %param.11) | copy-start | bytes 3538948
  56.7 7.2 %copy-start.9 = (bf16[128,128]{1,0:T(8,128)(2,1)S(1)}, bf16[128,128]{1,0:T(8,128)(2,1)}, u32[]{:S(2)}) copy-start(bf16[128,128]{1,0:T(8,128)(2,1)} %gate_w_ref.1) | copy-start | bytes 98308
  56.7 27.9 %all-to-all-start.1 = ((bf16[128,40,128]{2,1,0:T(8,128)(2,1)}), bf16[128,40,128]{2,1,0:T(8,128)(2,1)}, u32[]{:S(2)}, u32[]{:S(2)}) async-start(bf16[128,40,128]{2,1,0:T(8,128)(2,1)} %shard_map.110), calls=%async_computation.1 | async-start | bytes 2621440 | tf_op jit(solution)/shard_map/all_to_all | solution.py:481
  68.8 15.8 %copy-start.3 = (bf16[128,128]{1,0:T(8,128)(2,1)S(1)}, bf16[128,128]{1,0:T(8,128)(2,1)}, u32[]{:S(2)}) copy-start(bf16[128,128]{1,0:T(8,128)(2,1)} %out_w_ref.1) | copy-start | bytes 98308
  68.8 15.8 %copy-start.4 = (bf16[128,128]{1,0:T(8,128)(2,1)S(1)}, bf16[128,128]{1,0:T(8,128)(2,1)}, u32[]{:S(2)}) copy-start(bf16[128,128]{1,0:T(8,128)(2,1)} %attn_w_ref.1) | copy-start | bytes 98308
  68.8 15.8 %copy-start.6 = (bf16[128]{0:T(256)(128)(2,1)S(1)}, bf16[128]{0:T(256)(128)(2,1)}, u32[]{:S(2)}) copy-start(bf16[128]{0:T(256)(128)(2,1)} %param.18) | copy-start | bytes 772
  90.5 19.5 %copy-start.7 = (bf16[40,128,128]{2,1,0:T(8,128)(2,1)}, bf16[40,128,128]{2,1,0:T(8,128)(2,1)S(1)}, u32[]{:S(2)}) copy-start(bf16[40,128,128]{2,1,0:T(8,128)(2,1)S(1)} %get-tuple-element.12.slab_ref) | copy-start | bytes 3932164
  90.5 24.1 %copy-start.10 = (bf16[128,384]{1,0:T(8,128)(2,1)S(1)}, bf16[128,384]{1,0:T(8,128)(2,1)}, u32[]{:S(2)}) copy-start(bf16[128,384]{1,0:T(8,128)(2,1)} %constant.26.clone.move_ref) | copy-start | bytes 294916
  111.0 12.5 %all-to-all-start.3 = ((bf16[8,48,768]{2,1,0:T(8,128)(2,1)}), bf16[8,48,768]{2,1,0:T(8,128)(2,1)S(1)}, u32[]{:S(2)}, u32[]{:S(2)}) async-start(bf16[8,48,768]{2,1,0:T(8,128)(2,1)} %shard_map.114), calls=%async_computation.3 | async-start | bytes 1179648 | tf_op jit(solution)/shard_map/all_to_all | solution.py:481
  114.6 1.9 %copy-start.8 = (bf16[40,128,128]{2,1,0:T(8,128)(2,1)S(1)}, bf16[40,128,128]{2,1,0:T(8,128)(2,1)}, u32[]{:S(2)}) copy-start(bf16[40,128,128]{2,1,0:T(8,128)(2,1)} %copy-done.7) | copy-start | bytes 3932164
  123.5 8.4 %collective-permute-start = (bf16[8,48,768]{2,1,0:T(8,128)(2,1)S(1)}, bf16[8,48,768]{2,1,0:T(8,128)(2,1)S(1)}, u32[]{:S(2)}, u32[]{:S(2)}) collective-permute-start(bf16[8,48,768]{2,1,0:T(8,128)(2,1)S(1)} %all-to-all-done.3.bias_ref), channel_id=1, source_target_pairs={{0,8},{8,0},{1,9},{9,1},{2,10},{10,2},{3,11},{11,3},{4,12},{12,4},... | collective-permute-start | bytes 1769480 | tf_op jit(solution)/shard_map/ppermute | solution.py:544
  127.3 2.0 %copy-start = (bf16[6,768,384]{2,1,0:T(8,128)(2,1)S(1)}, bf16[6,768,384]{2,1,0:T(8,128)(2,1)}, u32[]{:S(2)}) copy-start(bf16[6,768,384]{2,1,0:T(8,128)(2,1)} %broadcast_maximum_fusion.keyed_ref) | copy-start | bytes 10616836
  135.3 10.6 %copy-start.5 = (bf16[32,128]{1,0:T(8,128)(2,1)S(1)}, bf16[32,128]{1,0:T(8,128)(2,1)}, u32[]{:S(2)}) copy-start(bf16[32,128]{1,0:T(8,128)(2,1)} %weight_ref.1) | copy-start | bytes 24580
  135.3 10.6 %all-to-all-start.4 = ((bf16[8,144,128]{2,1,0:T(8,128)(2,1)}), bf16[8,144,128]{2,1,0:T(8,128)(2,1)S(1)}, u32[]{:S(2)}, u32[]{:S(2)}) async-start(bf16[8,144,128]{2,1,0:T(8,128)(2,1)} %shard_map.116), calls=%async_computation.4 | async-start | bytes 589824 | tf_op jit(solution)/shard_map/all_to_all | solution.py:481

commit v4 on v3

--- a/solution.py
+++ b/solution.py
@@ -15,7 +15,10 @@
 PITCH = 136
 UNROLL_PROJECT = 2
 WORK_MINE = 30
-WORK_SCORE = 30
+WORK_LATE = 1
+TIE_FIRST = True
+TIE_GATE = True
+WORK_SCORE = 100
 LIMIT_OTHER = 20
 LIMIT_PROJECT = 60
 LIMIT_TRIANGLE = 20
@@ -38,16 +41,15 @@
     return (target[:, None] == at[None, :]).astype(np.float32)
 
 
-def move_matrix():
+def lanes_from(starts):
     row, lane = np.arange(128)[:, None], np.arange(128)[None, :]
-    key = (row == lane + 32) & (lane < 32)
-    return np.concatenate([key, row == lane % 32 + 64, row == lane % 32 + 96], axis=1).astype(
-        np.float32
-    )
+    return (row == np.asarray(starts)[lane // 32] + lane % 32).astype(np.float32)
 
 
 SWAP = swap_matrix()
-MOVE = move_matrix()
+KEY_MOVE = lanes_from([32, 64, 64, 64])
+GATE_MOVE = lanes_from([96, 96, 96, 96])
+SETTLE_FIRST = True
 
 
 def sigmoid(values):
@@ -239,10 +241,6 @@
 
 def gate_kernel(pair_ref, gate_w_ref, out_ref):
     gate_w = gate_w_ref[...].T
-    same = lax.broadcasted_iota(jnp.int32, (128, 128), 0) == lax.broadcasted_iota(
-        jnp.int32, (128, 128), 1
-    )
-    unit = jnp.where(same, 1.0, 0.0).astype(BF16)
 
     def step(ii, carry):
         held = [pair_ref[s, ii] for s in range(6)]
@@ -254,21 +252,17 @@
             rows = jnp.concatenate(
                 [normed[s * 96 + jc * 32 : s * 96 + jc * 32 + 32] for s, jc in chunks], axis=0
             )
-            plain = jnp.concatenate(
-                [held[s][jc * 32 : jc * 32 + 32] for s, jc in chunks], axis=0
+            gate = lax.dot_general(
+                gate_w, rows, (((1,), (1,)), ((), ())), preferred_element_type=F32
             )
-            contract = (((1,), (1,)), ((), ()))
-            gate = lax.dot_general(gate_w, rows, contract, preferred_element_type=F32)
             out_ref[base * 8 + ii] = sigmoid(gate).astype(BF16)
-            turned = lax.dot_general(unit, plain, contract, preferred_element_type=F32)
-            out_ref[40 + base * 8 + ii] = turned.astype(BF16)
         return carry
 
     lax.fori_loop(0, 8, step, 0)
 
 
 def first_kernel(
-    wire_ref, sides_ref, out_w_ref, attn_w_ref, bias_w_ref, mask_ref,
+    wire_ref, pair_ref, gate_ref, out_w_ref, attn_w_ref, bias_w_ref, mask_ref,
     send_ref, first_ref, norm_ref, bias_ref,
 ):
     def add(ch, total):
@@ -295,15 +289,24 @@
     query_scale = jnp.where(lane < 32, LOG2E / math.sqrt(32), 1.0)
     bias_w = jnp.broadcast_to(bias_w_ref[...], (16, 128))
     out_w = out_w_ref[...].T
+    same = lax.broadcasted_iota(jnp.int32, (128, 128), 0) == lax.broadcasted_iota(
+        jnp.int32, (128, 128), 1
+    )
+    unit = jnp.where(same, 1.0, 0.0).astype(BF16)
 
     def step(ii, carry):
         rows = [base * 8 + ii for base in range(5)]
         side = lambda values: jnp.concatenate(values, axis=1)
         tri = side([norm_ref[pl.ds(row, 128, stride=40), :].astype(BF16) for row in rows])
         update = jnp.dot(out_w, tri, preferred_element_type=F32)
-        first = side([sides_ref[40 + row].astype(F32) for row in rows]) + (
-            side([sides_ref[row].astype(F32) for row in rows]) * update
-        )
+        chunks = [chunk for base in range(5) for chunk in (slab_chunks(base) * 2)[:4]]
+        plain = jnp.concatenate(
+            [pair_ref[s, ii, jc * 32 : jc * 32 + 32, :] for s, jc in chunks], axis=0
+        )
+        pair = lax.dot_general(
+            unit, plain, (((1,), (1,)), ((), ())), preferred_element_type=F32
+        )
+        first = pair + side([gate_ref[row].astype(F32) for row in rows]) * update
         center = first - jnp.mean(first, axis=0, keepdims=True)
         spread = jnp.mean(center * center, axis=0, keepdims=True)
         normed = center * lax.rsqrt(spread + 1e-05)
@@ -330,14 +333,37 @@
         send_ref[ii, 576:624, :] = bias
 
 
-def turn_kernel(slab_ref, first_ref):
+def turn_kernel(slab_ref, attn_w_ref, move_ref, out_ref):
+    gate_w = jnp.dot(attn_w_ref[...], move_ref[...], preferred_element_type=F32).astype(BF16)
+    lane = lax.broadcasted_iota(jnp.int32, (24, 128), 1)
+
     def step(ii, carry):
+        first = jnp.concatenate(
+            [slab_ref[base * 8 + ii].astype(F32) for base in range(5)], axis=1
+        )
+        center = first - jnp.mean(first, axis=0, keepdims=True)
+        spread = jnp.mean(center * center, axis=0, keepdims=True)
+        normed = center * lax.rsqrt(spread + 1e-05)
+        turned = jnp.concatenate(
+            [normed[:, base * 128 : base * 128 + 128].T for base in range(5)], axis=0
+        )
+        gate = jnp.dot(turned.astype(BF16), gate_w, preferred_element_type=F32)
+        place = {}
         for base in range(5):
-            turned = slab_ref[base * 8 + ii].T
+            plain = first[:, base * 128 : base * 128 + 128].T.astype(BF16)
             for n, (s, jc) in enumerate(slab_chunks(base)):
-                first_ref[ii, s * 96 + jc * 32 : s * 96 + jc * 32 + 32, :] = turned[
+                out_ref[ii, s * 96 + jc * 32 : s * 96 + jc * 32 + 32, :] = plain[
                     n * 32 : n * 32 + 32
                 ]
+                place[s, jc] = gate[base * 128 + n * 32 : base * 128 + n * 32 + 32]
+        packed = []
+        for s in range(6):
+            whole = sigmoid(jnp.concatenate([place[s, jc] for jc in range(3)], axis=0))
+            g = [whole[q * 24 : q * 24 + 24] for q in range(4)]
+            low = jnp.where(lane < 32, g[0], g[1])
+            high = jnp.where(lane < 96, g[2], g[3])
+            packed.append(jnp.where(lane < 64, low, high))
+        out_ref[ii, 576:720, :] = jnp.concatenate(packed, axis=0).astype(BF16)
         return carry
 
     lax.fori_loop(0, 8, step, 0)
@@ -365,9 +391,6 @@
 
 def split_kernel(held_ref, move_ref, out_ref):
     def step(s, carry):
-        rows = jnp.concatenate(
-            [held_ref[c, pl.ds(pl.multiple_of(s * 96, 32), 96), :] for c in range(8)], axis=0
-        )
         turned = jnp.concatenate(
             [
                 held_ref[yl * 4 + z, pl.ds(pl.multiple_of(s * 96 + jc * 32, 32), 32), :]
@@ -377,10 +400,7 @@
             ],
             axis=0,
         )
-        moved = jnp.dot(turned, move_ref[:, 0:256], preferred_element_type=F32).astype(BF16)
-        out_ref[s, :, 0:256] = moved
-        gate = jnp.dot(rows, move_ref[:, 256:384], preferred_element_type=F32)
-        out_ref[s, :, 256:384] = sigmoid(gate).astype(BF16)
+        out_ref[s] = jnp.dot(turned, move_ref[...], preferred_element_type=F32).astype(BF16)
         return carry
 
     lax.fori_loop(0, 6, step, 0)
@@ -389,27 +409,26 @@
 def attend_half(half, held_ref, keyed_ref, bias_ref, extra_ref, packed_ref):
     for c in range(8):
         extra_ref[c * 48 : c * 48 + 48, :] = bias_ref[c].astype(F32)
-    place = lax.broadcasted_iota(jnp.int32, (24, 128), 1) // 32 - 2 * half
+    wide = lax.broadcasted_iota(jnp.int32, (192, 128), 1)
+    lane = lax.broadcasted_iota(jnp.int32, (24, 128), 1)
 
     def step(s, carry):
-        value = jnp.concatenate([keyed_ref[s, :, 128:256], jnp.ones((768, 128), BF16)], axis=1)
+        value = jnp.concatenate([keyed_ref[s], jnp.ones((768, 128), BF16)], axis=1)
+        at = pl.ds(pl.multiple_of(s * 96 + half * 48, 16), 48)
         for t in range(2):
-            at = [pl.ds(pl.multiple_of(s * 96 + half * 48, 16), 48)] * 4
-            rows = jnp.concatenate([held_ref[t * 4 + c, at[c], :] for c in range(4)], axis=0)
+            rows = jnp.concatenate([held_ref[t * 4 + c, at, :] for c in range(4)], axis=0)
+            query = jnp.where(wide < 32, rows, jnp.zeros_like(rows))
             scores = lax.dot_general(
-                rows, keyed_ref[s, :, 0:128], (((1,), (1,)), ((), ())), preferred_element_type=F32
+                query, keyed_ref[s], (((1,), (1,)), ((), ())), preferred_element_type=F32
             )
             scores = scores + extra_ref[t * 192 : t * 192 + 192, :]
             top = jnp.max(scores, axis=-1, keepdims=True)
             weights = jnp.exp2(scores - top).astype(BF16)
             summed = jnp.dot(weights, value, preferred_element_type=F32)
+            result = summed[:, 0:128] / summed[:, 128:256]
             for h in range(4):
-                c = t * 4 + h
-                part = summed[h * 48 : h * 48 + 48]
-                gate = keyed_ref[s, pl.ds(pl.multiple_of(c * 96 + half * 48, 16), 48), 256:384]
-                gated = gate.astype(F32) * (part[:, 0:128] / part[:, 128:256])
-                packed_ref[pl.ds(pl.multiple_of(c * 144 + s * 24, 8), 24), :] = jnp.where(
-                    place == 0, gated[0:24], jnp.where(place == 1, gated[24:48], 0.0)
+                packed_ref[pl.ds(pl.multiple_of((t * 4 + h) * 144 + s * 24, 8), 24), :] = jnp.where(
+                    lane < 96, result[h * 48 : h * 48 + 24], result[h * 48 + 24 : h * 48 + 48]
                 )
         return carry
 
@@ -426,10 +445,12 @@
 def attend_other_kernel(held_ref, keyed_ref, bias_ref, mine_ref, out_ref, extra_ref, packed_ref):
     half = 1 - lax.axis_index("core")
     attend_half(half, held_ref, keyed_ref, bias_ref, extra_ref, packed_ref)
+    lane = lax.broadcasted_iota(jnp.int32, (144, 128), 1)
     for c in range(8):
-        out_ref[c] = (
-            packed_ref[c * 144 : (c + 1) * 144, :] + mine_ref[c].astype(F32)
-        ).astype(BF16)
+        mine, other = mine_ref[c].astype(F32), packed_ref[c * 144 : (c + 1) * 144, :]
+        low = jnp.where(half == 0, other, mine)
+        high = jnp.where(half == 0, mine, other)
+        out_ref[c] = jnp.where(lane < 64, pltpu.roll(low, 64, 1), high).astype(BF16)
 
 
 def update_kernel(held_ref, first_ref, weight_ref, out_hbm, wide_ref, done_ref, out_sems):
@@ -441,7 +462,8 @@
         wide_ref[g * 32 : g * 32 + 32, g * 128 : g * 128 + 128] = weight_ref[...]
 
     def step(ii, carry):
-        add = jnp.dot(held_ref[ii], wide_ref[...], preferred_element_type=F32)
+        gated = held_ref[ii].astype(F32) * first_ref[ii, 576:720, :].astype(F32)
+        add = jnp.dot(gated.astype(BF16), wide_ref[...], preferred_element_type=F32)
         for s in range(6):
             rows = jnp.concatenate(
                 [add[s * 24 : s * 24 + 24, g * 128 : (g + 1) * 128] for g in range(4)], axis=0
@@ -513,6 +535,16 @@
         LIMIT_PROJECT,
     )(pair, residue_mask, left_weight, right_weight)
     wire = exchange(wire, ALL)
+    gate = call(gate_kernel, shape((40, 128, 128)), [VMEM] * 2, VMEM, [], work=3)(
+        pair, gate_weight
+    )
+
+    col_mask = lax.dynamic_slice_in_dim(residue_mask, lax.axis_index(COL) * 96, 96).reshape(3, 32)
+    chunk = lambda jc: jnp.tile(col_mask[jc], 4)
+    split = jnp.concatenate([col_mask[0], col_mask[0], col_mask[1], col_mask[1]])
+    mask = jnp.repeat(jnp.stack([chunk(0), chunk(1), chunk(2), split, chunk(2)]), 8, axis=0)
+    if TIE_GATE:
+        gate, mask, wire = lax.optimization_barrier((gate, mask, wire))
     sums = call(
         triangle_kernel,
         shape((128, 40, 128)),
@@ -521,31 +553,28 @@
         [pltpu.VMEM((768, 768), BF16), pltpu.VMEM((768, 768), BF16), pltpu.VMEM((768, 768), F32)],
     )(wire, jnp.asarray(SWAP, BF16))
     sums = exchange(sums, ALL)
-    sides = call(gate_kernel, shape((80, 128, 128)), [VMEM] * 2, VMEM, [], work=3)(
-        pair, gate_weight
-    )
-    sides = settle(sides)
-
-    col_mask = lax.dynamic_slice_in_dim(residue_mask, lax.axis_index(COL) * 96, 96).reshape(3, 32)
-    chunk = lambda jc: jnp.tile(col_mask[jc], 4)
-    split = jnp.concatenate([col_mask[0], col_mask[0], col_mask[1], col_mask[1]])
-    mask = jnp.repeat(jnp.stack([chunk(0), chunk(1), chunk(2), split, chunk(2)]), 8, axis=0)
     send, first = call(
         first_kernel,
         (shape((8, 624, 128)), shape((40, 128, 128))),
-        [VMEM] * 6,
+        [VMEM] * 7,
         (VMEM, VMEM),
         [pltpu.VMEM((128 * 40, 128), F32), pltpu.VMEM((40, 128), F32)],
-    )(sums, sides, out_weight, attn_weight, bias_weight[None, :], mask)
+    )(sums, pair, gate, out_weight, attn_weight, bias_weight[None, :], mask)
     held = exchange(send, COL)
     first, held = lax.optimization_barrier((first, held))
     bias = call(bias_kernel, shape((8, 48, 768)), [VMEM], VMEM, [])(held)
     bias = exchange(bias, ("x", "yh"))
+    first = call(turn_kernel, shape((8, 720, 128)), [VMEM] * 3, VMEM, [], work=WORK_LATE)(
+        first, attn_weight, jnp.asarray(GATE_MOVE, BF16)
+    )
+    if SETTLE_FIRST:
+        first = settle(first)
+    if TIE_FIRST:
+        first, bias = lax.optimization_barrier((first, bias))
     other = lax.ppermute(bias, "core", [(0, 1), (1, 0)])
     keyed = call(
-        split_kernel, shape((6, 768, 384)), [VMEM] * 2, VMEM, [], work=WORK_SCORE
-    )(held, jnp.asarray(MOVE, BF16))
-    keyed = settle(keyed)
+        split_kernel, shape((6, 768, 128)), [VMEM] * 2, VMEM, [], work=WORK_SCORE
+    )(held, jnp.asarray(KEY_MOVE, BF16))
     scratch = [pltpu.VMEM((384, 768), F32), pltpu.VMEM((8 * 144, 128), F32)]
     mine = call(
         attend_mine_kernel, shape((8, 144, 128)), [VMEM] * 3, VMEM, scratch, work=WORK_MINE
@@ -553,8 +582,6 @@
     gated = call(
         attend_other_kernel, shape((8, 144, 128)), [VMEM] * 4, VMEM, scratch, work=2
     )(held, keyed, other, mine)
-    first = call(turn_kernel, shape((8, 576, 128)), [VMEM], VMEM, [], work=2)(first)
-    first = settle(first)
     gated = exchange(gated, COL)
     updated = call(
         update_kernel,

time: 148 us -> 144 us (0.973)
  blocking collectives: 63.9 us -> 56 us
  local copies, waits for them, and re-layouts: 3.18 us -> 9.48 us
  other arithmetic: 2.57 us -> 0.2 us
  Pallas kernels: 34 us -> 31.9 us
  starting transfers between devices: 16.8 us -> 18.8 us
    all_to_all x2 -> x3, blocking collectives: 63.9 us -> 56 us  [exchange(): return lax.all_to_all(values, axes, 0, 0, tiled=True)]
    another operation x4, local copies, waits for them, and re-layouts: 0.28 us -> 2.68 us  [body(): jnp.stack([chunk(0), chunk(1), chunk(2), split, chunk(2)])]
    max x3 -> x1, other arithmetic: 2.49 us -> 0.13 us  [settle(): return jnp.maximum(values, jnp.asarray(-3e+38, values.dtype))]
    unnamed x22 -> x28, local copies, waits for them, and re-layouts: 2.05 us -> 4.18 us
    all_to_all x3 -> x2, starting transfers between devices: 13 us -> 15 us  [exchange(): return lax.all_to_all(values, axes, 0, 0, tiled=True)]
    all_to_all x3 -> x2, waiting for transfers between devices: 26.6 us -> 26.7 us  [exchange(): return lax.all_to_all(values, axes, 0, 0, tiled=True)]
  transfers between devices with their start and end apart: 4 -> 3, of which waited for: 3 -> 2; matrix products, arithmetic and copies ran while one was open for 3% -> 4% of each run, Pallas kernels for 7% -> 7%
where the time goes in v4:
time: 144 us; the launch traced here: 143 us
  blocking collectives  56 us (39%)
  Pallas kernels  31.9 us (22%)
  waiting for transfers between devices  26.8 us (19%)
  starting transfers between devices  18.8 us (13%)
  local copies, waits for them, and re-layouts  9.48 us (7%)
    all_to_all x3, blocking collectives, exchange(): return lax.all_to_all(values, axes, 0, 0, tiled=True)  56 us
    all_to_all x2, waiting for transfers between devices, exchange(): return lax.all_to_all(values, axes, 0, 0, tiled=True)  26.7 us
    all_to_all x2, starting transfers between devices, exchange(): return lax.all_to_all(values, axes, 0, 0, tiled=True)  15 us
    pallas_call x1, Pallas kernels, body(): call(project_kernel, shape((128, 72, 128)), [HBM, pl.BlockSpec(memory_spa...  6.95 us
    pallas_call x1, Pallas kernels, body(): call(first_kernel, (shape((8, 624, 128)), shape((40, 128, 128))), [VMEM]...  5.11 us
    pallas_call x1, Pallas kernels, body(): call(triangle_kernel, shape((128, 40, 128)), [VMEM, VMEM], VMEM, [pltpu.V...  4.22 us
    unnamed x28, local copies, waits for them, and re-layouts  4.18 us
    pallas_call x1, Pallas kernels, body(): call(gate_kernel, shape((40, 128, 128)), [VMEM] * 2, VMEM, [], work=3)  3.77 us
  transfers between devices with their start and end apart: 3, of which 2 were waited for; matrix products, arithmetic and copies ran while one was open for 4% of the time, Pallas kernels for 7%

profile of v4, /device:TPU:1, one launch (start us, length us, event | category | flops | bytes accessed | tf_op | source)
XLA Modules:
  0.0 143.5 jit_solution(17576183522957872244)
XLA Ops:
  0.0 6.9 %shard_map.119 = bf16[128,72,128]{2,1,0:T(8,128)(2,1)} custom-call(bf16[6,8,96,128]{3,2,1,0:T(8,128)(2,1)} %bitcast.8, s32[768]{0:T(1024)} %mask_ref.1, bf16[128,256]{1,0:T(8,128)(2,1)} %left_hbm.1, bf16[128,256]{1,0:T(8,128)(2,1)} %right_hbm.1), custom_call_target="tpu_custom_call" | custom-call | tf_op jit(solution)/shard_map/pallas_call | solution.py:518
  7.0 0.0 copy-start
  7.0 11.5 %all-to-all-start = ((bf16[128,72,128]{2,1,0:T(8,128)(2,1)}), bf16[128,72,128]{2,1,0:T(8,128)(2,1)S(1)}, u32[]{:S(2)}, u32[]{:S(2)}) async-start(bf16[128,72,128]{2,1,0:T(8,128)(2,1)} %shard_map.119), calls=%async_computation | async-start | bytes 4718592 | tf_op jit(solution)/shard_map/all_to_all | solution.py:503
  18.5 0.8 dynamic_slice.3
  19.2 0.6 fusion
  19.8 0.7 stack_tile.10
  20.5 0.7 stack_tile.11
  21.2 0.7 tile.8
  21.8 0.6 stack_tile.12
  22.4 0.1 add_bitcast_fusion
  22.5 0.8 stack.7
  23.3 0.6 broadcast_bitcast_fusion.mask_ref
  23.9 0.0 copy-done
  23.9 0.8 copy-done.9
  24.6 3.8 %shard_map.118.gate_ref = bf16[40,128,128]{2,1,0:T(8,128)(2,1)S(1)} custom-call(bf16[6,8,96,128]{3,2,1,0:T(8,128)(2,1)S(1)} %bitcast.9, bf16[128,128]{1,0:T(8,128)(2,1)S(1)} %copy-done.9), custom_call_target="tpu_custom_call" | custom-call | flops 3000000000 | bytes 3000000 | tf_op jit(solution)/shard_map/pallas_call | solution.py:538
  28.4 0.0 copy-start.1
  28.4 1.0 copy-done.1
  29.5 21.9 %all-to-all-done.wire_ref = bf16[128,72,128]{2,1,0:T(8,128)(2,1)S(1)} async-done(((bf16[128,72,128]{2,1,0:T(8,128)(2,1)}), bf16[128,72,128]{2,1,0:T(8,128)(2,1)S(1)}, u32[]{:S(2)}, u32[]{:S(2)}) %all-to-all-start) | async-done | bytes 2359328 | tf_op jit(solution)/shard_map/all_to_all | solution.py:503
  51.4 1.0 copy-done.3
  52.4 4.2 %shard_map.120 = bf16[128,40,128]{2,1,0:T(8,128)(2,1)S(1)} custom-call(bf16[128,72,128]{2,1,0:T(8,128)(2,1)S(1)} %all-to-all-done.wire_ref, bf16[512,512]{1,0:T(8,128)(2,1)S(1)} %copy-done.3), custom_call_target="tpu_custom_call" | custom-call | tf_op jit(solution)/shard_map/pallas_call | solution.py:548
  56.7 0.0 copy-start.2
  56.7 0.0 copy-start.4
  56.7 0.0 copy-start.5
  56.7 0.0 copy-start.6
  56.7 0.0 copy-start.8
  56.7 26.6 %all_to_all.25.wire_ref = bf16[128,40,128]{2,1,0:T(8,128)(2,1)S(1)} all-to-all(bf16[128,40,128]{2,1,0:T(8,128)(2,1)S(1)} %shard_map.120), channel_id=1, replica_groups=mesh['x'=4,'yh'=2,'core'=2,'yl'=2,'z'=4] {'x','yh','core','yl','z'}, dimensions={0} | all-to-all | bytes 2621440 | tf_op jit(solution)/shard_map/all_to_all | solution.py:503
  83.3 0.0 copy-done.2
  83.3 0.0 copy-done.4
  83.3 0.0 copy-done.5
  83.3 5.1 %shard_map.121 = (bf16[8,624,128]{2,1,0:T(8,128)(2,1)S(1)}, bf16[40,128,128]{2,1,0:T(8,128)(2,1)S(1)}) custom-call(bf16[128,40,128]{2,1,0:T(8,128)(2,1)S(1)} %all_to_all.25.wire_ref, bf16[6,8,96,128]{3,2,1,0:T(8,128)(2,1)S(1)} %bitcast.10, bf16[40,128,128]{2,1,0:T(8,128)(2,1)S(1)} %copy-done.2, bf16[128,128]{1,0:T(8,128)(2,1)S(1)} %copy-done.5, ...), custom_call_target="tpu_custom_call" | custom-call | tf_op jit(solution)/shard_map/pallas_call | solution.py:556
  88.4 19.4 %all_to_all.26.held_ref = bf16[8,624,128]{2,1,0:T(8,128)(2,1)S(1)} all-to-all(bf16[8,624,128]{2,1,0:T(8,128)(2,1)S(1)} %get-tuple-element.18), channel_id=1, replica_groups=mesh['x'=4,'yh'=2,'core'=2,'yl'=2,'z'=4] {'yl','z'}, dimensions={0} | all-to-all | bytes 2555904 | tf_op jit(solution)/shard_map/all_to_all | solution.py:503
  107.8 1.0 shard_map.124
  108.8 3.5 %all-to-all-start.3 = ((bf16[8,48,768]{2,1,0:T(8,128)(2,1)}), bf16[8,48,768]{2,1,0:T(8,128)(2,1)S(1)}, u32[]{:S(2)}, u32[]{:S(2)}) async-start(bf16[8,48,768]{2,1,0:T(8,128)(2,1)} %shard_map.124), calls=%async_computation.3 | async-start | bytes 1179648 | tf_op jit(solution)/shard_map/all_to_all | solution.py:503
  112.4 0.0 copy-done.11
  112.4 0.0 copy-start.10
  112.4 1.2 shard_map.122.keyed_ref
  113.6 0.0 copy-start.12
  113.6 2.8 %shard_map.123 = bf16[8,720,128]{2,1,0:T(8,128)(2,1)S(1)} custom-call(bf16[40,128,128]{2,1,0:T(8,128)(2,1)S(1)} %get-tuple-element.20.slab_ref, bf16[128,128]{1,0:T(8,128)(2,1)S(1)} %copy-done.6, bf16[128,128]{1,0:T(8,128)(2,1)S(1)} %copy-done.10), custom_call_target="tpu_custom_call" | custom-call | flops 1000000000 | bytes 1000000 | tf_op jit(solution)/shard_map/pallas_call | solution.py:567
  116.4 0.1 broadcast_maximum_fusion.first_ref
  116.5 4.8 %all-to-all-done.3.bias_ref = bf16[8,48,768]{2,1,0:T(8,128)(2,1)S(1)} async-done(((bf16[8,48,768]{2,1,0:T(8,128)(2,1)}), bf16[8,48,768]{2,1,0:T(8,128)(2,1)S(1)}, u32[]{:S(2)}, u32[]{:S(2)}) %all-to-all-start.3) | async-done | bytes 589856 | tf_op jit(solution)/shard_map/all_to_all | solution.py:503
  121.3 3.8 %collective-permute-start = (bf16[8,48,768]{2,1,0:T(8,128)(2,1)S(1)}, bf16[8,48,768]{2,1,0:T(8,128)(2,1)S(1)}, u32[]{:S(2)}, u32[]{:S(2)}) collective-permute-start(bf16[8,48,768]{2,1,0:T(8,128)(2,1)S(1)} %all-to-all-done.3.bias_ref), channel_id=1, source_target_pairs={{0,8},{8,0},{1,9},{9,1},{2,10},{10,2},{3,11},{11,3},{4,12},{12,4},... | collective-permute-start | bytes 1769480 | tf_op jit(solution)/shard_map/ppermute | solution.py:574
  125.1 1.3 copy-done.13
  126.3 2.7 %shard_map.125.mine_ref = bf16[8,144,128]{2,1,0:T(8,128)(2,1)S(1)} custom-call(bf16[8,624,128]{2,1,0:T(8,128)(2,1)S(1)} %all_to_all.26.held_ref, bf16[6,768,128]{2,1,0:T(8,128)(2,1)S(1)} %copy-done.13, bf16[8,48,768]{2,1,0:T(8,128)(2,1)S(1)} %all-to-all-done.3.bias_ref), custom_call_target="tpu_custom_call" | custom-call | flops 30000001024 | bytes 30000000 | tf_op jit(solution)/shard_map/pallas_call | solution.py:579
  129.0 0.0 copy-start.7
  129.0 0.0 collective-permute-done.bias_ref
  129.0 2.8 %shard_map.126 = bf16[8,144,128]{2,1,0:T(8,128)(2,1)S(1)} custom-call(bf16[8,624,128]{2,1,0:T(8,128)(2,1)S(1)} %all_to_all.26.held_ref, bf16[6,768,128]{2,1,0:T(8,128)(2,1)S(1)} %copy-done.13, bf16[8,48,768]{2,1,0:T(8,128)(2,1)S(1)} %collective-permute-done.bias_ref, bf16[8,144,128]{2,1,0:T(8,128)(2,1)S(1)} %shard_map.125.mine_ref), custom_call_target="tpu_custom_call" | custom-call | flops 2000000000 | bytes 2000000 | tf_op jit(solution)/shard_map/pallas_call | solution.py:582
  131.8 10.1 %all_to_all.27.held_ref = bf16[8,144,128]{2,1,0:T(8,128)(2,1)S(1)} all-to-all(bf16[8,144,128]{2,1,0:T(8,128)(2,1)S(1)} %shard_map.126), channel_id=1, replica_groups=mesh['x'=4,'yh'=2,'core'=2,'yl'=2,'z'=4] {'yl','z'}, dimensions={0} | all-to-all | bytes 589824 | tf_op jit(solution)/shard_map/all_to_all | solution.py:503
  141.9 1.4 shard_map.127
  (11 shorter events, 0.0 us)
Async XLA Ops:
  7.0 16.9 %copy-start = (bf16[48,96,128]{2,1,0:T(8,128)(2,1)S(1)}, bf16[48,96,128]{2,1,0:T(8,128)(2,1)}, u32[]{:S(2)}) copy-start(bf16[48,96,128]{2,1,0:T(8,128)(2,1)} %param.12) | copy-start | bytes 3538948
  7.0 44.4 %all-to-all-start = ((bf16[128,72,128]{2,1,0:T(8,128)(2,1)}), bf16[128,72,128]{2,1,0:T(8,128)(2,1)S(1)}, u32[]{:S(2)}, u32[]{:S(2)}) async-start(bf16[128,72,128]{2,1,0:T(8,128)(2,1)} %shard_map.119), calls=%async_computation | async-start | bytes 4718592 | tf_op jit(solution)/shard_map/all_to_all | solution.py:503
  23.9 0.8 copy-start.9
  28.4 1.1 copy-start.1
  51.4 1.0 copy-start.3
  56.7 26.6 %copy-start.2 = (bf16[40,128,128]{2,1,0:T(8,128)(2,1)S(1)}, bf16[40,128,128]{2,1,0:T(8,128)(2,1)}, u32[]{:S(2)}) copy-start(bf16[40,128,128]{2,1,0:T(8,128)(2,1)} %copy-done.1) | copy-start | bytes 3932164
  56.7 26.6 %copy-start.4 = (s32[40,128]{1,0:T(8,128)S(1)}, s32[40,128]{1,0:T(8,128)}, u32[]{:S(2)}) copy-start(s32[40,128]{1,0:T(8,128)} %broadcast_bitcast_fusion.mask_ref) | copy-start | bytes 61444
  56.7 26.6 %copy-start.5 = (bf16[128,128]{1,0:T(8,128)(2,1)S(1)}, bf16[128,128]{1,0:T(8,128)(2,1)}, u32[]{:S(2)}) copy-start(bf16[128,128]{1,0:T(8,128)(2,1)} %out_w_ref.1) | copy-start | bytes 98308
  56.7 26.6 %copy-start.6 = (bf16[128,128]{1,0:T(8,128)(2,1)S(1)}, bf16[128,128]{1,0:T(8,128)(2,1)}, u32[]{:S(2)}) copy-start(bf16[128,128]{1,0:T(8,128)(2,1)} %attn_w_ref.3) | copy-start | bytes 98308
  56.7 26.6 %copy-start.8 = (bf16[128]{0:T(256)(128)(2,1)S(1)}, bf16[128]{0:T(256)(128)(2,1)}, u32[]{:S(2)}) copy-start(bf16[128]{0:T(256)(128)(2,1)} %param.19) | copy-start | bytes 772
  107.8 4.6 %copy-start.11 = (bf16[128,128]{1,0:T(8,128)(2,1)S(1)}, bf16[128,128]{1,0:T(8,128)(2,1)}, u32[]{:S(2)}) copy-start(bf16[128,128]{1,0:T(8,128)(2,1)} %constant.27.clone.move_ref) | copy-start | bytes 98308
  108.8 12.5 %all-to-all-start.3 = ((bf16[8,48,768]{2,1,0:T(8,128)(2,1)}), bf16[8,48,768]{2,1,0:T(8,128)(2,1)S(1)}, u32[]{:S(2)}, u32[]{:S(2)}) async-start(bf16[8,48,768]{2,1,0:T(8,128)(2,1)} %shard_map.124), calls=%async_computation.3 | async-start | bytes 1179648 | tf_op jit(solution)/shard_map/all_to_all | solution.py:503
  112.4 1.2 copy-start.10
  113.6 2.8 %copy-start.12 = (bf16[6,768,128]{2,1,0:T(8,128)(2,1)}, bf16[6,768,128]{2,1,0:T(8,128)(2,1)S(1)}, u32[]{:S(2)}) copy-start(bf16[6,768,128]{2,1,0:T(8,128)(2,1)S(1)} %shard_map.122.keyed_ref) | copy-start | bytes 3538948
  121.3 7.7 %collective-permute-start = (bf16[8,48,768]{2,1,0:T(8,128)(2,1)S(1)}, bf16[8,48,768]{2,1,0:T(8,128)(2,1)S(1)}, u32[]{:S(2)}, u32[]{:S(2)}) collective-permute-start(bf16[8,48,768]{2,1,0:T(8,128)(2,1)S(1)} %all-to-all-done.3.bias_ref), channel_id=1, source_target_pairs={{0,8},{8,0},{1,9},{9,1},{2,10},{10,2},{3,11},{11,3},{4,12},{12,4},... | collective-permute-start | bytes 1769480 | tf_op jit(solution)/shard_map/ppermute | solution.py:574
  125.1 1.3 copy-start.13
  129.0 12.9 %copy-start.7 = (bf16[32,128]{1,0:T(8,128)(2,1)S(1)}, bf16[32,128]{1,0:T(8,128)(2,1)}, u32[]{:S(2)}) copy-start(bf16[32,128]{1,0:T(8,128)(2,1)} %weight_ref.1) | copy-start | bytes 24580

commit v5 on v4

--- a/solution.py
+++ b/solution.py
@@ -16,40 +16,31 @@
 UNROLL_PROJECT = 2
 WORK_MINE = 30
 WORK_LATE = 1
-TIE_FIRST = True
-TIE_GATE = True
 WORK_SCORE = 100
 LIMIT_OTHER = 20
 LIMIT_PROJECT = 60
 LIMIT_TRIANGLE = 20
 LIMIT_FIRST = 20
 LIMIT_UPDATE = 20
-UNROLL_UNPACK = 4
+UNROLL_UNPACK = 8
 UNROLL_PACK = 2
-UNROLL_FIRST = 2
+UNROLL_FIRST = 8
 UNROLL_ATTEND = 6
-UNROLL_UPDATE = 4
+PARTS = 2
+UNROLL_UPDATE = 8
 ALL = ("x", "yh", "core", "yl", "z")
 COL = ("yl", "z")
 VMEM = pl.BlockSpec(memory_space=pltpu.VMEM)
 HBM = pl.BlockSpec(memory_space=pltpu.HBM)
 
 
-def swap_matrix():
-    at = np.arange(512)
-    target = at % 128 // 32 * 128 + at // 128 * 32 + at % 32
-    return (target[:, None] == at[None, :]).astype(np.float32)
-
-
 def lanes_from(starts):
     row, lane = np.arange(128)[:, None], np.arange(128)[None, :]
     return (row == np.asarray(starts)[lane // 32] + lane % 32).astype(np.float32)
 
 
-SWAP = swap_matrix()
 KEY_MOVE = lanes_from([32, 64, 64, 64])
 GATE_MOVE = lanes_from([96, 96, 96, 96])
-SETTLE_FIRST = True
 
 
 def sigmoid(values):
@@ -163,7 +154,17 @@
         copy.wait()
 
 
-def triangle_kernel(wire_ref, perm_ref, out_ref, left_ref, right_ref, sums_ref):
+def triangle_kernel(wire_ref, out_ref, left_ref, right_ref, sums_ref, perm_ref):
+    row = lax.broadcasted_iota(jnp.int32, (128, 128), 0)
+    col = lax.broadcasted_iota(jnp.int32, (128, 128), 1)
+    same = jnp.bitwise_and(row, 31) == jnp.bitwise_and(col, 31)
+    for z in range(4):
+        for b in range(4):
+            hit = same & (row >= b * 32) & (row < b * 32 + 32) & (col >= z * 32) & (col < z * 32 + 32)
+            perm_ref[z * 128 : z * 128 + 128, b * 128 : b * 128 + 128] = jnp.where(
+                hit, 1.0, 0.0
+            ).astype(BF16)
+
     def unpack(c_pair, carry):
         groups = [(half, yl) for half in range(2) for yl in range(2)]
         source = lambda half, yl, z: wire_ref[(c_pair * 2 + half) * 8 + yl * 4 + z]
@@ -328,9 +329,14 @@
 
     lax.fori_loop(0, 8, step, 0, unroll=UNROLL_FIRST)
     bias = jnp.where(mask_ref[...] > 0, bias_ref[...] * LOG2E, -1e9 * LOG2E)
-    bias = jnp.concatenate([bias, jnp.zeros((8, 128), F32)], axis=0).astype(BF16)
-    for ii in range(8):
-        send_ref[ii, 576:624, :] = bias
+    bias = jnp.concatenate([bias, jnp.zeros((8, 128), F32)], axis=0)
+    wide = lax.broadcasted_iota(jnp.int32, (48, 128), 1)
+    for g in range(4):
+        rows = slice(g * 48, g * 48 + 48)
+        part = bias if g == 3 else pltpu.roll(bias, 96 - 32 * g, 1)
+        for ii in range(8):
+            held = send_ref[ii, rows, :].astype(F32)
+            send_ref[ii, rows, :] = jnp.where(wide < 96, held, part).astype(BF16)
 
 
 def turn_kernel(slab_ref, attn_w_ref, move_ref, out_ref):
@@ -370,13 +376,16 @@
 
 
 def bias_kernel(held_ref, out_ref):
+    wide = lax.broadcasted_iota(jnp.int32, (48, 128), 1)
+
+    def slabs(block):
+        g = [held_ref[block, q * 48 : q * 48 + 48, :].astype(F32) for q in range(4)]
+        g = [pltpu.roll(g[q], 32 * q + 32, 1) for q in range(3)] + [g[3]]
+        low = jnp.where(wide < 32, g[0], g[1])
+        return jnp.where(wide < 64, low, jnp.where(wide < 96, g[2], g[3]))[0:40]
+
     both = swap_blocks(
-        [
-            jnp.concatenate(
-                [held_ref[yl * 4 + z, 576:624, :].astype(F32)[0:40] for yl in range(2)], axis=0
-            )
-            for z in range(4)
-        ]
+        [jnp.concatenate([slabs(yl * 4 + z) for yl in range(2)], axis=0) for z in range(4)]
     )
     tiles = []
     for yl in range(2):
@@ -409,25 +418,30 @@
 def attend_half(half, held_ref, keyed_ref, bias_ref, extra_ref, packed_ref):
     for c in range(8):
         extra_ref[c * 48 : c * 48 + 48, :] = bias_ref[c].astype(F32)
-    wide = lax.broadcasted_iota(jnp.int32, (192, 128), 1)
+    blocks = 8 // PARTS
+    size = blocks * 48
+    wide = lax.broadcasted_iota(jnp.int32, (size, 128), 1)
     lane = lax.broadcasted_iota(jnp.int32, (24, 128), 1)
 
     def step(s, carry):
         value = jnp.concatenate([keyed_ref[s], jnp.ones((768, 128), BF16)], axis=1)
         at = pl.ds(pl.multiple_of(s * 96 + half * 48, 16), 48)
-        for t in range(2):
-            rows = jnp.concatenate([held_ref[t * 4 + c, at, :] for c in range(4)], axis=0)
+        for t in range(PARTS):
+            rows = jnp.concatenate(
+                [held_ref[t * blocks + c, at, :] for c in range(blocks)], axis=0
+            )
             query = jnp.where(wide < 32, rows, jnp.zeros_like(rows))
             scores = lax.dot_general(
                 query, keyed_ref[s], (((1,), (1,)), ((), ())), preferred_element_type=F32
             )
-            scores = scores + extra_ref[t * 192 : t * 192 + 192, :]
+            scores = scores + extra_ref[t * size : (t + 1) * size, :]
             top = jnp.max(scores, axis=-1, keepdims=True)
             weights = jnp.exp2(scores - top).astype(BF16)
             summed = jnp.dot(weights, value, preferred_element_type=F32)
             result = summed[:, 0:128] / summed[:, 128:256]
-            for h in range(4):
-                packed_ref[pl.ds(pl.multiple_of((t * 4 + h) * 144 + s * 24, 8), 24), :] = jnp.where(
+            for h in range(blocks):
+                row = pl.multiple_of((t * blocks + h) * 144 + s * 24, 8)
+                packed_ref[pl.ds(row, 24), :] = jnp.where(
                     lane < 96, result[h * 48 : h * 48 + 24], result[h * 48 + 24 : h * 48 + 48]
                 )
         return carry
@@ -493,10 +507,6 @@
 
 def shape(dims, dtype=BF16):
     return jax.ShapeDtypeStruct(dims, dtype)
-
-
-def settle(values):
-    return jnp.maximum(values, jnp.asarray(-3e38, values.dtype))
 
 
 def exchange(values, axes):
@@ -543,19 +553,23 @@
     chunk = lambda jc: jnp.tile(col_mask[jc], 4)
     split = jnp.concatenate([col_mask[0], col_mask[0], col_mask[1], col_mask[1]])
     mask = jnp.repeat(jnp.stack([chunk(0), chunk(1), chunk(2), split, chunk(2)]), 8, axis=0)
-    if TIE_GATE:
-        gate, mask, wire = lax.optimization_barrier((gate, mask, wire))
+    gate, mask, wire = lax.optimization_barrier((gate, mask, wire))
     sums = call(
         triangle_kernel,
         shape((128, 40, 128)),
-        [VMEM, VMEM],
+        [VMEM],
         VMEM,
-        [pltpu.VMEM((768, 768), BF16), pltpu.VMEM((768, 768), BF16), pltpu.VMEM((768, 768), F32)],
-    )(wire, jnp.asarray(SWAP, BF16))
+        [
+            pltpu.VMEM((768, 768), BF16),
+            pltpu.VMEM((768, 768), BF16),
+            pltpu.VMEM((768, 768), F32),
+            pltpu.VMEM((512, 512), BF16),
+        ],
+    )(wire)
     sums = exchange(sums, ALL)
     send, first = call(
         first_kernel,
-        (shape((8, 624, 128)), shape((40, 128, 128))),
+        (shape((8, 576, 128)), shape((40, 128, 128))),
         [VMEM] * 7,
         (VMEM, VMEM),
         [pltpu.VMEM((128 * 40, 128), F32), pltpu.VMEM((40, 128), F32)],
@@ -567,10 +581,7 @@
     first = call(turn_kernel, shape((8, 720, 128)), [VMEM] * 3, VMEM, [], work=WORK_LATE)(
         first, attn_weight, jnp.asarray(GATE_MOVE, BF16)
     )
-    if SETTLE_FIRST:
-        first = settle(first)
-    if TIE_FIRST:
-        first, bias = lax.optimization_barrier((first, bias))
+    first, bias = lax.optimization_barrier((first, bias))
     other = lax.ppermute(bias, "core", [(0, 1), (1, 0)])
     keyed = call(
         split_kernel, shape((6, 768, 128)), [VMEM] * 2, VMEM, [], work=WORK_SCORE

time: 144 us -> 141 us (0.979)
    unnamed x28 -> x34, local copies, waits for them, and re-layouts: 4.18 us -> 4.16 us
where the time goes in v5:
time: 141 us
  blocking collectives  55 us (39%)
  Pallas kernels  31 us (22%)
  waiting for transfers between devices  26 us (18%)
  starting transfers between devices  18.8 us (13%)
  local copies, waits for them, and re-layouts  9.38 us (7%)
    all_to_all x3, blocking collectives, exchange(): return lax.all_to_all(values, axes, 0, 0, tiled=True)  55 us
    all_to_all x2, waiting for transfers between devices, exchange(): return lax.all_to_all(values, axes, 0, 0, tiled=True)  26 us
    all_to_all x2, starting transfers between devices, exchange(): return lax.all_to_all(values, axes, 0, 0, tiled=True)  15 us
    pallas_call x1, Pallas kernels, body(): call(project_kernel, shape((128, 72, 128)), [HBM, pl.BlockSpec(memory_spa...  6.96 us
    pallas_call x1, Pallas kernels, body(): call(first_kernel, (shape((8, 576, 128)), shape((40, 128, 128))), [VMEM]...  4.56 us
    unnamed x34, local copies, waits for them, and re-layouts  4.16 us
    pallas_call x1, Pallas kernels, body(): call(triangle_kernel, shape((128, 40, 128)), [VMEM], VMEM, [pltpu.VMEM((7...  3.92 us
    pallas_call x1, Pallas kernels, body(): call(gate_kernel, shape((40, 128, 128)), [VMEM] * 2, VMEM, [], work=3)  3.77 us
  transfers between devices with their start and end apart: 3, of which 2 were waited for; matrix products, arithmetic and copies ran while one was open for 4% of the time, Pallas kernels for 7%

profile of v5, /device:TPU:1, one launch (start us, length us, event | category | flops | bytes accessed | tf_op | source)
XLA Modules:
  0.0 140.6 jit_solution(8934376682468239618)
XLA Ops:
  0.0 7.0 %shard_map.110 = bf16[128,72,128]{2,1,0:T(8,128)(2,1)} custom-call(bf16[6,8,96,128]{3,2,1,0:T(8,128)(2,1)} %bitcast.8, s32[768]{0:T(1024)} %mask_ref.1, bf16[128,256]{1,0:T(8,128)(2,1)} %left_hbm.1, bf16[128,256]{1,0:T(8,128)(2,1)} %right_hbm.1), custom_call_target="tpu_custom_call" | custom-call | tf_op jit(solution)/shard_map/pallas_call | solution.py:528
  7.0 0.0 copy-start
  7.0 11.5 %all-to-all-start = ((bf16[128,72,128]{2,1,0:T(8,128)(2,1)}), bf16[128,72,128]{2,1,0:T(8,128)(2,1)S(1)}, u32[]{:S(2)}, u32[]{:S(2)}) async-start(bf16[128,72,128]{2,1,0:T(8,128)(2,1)} %shard_map.110), calls=%async_computation | async-start | bytes 4718592 | tf_op jit(solution)/shard_map/all_to_all | solution.py:513
  18.5 0.8 dynamic_slice.3
  19.3 0.6 fusion
  19.8 0.7 stack_tile.10
  20.5 0.6 stack_tile.11
  21.1 0.7 tile.8
  21.8 0.6 stack_tile.12
  22.4 0.1 add_bitcast_fusion
  22.4 0.8 stack.7
  23.2 0.6 broadcast_bitcast_fusion.mask_ref
  23.8 0.0 copy-done
  23.8 0.8 copy-done.11
  24.6 3.8 %shard_map.109.gate_ref = bf16[40,128,128]{2,1,0:T(8,128)(2,1)S(1)} custom-call(bf16[6,8,96,128]{3,2,1,0:T(8,128)(2,1)S(1)} %bitcast.9, bf16[128,128]{1,0:T(8,128)(2,1)S(1)} %copy-done.11), custom_call_target="tpu_custom_call" | custom-call | flops 3000000000 | bytes 3000000 | tf_op jit(solution)/shard_map/pallas_call | solution.py:548
  28.3 0.0 copy-start.1
  28.4 1.0 copy-done.1
  29.4 22.0 %all-to-all-done.wire_ref = bf16[128,72,128]{2,1,0:T(8,128)(2,1)S(1)} async-done(((bf16[128,72,128]{2,1,0:T(8,128)(2,1)}), bf16[128,72,128]{2,1,0:T(8,128)(2,1)S(1)}, u32[]{:S(2)}, u32[]{:S(2)}) %all-to-all-start) | async-done | bytes 2359328 | tf_op jit(solution)/shard_map/all_to_all | solution.py:513
  51.4 3.9 %shard_map.111 = bf16[128,40,128]{2,1,0:T(8,128)(2,1)S(1)} custom-call(bf16[128,72,128]{2,1,0:T(8,128)(2,1)S(1)} %all-to-all-done.wire_ref), custom_call_target="tpu_custom_call" | custom-call | tf_op jit(solution)/shard_map/pallas_call | solution.py:557
  55.3 0.0 copy-start.2
  55.4 0.0 copy-start.3
  55.4 0.0 copy-start.4
  55.4 0.0 copy-start.5
  55.4 0.0 copy-start.8
  55.4 26.6 %all_to_all.25.wire_ref = bf16[128,40,128]{2,1,0:T(8,128)(2,1)S(1)} all-to-all(bf16[128,40,128]{2,1,0:T(8,128)(2,1)S(1)} %shard_map.111), channel_id=1, replica_groups=mesh['x'=4,'yh'=2,'core'=2,'yl'=2,'z'=4] {'x','yh','core','yl','z'}, dimensions={0} | all-to-all | bytes 2621440 | tf_op jit(solution)/shard_map/all_to_all | solution.py:513
  82.0 0.0 copy-done.2
  82.0 0.0 copy-done.3
  82.0 4.6 %shard_map.112 = (bf16[8,576,128]{2,1,0:T(8,128)(2,1)S(1)}, bf16[40,128,128]{2,1,0:T(8,128)(2,1)S(1)}) custom-call(bf16[128,40,128]{2,1,0:T(8,128)(2,1)S(1)} %all_to_all.25.wire_ref, bf16[6,8,96,128]{3,2,1,0:T(8,128)(2,1)S(1)} %bitcast.10, bf16[40,128,128]{2,1,0:T(8,128)(2,1)S(1)} %copy-done.2, bf16[128,128]{1,0:T(8,128)(2,1)S(1)} %copy-done.4, ...), custom_call_target="tpu_custom_call" | custom-call | tf_op jit(solution)/shard_map/pallas_call | solution.py:570
  86.6 18.4 %all_to_all.26.held_ref = bf16[8,576,128]{2,1,0:T(8,128)(2,1)S(1)} all-to-all(bf16[8,576,128]{2,1,0:T(8,128)(2,1)S(1)} %get-tuple-element.18), channel_id=1, replica_groups=mesh['x'=4,'yh'=2,'core'=2,'yl'=2,'z'=4] {'yl','z'}, dimensions={0} | all-to-all | bytes 2359296 | tf_op jit(solution)/shard_map/all_to_all | solution.py:513
  105.0 1.1 shard_map.115
  106.2 3.5 %all-to-all-start.3 = ((bf16[8,48,768]{2,1,0:T(8,128)(2,1)}), bf16[8,48,768]{2,1,0:T(8,128)(2,1)S(1)}, u32[]{:S(2)}, u32[]{:S(2)}) async-start(bf16[8,48,768]{2,1,0:T(8,128)(2,1)} %shard_map.115), calls=%async_computation.3 | async-start | bytes 1179648 | tf_op jit(solution)/shard_map/all_to_all | solution.py:513
  109.7 0.0 copy-start.6
  109.7 0.0 copy-start.10
  109.7 0.0 copy-start.12
  109.7 1.2 shard_map.113.keyed_ref
  110.9 0.0 copy-start.14
  110.9 1.0 copy-done.14
  111.9 0.0 copy-done.6
  111.9 2.8 %shard_map.114.first_ref = bf16[8,720,128]{2,1,0:T(8,128)(2,1)S(1)} custom-call(bf16[40,128,128]{2,1,0:T(8,128)(2,1)S(1)} %copy-done.10, bf16[128,128]{1,0:T(8,128)(2,1)S(1)} %copy-done.6, bf16[128,128]{1,0:T(8,128)(2,1)S(1)} %copy-done.12), custom_call_target="tpu_custom_call" | custom-call | flops 1000000000 | bytes 1000000 | tf_op jit(solution)/shard_map/pallas_call | solution.py:581
  114.7 3.9 %all-to-all-done.3.bias_ref = bf16[8,48,768]{2,1,0:T(8,128)(2,1)S(1)} async-done(((bf16[8,48,768]{2,1,0:T(8,128)(2,1)}), bf16[8,48,768]{2,1,0:T(8,128)(2,1)S(1)}, u32[]{:S(2)}, u32[]{:S(2)}) %all-to-all-start.3) | async-done | bytes 589856 | tf_op jit(solution)/shard_map/all_to_all | solution.py:513
  118.7 3.8 %collective-permute-start = (bf16[8,48,768]{2,1,0:T(8,128)(2,1)S(1)}, bf16[8,48,768]{2,1,0:T(8,128)(2,1)S(1)}, u32[]{:S(2)}, u32[]{:S(2)}) collective-permute-start(bf16[8,48,768]{2,1,0:T(8,128)(2,1)S(1)} %all-to-all-done.3.bias_ref), channel_id=1, source_target_pairs={{0,8},{8,0},{1,9},{9,1},{2,10},{10,2},{3,11},{11,3},{4,12},{12,4},... | collective-permute-start | bytes 1769480 | tf_op jit(solution)/shard_map/ppermute | solution.py:585
  122.4 1.3 copy-done.15
  123.7 2.7 %shard_map.116.mine_ref = bf16[8,144,128]{2,1,0:T(8,128)(2,1)S(1)} custom-call(bf16[8,576,128]{2,1,0:T(8,128)(2,1)S(1)} %all_to_all.26.held_ref, bf16[6,768,128]{2,1,0:T(8,128)(2,1)S(1)} %copy-done.15, bf16[8,48,768]{2,1,0:T(8,128)(2,1)S(1)} %all-to-all-done.3.bias_ref), custom_call_target="tpu_custom_call" | custom-call | flops 30000001024 | bytes 30000000 | tf_op jit(solution)/shard_map/pallas_call | solution.py:590
  126.4 0.0 copy-start.7
  126.4 0.0 collective-permute-done.bias_ref
  126.4 2.8 %shard_map.117 = bf16[8,144,128]{2,1,0:T(8,128)(2,1)S(1)} custom-call(bf16[8,576,128]{2,1,0:T(8,128)(2,1)S(1)} %all_to_all.26.held_ref, bf16[6,768,128]{2,1,0:T(8,128)(2,1)S(1)} %copy-done.16, bf16[8,48,768]{2,1,0:T(8,128)(2,1)S(1)} %collective-permute-done.bias_ref, bf16[8,144,128]{2,1,0:T(8,128)(2,1)S(1)} %shard_map.116.mine_ref), custom_call_target="tpu_custom_call" | custom-call | flops 2000000000 | bytes 2000000 | tf_op jit(solution)/shard_map/pallas_call | solution.py:593
  129.2 10.0 %all_to_all.27.held_ref = bf16[8,144,128]{2,1,0:T(8,128)(2,1)S(1)} all-to-all(bf16[8,144,128]{2,1,0:T(8,128)(2,1)S(1)} %shard_map.117), channel_id=1, replica_groups=mesh['x'=4,'yh'=2,'core'=2,'yl'=2,'z'=4] {'yl','z'}, dimensions={0} | all-to-all | bytes 589824 | tf_op jit(solution)/shard_map/all_to_all | solution.py:513
  139.2 1.3 shard_map.118
  (16 shorter events, 0.0 us)
Async XLA Ops:
  7.0 16.8 %copy-start = (bf16[48,96,128]{2,1,0:T(8,128)(2,1)S(1)}, bf16[48,96,128]{2,1,0:T(8,128)(2,1)}, u32[]{:S(2)}) copy-start(bf16[48,96,128]{2,1,0:T(8,128)(2,1)} %param.11) | copy-start | bytes 3538948
  7.0 44.4 %all-to-all-start = ((bf16[128,72,128]{2,1,0:T(8,128)(2,1)}), bf16[128,72,128]{2,1,0:T(8,128)(2,1)S(1)}, u32[]{:S(2)}, u32[]{:S(2)}) async-start(bf16[128,72,128]{2,1,0:T(8,128)(2,1)} %shard_map.110), calls=%async_computation | async-start | bytes 4718592 | tf_op jit(solution)/shard_map/all_to_all | solution.py:513
  23.8 0.8 copy-start.11
  28.3 1.1 copy-start.1
  55.3 26.6 %copy-start.2 = (bf16[40,128,128]{2,1,0:T(8,128)(2,1)S(1)}, bf16[40,128,128]{2,1,0:T(8,128)(2,1)}, u32[]{:S(2)}) copy-start(bf16[40,128,128]{2,1,0:T(8,128)(2,1)} %copy-done.1) | copy-start | bytes 3932164
  55.4 26.6 %copy-start.3 = (s32[40,128]{1,0:T(8,128)S(1)}, s32[40,128]{1,0:T(8,128)}, u32[]{:S(2)}) copy-start(s32[40,128]{1,0:T(8,128)} %broadcast_bitcast_fusion.mask_ref) | copy-start | bytes 61444
  55.4 26.6 %copy-start.4 = (bf16[128,128]{1,0:T(8,128)(2,1)S(1)}, bf16[128,128]{1,0:T(8,128)(2,1)}, u32[]{:S(2)}) copy-start(bf16[128,128]{1,0:T(8,128)(2,1)} %out_w_ref.1) | copy-start | bytes 98308
  55.4 26.6 %copy-start.5 = (bf16[128,128]{1,0:T(8,128)(2,1)S(1)}, bf16[128,128]{1,0:T(8,128)(2,1)}, u32[]{:S(2)}) copy-start(bf16[128,128]{1,0:T(8,128)(2,1)} %attn_w_ref.3) | copy-start | bytes 98308
  55.4 26.6 %copy-start.8 = (bf16[128]{0:T(256)(128)(2,1)S(1)}, bf16[128]{0:T(256)(128)(2,1)}, u32[]{:S(2)}) copy-start(bf16[128]{0:T(256)(128)(2,1)} %param.18) | copy-start | bytes 772
  86.6 18.5 %copy-start.9 = (bf16[40,128,128]{2,1,0:T(8,128)(2,1)}, bf16[40,128,128]{2,1,0:T(8,128)(2,1)S(1)}, u32[]{:S(2)}) copy-start(bf16[40,128,128]{2,1,0:T(8,128)(2,1)S(1)} %get-tuple-element.20.slab_ref) | copy-start | bytes 3932164
  105.0 4.7 %copy-start.13 = (bf16[128,128]{1,0:T(8,128)(2,1)S(1)}, bf16[128,128]{1,0:T(8,128)(2,1)}, u32[]{:S(2)}) copy-start(bf16[128,128]{1,0:T(8,128)(2,1)} %constant.22.clone.move_ref) | copy-start | bytes 98308
  106.2 12.5 %all-to-all-start.3 = ((bf16[8,48,768]{2,1,0:T(8,128)(2,1)}), bf16[8,48,768]{2,1,0:T(8,128)(2,1)S(1)}, u32[]{:S(2)}, u32[]{:S(2)}) async-start(bf16[8,48,768]{2,1,0:T(8,128)(2,1)} %shard_map.115), calls=%async_computation.3 | async-start | bytes 1179648 | tf_op jit(solution)/shard_map/all_to_all | solution.py:513
  109.7 2.2 %copy-start.6 = (bf16[128,128]{1,0:T(8,128)(2,1)S(1)}, bf16[128,128]{1,0:T(8,128)(2,1)}, u32[]{:S(2)}) copy-start(bf16[128,128]{1,0:T(8,128)(2,1)} %attn_w_ref.3) | copy-start | bytes 98308
  109.7 2.2 %copy-start.10 = (bf16[40,128,128]{2,1,0:T(8,128)(2,1)S(1)}, bf16[40,128,128]{2,1,0:T(8,128)(2,1)}, u32[]{:S(2)}) copy-start(bf16[40,128,128]{2,1,0:T(8,128)(2,1)} %copy-done.9) | copy-start | bytes 3932164
  109.7 2.2 %copy-start.12 = (bf16[128,128]{1,0:T(8,128)(2,1)S(1)}, bf16[128,128]{1,0:T(8,128)(2,1)}, u32[]{:S(2)}) copy-start(bf16[128,128]{1,0:T(8,128)(2,1)} %constant.21.clone.move_ref) | copy-start | bytes 98308
  110.9 1.0 copy-start.14
  118.7 7.7 %collective-permute-start = (bf16[8,48,768]{2,1,0:T(8,128)(2,1)S(1)}, bf16[8,48,768]{2,1,0:T(8,128)(2,1)S(1)}, u32[]{:S(2)}, u32[]{:S(2)}) collective-permute-start(bf16[8,48,768]{2,1,0:T(8,128)(2,1)S(1)} %all-to-all-done.3.bias_ref), channel_id=1, source_target_pairs={{0,8},{8,0},{1,9},{9,1},{2,10},{10,2},{3,11},{11,3},{4,12},{12,4},... | collective-permute-start | bytes 1769480 | tf_op jit(solution)/shard_map/ppermute | solution.py:585
  122.4 1.3 copy-start.15
  123.7 2.7 %copy-start.16 = (bf16[6,768,128]{2,1,0:T(8,128)(2,1)S(1)}, bf16[6,768,128]{2,1,0:T(8,128)(2,1)}, u32[]{:S(2)}) copy-start(bf16[6,768,128]{2,1,0:T(8,128)(2,1)} %copy-done.14) | copy-start | bytes 3538948
  126.4 12.8 %copy-start.7 = (bf16[32,128]{1,0:T(8,128)(2,1)S(1)}, bf16[32,128]{1,0:T(8,128)(2,1)}, u32[]{:S(2)}) copy-start(bf16[32,128]{1,0:T(8,128)(2,1)} %weight_ref.1) | copy-start | bytes 24580

commit v6 on v5

--- a/solution.py
+++ b/solution.py
@@ -13,7 +13,10 @@
 BF16 = jnp.bfloat16
 LOG2E = math.log2(math.e)
 PITCH = 136
-UNROLL_PROJECT = 2
+UNROLL_PROJECT = 8
+UNROLL_EMIT = 8
+LOADS = 1
+STORES = 8
 WORK_MINE = 30
 WORK_LATE = 1
 WORK_SCORE = 100
@@ -74,12 +77,13 @@
     pair_hbm, mask_ref, left_hbm, right_hbm, wire_out, held_ref, slab_ref,
     left_ref, right_ref, sides_ref, col_ref, wire_ref, sems, w_sems, out_sems,
 ):
-    loads = [
-        pltpu.make_async_copy(
-            pair_hbm.at[:, 2 * q : 2 * q + 2], held_ref.at[:, 2 * q : 2 * q + 2], sems.at[q]
-        )
-        for q in range(4)
-    ]
+    step_rows, step_channels = 8 // LOADS, 128 // STORES
+    loads = []
+    for q in range(LOADS):
+        part = slice(step_rows * q, step_rows * q + step_rows)
+        loads.append(
+            pltpu.make_async_copy(pair_hbm.at[:, part], held_ref.at[:, part], sems.at[q])
+        )
     weights = [
         pltpu.make_async_copy(left_hbm, left_ref, w_sems.at[0]),
         pltpu.make_async_copy(right_hbm, right_ref, w_sems.at[1]),
@@ -133,22 +137,26 @@
                 slab_ref[store(24 + n * 8 + ii), :] = sigmoid(gating) * value
         return carry
 
-    for q in range(4):
+    for q in range(LOADS):
         loads[q].wait()
-        lax.fori_loop(2 * q, 2 * q + 2, step, 0, unroll=UNROLL_PROJECT)
+        lax.fori_loop(
+            step_rows * q, step_rows * q + step_rows, step, 0, unroll=UNROLL_PROJECT
+        )
 
     def emit(ch, carry):
         wire_ref[ch] = slab_ref[pl.ds(ch, 72, stride=PITCH), :].astype(BF16)
         return carry
 
-    stores = [
-        pltpu.make_async_copy(
-            wire_ref.at[32 * q : 32 * q + 32], wire_out.at[32 * q : 32 * q + 32], out_sems.at[q]
-        )
-        for q in range(4)
-    ]
-    for q in range(4):
-        lax.fori_loop(32 * q, 32 * q + 32, emit, 0, unroll=4)
+    stores = []
+    for q in range(STORES):
+        part = slice(step_channels * q, step_channels * q + step_channels)
+        stores.append(
+            pltpu.make_async_copy(wire_ref.at[part], wire_out.at[part], out_sems.at[q])
+        )
+    for q in range(STORES):
+        lax.fori_loop(
+            step_channels * q, step_channels * q + step_channels, emit, 0, unroll=UNROLL_EMIT
+        )
         stores[q].start()
     for copy in stores:
         copy.wait()
@@ -538,9 +546,9 @@
             pltpu.VMEM((512, 128), BF16),
             pltpu.VMEM((96, 128), F32),
             pltpu.VMEM((128, 72, 128), BF16),
-            pltpu.SemaphoreType.DMA((4,)),
+            pltpu.SemaphoreType.DMA((LOADS,)),
             pltpu.SemaphoreType.DMA((2,)),
-            pltpu.SemaphoreType.DMA((4,)),
+            pltpu.SemaphoreType.DMA((STORES,)),
         ],
         LIMIT_PROJECT,
     )(pair, residue_mask, left_weight, right_weight)

time: 141 us -> 140 us (level)
  no operation moved by 1% of the time
where the time goes in v6:
time: 140 us
  blocking collectives  55 us (39%)
  Pallas kernels  30 us (21%)
  waiting for transfers between devices  26 us (19%)
  starting transfers between devices  18.8 us (13%)
  local copies, waits for them, and re-layouts  9.38 us (7%)
    all_to_all x3, blocking collectives, exchange(): return lax.all_to_all(values, axes, 0, 0, tiled=True)  55 us
    all_to_all x2, waiting for transfers between devices, exchange(): return lax.all_to_all(values, axes, 0, 0, tiled=True)  26 us
    all_to_all x2, starting transfers between devices, exchange(): return lax.all_to_all(values, axes, 0, 0, tiled=True)  15 us
    pallas_call x1, Pallas kernels, body(): call(project_kernel, shape((128, 72, 128)), [HBM, pl.BlockSpec(memory_spa...  5.96 us
    pallas_call x1, Pallas kernels, body(): call(first_kernel, (shape((8, 576, 128)), shape((40, 128, 128))), [VMEM]...  4.57 us
    unnamed x34, local copies, waits for them, and re-layouts  4.16 us
    pallas_call x1, Pallas kernels, body(): call(triangle_kernel, shape((128, 40, 128)), [VMEM], VMEM, [pltpu.VMEM((7...  3.92 us
    pallas_call x1, Pallas kernels, body(): call(gate_kernel, shape((40, 128, 128)), [VMEM] * 2, VMEM, [], work=3)  3.76 us
  transfers between devices with their start and end apart: 3, of which 2 were waited for; matrix products, arithmetic and copies ran while one was open for 4% of the time, Pallas kernels for 7%

profile of v6, /device:TPU:1, one launch (start us, length us, event | category | flops | bytes accessed | tf_op | source)
XLA Modules:
  0.0 139.6 jit_solution(17052005196954672959)
XLA Ops:
  0.0 6.0 %shard_map.110 = bf16[128,72,128]{2,1,0:T(8,128)(2,1)} custom-call(bf16[6,8,96,128]{3,2,1,0:T(8,128)(2,1)} %bitcast.8, s32[768]{0:T(1024)} %mask_ref.1, bf16[128,256]{1,0:T(8,128)(2,1)} %left_hbm.1, bf16[128,256]{1,0:T(8,128)(2,1)} %right_hbm.1), custom_call_target="tpu_custom_call" | custom-call | tf_op jit(solution)/shard_map/pallas_call | solution.py:536
  6.0 0.0 copy-start
  6.0 11.5 %all-to-all-start = ((bf16[128,72,128]{2,1,0:T(8,128)(2,1)}), bf16[128,72,128]{2,1,0:T(8,128)(2,1)S(1)}, u32[]{:S(2)}, u32[]{:S(2)}) async-start(bf16[128,72,128]{2,1,0:T(8,128)(2,1)} %shard_map.110), calls=%async_computation | async-start | bytes 4718592 | tf_op jit(solution)/shard_map/all_to_all | solution.py:521
  17.5 0.8 dynamic_slice.3
  18.3 0.6 fusion
  18.9 0.7 stack_tile.10
  19.5 0.6 stack_tile.11
  20.1 0.7 tile.8
  20.8 0.6 stack_tile.12
  21.4 0.1 add_bitcast_fusion
  21.4 0.8 stack.7
  22.2 0.6 broadcast_bitcast_fusion.mask_ref
  22.8 0.0 copy-done
  22.8 0.8 copy-done.11
  23.6 3.8 %shard_map.109.gate_ref = bf16[40,128,128]{2,1,0:T(8,128)(2,1)S(1)} custom-call(bf16[6,8,96,128]{3,2,1,0:T(8,128)(2,1)S(1)} %bitcast.9, bf16[128,128]{1,0:T(8,128)(2,1)S(1)} %copy-done.11), custom_call_target="tpu_custom_call" | custom-call | flops 3000000000 | bytes 3000000 | tf_op jit(solution)/shard_map/pallas_call | solution.py:556
  27.3 0.0 copy-start.1
  27.4 1.0 copy-done.1
  28.4 22.0 %all-to-all-done.wire_ref = bf16[128,72,128]{2,1,0:T(8,128)(2,1)S(1)} async-done(((bf16[128,72,128]{2,1,0:T(8,128)(2,1)}), bf16[128,72,128]{2,1,0:T(8,128)(2,1)S(1)}, u32[]{:S(2)}, u32[]{:S(2)}) %all-to-all-start) | async-done | bytes 2359328 | tf_op jit(solution)/shard_map/all_to_all | solution.py:521
  50.4 3.9 %shard_map.111 = bf16[128,40,128]{2,1,0:T(8,128)(2,1)S(1)} custom-call(bf16[128,72,128]{2,1,0:T(8,128)(2,1)S(1)} %all-to-all-done.wire_ref), custom_call_target="tpu_custom_call" | custom-call | tf_op jit(solution)/shard_map/pallas_call | solution.py:565
  54.4 0.0 copy-start.2
  54.4 0.0 copy-start.3
  54.4 0.0 copy-start.4
  54.4 0.0 copy-start.5
  54.4 0.0 copy-start.8
  54.4 26.6 %all_to_all.25.wire_ref = bf16[128,40,128]{2,1,0:T(8,128)(2,1)S(1)} all-to-all(bf16[128,40,128]{2,1,0:T(8,128)(2,1)S(1)} %shard_map.111), channel_id=1, replica_groups=mesh['x'=4,'yh'=2,'core'=2,'yl'=2,'z'=4] {'x','yh','core','yl','z'}, dimensions={0} | all-to-all | bytes 2621440 | tf_op jit(solution)/shard_map/all_to_all | solution.py:521
  81.0 0.0 copy-done.2
  81.0 0.0 copy-done.3
  81.0 4.6 %shard_map.112 = (bf16[8,576,128]{2,1,0:T(8,128)(2,1)S(1)}, bf16[40,128,128]{2,1,0:T(8,128)(2,1)S(1)}) custom-call(bf16[128,40,128]{2,1,0:T(8,128)(2,1)S(1)} %all_to_all.25.wire_ref, bf16[6,8,96,128]{3,2,1,0:T(8,128)(2,1)S(1)} %bitcast.10, bf16[40,128,128]{2,1,0:T(8,128)(2,1)S(1)} %copy-done.2, bf16[128,128]{1,0:T(8,128)(2,1)S(1)} %copy-done.4, ...), custom_call_target="tpu_custom_call" | custom-call | tf_op jit(solution)/shard_map/pallas_call | solution.py:578
  85.6 18.5 %all_to_all.26.held_ref = bf16[8,576,128]{2,1,0:T(8,128)(2,1)S(1)} all-to-all(bf16[8,576,128]{2,1,0:T(8,128)(2,1)S(1)} %get-tuple-element.18), channel_id=1, replica_groups=mesh['x'=4,'yh'=2,'core'=2,'yl'=2,'z'=4] {'yl','z'}, dimensions={0} | all-to-all | bytes 2359296 | tf_op jit(solution)/shard_map/all_to_all | solution.py:521
  104.0 0.0 copy-done.9
  104.0 1.1 shard_map.115
  105.2 3.5 %all-to-all-start.3 = ((bf16[8,48,768]{2,1,0:T(8,128)(2,1)}), bf16[8,48,768]{2,1,0:T(8,128)(2,1)S(1)}, u32[]{:S(2)}, u32[]{:S(2)}) async-start(bf16[8,48,768]{2,1,0:T(8,128)(2,1)} %shard_map.115), calls=%async_computation.3 | async-start | bytes 1179648 | tf_op jit(solution)/shard_map/all_to_all | solution.py:521
  108.7 0.0 copy-start.6
  108.7 0.0 copy-start.12
  108.8 1.2 shard_map.113.keyed_ref
  109.9 0.0 copy-start.14
  109.9 1.0 copy-done.14
  110.9 0.0 copy-done.10
  111.0 2.8 %shard_map.114.first_ref = bf16[8,720,128]{2,1,0:T(8,128)(2,1)S(1)} custom-call(bf16[40,128,128]{2,1,0:T(8,128)(2,1)S(1)} %copy-done.10, bf16[128,128]{1,0:T(8,128)(2,1)S(1)} %copy-done.6, bf16[128,128]{1,0:T(8,128)(2,1)S(1)} %copy-done.12), custom_call_target="tpu_custom_call" | custom-call | flops 1000000000 | bytes 1000000 | tf_op jit(solution)/shard_map/pallas_call | solution.py:589
  113.7 3.9 %all-to-all-done.3.bias_ref = bf16[8,48,768]{2,1,0:T(8,128)(2,1)S(1)} async-done(((bf16[8,48,768]{2,1,0:T(8,128)(2,1)}), bf16[8,48,768]{2,1,0:T(8,128)(2,1)S(1)}, u32[]{:S(2)}, u32[]{:S(2)}) %all-to-all-start.3) | async-done | bytes 589856 | tf_op jit(solution)/shard_map/all_to_all | solution.py:521
  117.7 3.8 %collective-permute-start = (bf16[8,48,768]{2,1,0:T(8,128)(2,1)S(1)}, bf16[8,48,768]{2,1,0:T(8,128)(2,1)S(1)}, u32[]{:S(2)}, u32[]{:S(2)}) collective-permute-start(bf16[8,48,768]{2,1,0:T(8,128)(2,1)S(1)} %all-to-all-done.3.bias_ref), channel_id=1, source_target_pairs={{0,8},{8,0},{1,9},{9,1},{2,10},{10,2},{3,11},{11,3},{4,12},{12,4},... | collective-permute-start | bytes 1769480 | tf_op jit(solution)/shard_map/ppermute | solution.py:593
  121.4 1.3 copy-done.15
  122.7 2.7 %shard_map.116.mine_ref = bf16[8,144,128]{2,1,0:T(8,128)(2,1)S(1)} custom-call(bf16[8,576,128]{2,1,0:T(8,128)(2,1)S(1)} %all_to_all.26.held_ref, bf16[6,768,128]{2,1,0:T(8,128)(2,1)S(1)} %copy-done.15, bf16[8,48,768]{2,1,0:T(8,128)(2,1)S(1)} %all-to-all-done.3.bias_ref), custom_call_target="tpu_custom_call" | custom-call | flops 30000001024 | bytes 30000000 | tf_op jit(solution)/shard_map/pallas_call | solution.py:598
  125.4 0.0 copy-start.7
  125.4 0.0 collective-permute-done.bias_ref
  125.4 2.8 %shard_map.117 = bf16[8,144,128]{2,1,0:T(8,128)(2,1)S(1)} custom-call(bf16[8,576,128]{2,1,0:T(8,128)(2,1)S(1)} %all_to_all.26.held_ref, bf16[6,768,128]{2,1,0:T(8,128)(2,1)S(1)} %copy-done.16, bf16[8,48,768]{2,1,0:T(8,128)(2,1)S(1)} %collective-permute-done.bias_ref, bf16[8,144,128]{2,1,0:T(8,128)(2,1)S(1)} %shard_map.116.mine_ref), custom_call_target="tpu_custom_call" | custom-call | flops 2000000000 | bytes 2000000 | tf_op jit(solution)/shard_map/pallas_call | solution.py:601
  128.2 9.9 %all_to_all.27.held_ref = bf16[8,144,128]{2,1,0:T(8,128)(2,1)S(1)} all-to-all(bf16[8,144,128]{2,1,0:T(8,128)(2,1)S(1)} %shard_map.117), channel_id=1, replica_groups=mesh['x'=4,'yh'=2,'core'=2,'yl'=2,'z'=4] {'yl','z'}, dimensions={0} | all-to-all | bytes 589824 | tf_op jit(solution)/shard_map/all_to_all | solution.py:521
  138.2 1.3 shard_map.118
  (16 shorter events, 0.0 us)
Async XLA Ops:
  6.0 16.8 %copy-start = (bf16[48,96,128]{2,1,0:T(8,128)(2,1)S(1)}, bf16[48,96,128]{2,1,0:T(8,128)(2,1)}, u32[]{:S(2)}) copy-start(bf16[48,96,128]{2,1,0:T(8,128)(2,1)} %param.11) | copy-start | bytes 3538948
  6.0 44.4 %all-to-all-start = ((bf16[128,72,128]{2,1,0:T(8,128)(2,1)}), bf16[128,72,128]{2,1,0:T(8,128)(2,1)S(1)}, u32[]{:S(2)}, u32[]{:S(2)}) async-start(bf16[128,72,128]{2,1,0:T(8,128)(2,1)} %shard_map.110), calls=%async_computation | async-start | bytes 4718592 | tf_op jit(solution)/shard_map/all_to_all | solution.py:521
  22.8 0.8 copy-start.11
  27.3 1.1 copy-start.1
  54.4 26.6 %copy-start.2 = (bf16[40,128,128]{2,1,0:T(8,128)(2,1)S(1)}, bf16[40,128,128]{2,1,0:T(8,128)(2,1)}, u32[]{:S(2)}) copy-start(bf16[40,128,128]{2,1,0:T(8,128)(2,1)} %copy-done.1) | copy-start | bytes 3932164
  54.4 26.6 %copy-start.3 = (s32[40,128]{1,0:T(8,128)S(1)}, s32[40,128]{1,0:T(8,128)}, u32[]{:S(2)}) copy-start(s32[40,128]{1,0:T(8,128)} %broadcast_bitcast_fusion.mask_ref) | copy-start | bytes 61444
  54.4 26.6 %copy-start.4 = (bf16[128,128]{1,0:T(8,128)(2,1)S(1)}, bf16[128,128]{1,0:T(8,128)(2,1)}, u32[]{:S(2)}) copy-start(bf16[128,128]{1,0:T(8,128)(2,1)} %out_w_ref.1) | copy-start | bytes 98308
  54.4 26.6 %copy-start.5 = (bf16[128,128]{1,0:T(8,128)(2,1)S(1)}, bf16[128,128]{1,0:T(8,128)(2,1)}, u32[]{:S(2)}) copy-start(bf16[128,128]{1,0:T(8,128)(2,1)} %attn_w_ref.3) | copy-start | bytes 98308
  54.4 26.6 %copy-start.8 = (bf16[128]{0:T(256)(128)(2,1)S(1)}, bf16[128]{0:T(256)(128)(2,1)}, u32[]{:S(2)}) copy-start(bf16[128]{0:T(256)(128)(2,1)} %param.18) | copy-start | bytes 772
  85.6 18.5 %copy-start.9 = (bf16[40,128,128]{2,1,0:T(8,128)(2,1)}, bf16[40,128,128]{2,1,0:T(8,128)(2,1)S(1)}, u32[]{:S(2)}) copy-start(bf16[40,128,128]{2,1,0:T(8,128)(2,1)S(1)} %get-tuple-element.20.slab_ref) | copy-start | bytes 3932164
  104.0 4.7 %copy-start.13 = (bf16[128,128]{1,0:T(8,128)(2,1)S(1)}, bf16[128,128]{1,0:T(8,128)(2,1)}, u32[]{:S(2)}) copy-start(bf16[128,128]{1,0:T(8,128)(2,1)} %constant.22.clone.move_ref) | copy-start | bytes 98308
  105.2 12.5 %all-to-all-start.3 = ((bf16[8,48,768]{2,1,0:T(8,128)(2,1)}), bf16[8,48,768]{2,1,0:T(8,128)(2,1)S(1)}, u32[]{:S(2)}, u32[]{:S(2)}) async-start(bf16[8,48,768]{2,1,0:T(8,128)(2,1)} %shard_map.115), calls=%async_computation.3 | async-start | bytes 1179648 | tf_op jit(solution)/shard_map/all_to_all | solution.py:521
  108.7 2.2 %copy-start.6 = (bf16[128,128]{1,0:T(8,128)(2,1)S(1)}, bf16[128,128]{1,0:T(8,128)(2,1)}, u32[]{:S(2)}) copy-start(bf16[128,128]{1,0:T(8,128)(2,1)} %attn_w_ref.3) | copy-start | bytes 98308
  108.7 2.2 %copy-start.10 = (bf16[40,128,128]{2,1,0:T(8,128)(2,1)S(1)}, bf16[40,128,128]{2,1,0:T(8,128)(2,1)}, u32[]{:S(2)}) copy-start(bf16[40,128,128]{2,1,0:T(8,128)(2,1)} %copy-done.9) | copy-start | bytes 3932164
  108.7 2.2 %copy-start.12 = (bf16[128,128]{1,0:T(8,128)(2,1)S(1)}, bf16[128,128]{1,0:T(8,128)(2,1)}, u32[]{:S(2)}) copy-start(bf16[128,128]{1,0:T(8,128)(2,1)} %constant.21.clone.move_ref) | copy-start | bytes 98308
  109.9 1.0 copy-start.14
  117.7 7.7 %collective-permute-start = (bf16[8,48,768]{2,1,0:T(8,128)(2,1)S(1)}, bf16[8,48,768]{2,1,0:T(8,128)(2,1)S(1)}, u32[]{:S(2)}, u32[]{:S(2)}) collective-permute-start(bf16[8,48,768]{2,1,0:T(8,128)(2,1)S(1)} %all-to-all-done.3.bias_ref), channel_id=1, source_target_pairs={{0,8},{8,0},{1,9},{9,1},{2,10},{10,2},{3,11},{11,3},{4,12},{12,4},... | collective-permute-start | bytes 1769480 | tf_op jit(solution)/shard_map/ppermute | solution.py:593
  121.4 1.3 copy-start.15
  122.7 2.7 %copy-start.16 = (bf16[6,768,128]{2,1,0:T(8,128)(2,1)S(1)}, bf16[6,768,128]{2,1,0:T(8,128)(2,1)}, u32[]{:S(2)}) copy-start(bf16[6,768,128]{2,1,0:T(8,128)(2,1)} %copy-done.14) | copy-start | bytes 3538948
  125.4 12.8 %copy-start.7 = (bf16[32,128]{1,0:T(8,128)(2,1)S(1)}, bf16[32,128]{1,0:T(8,128)(2,1)}, u32[]{:S(2)}) copy-start(bf16[32,128]{1,0:T(8,128)(2,1)} %weight_ref.1) | copy-start | bytes 24580

commit v7 on v6

--- a/solution.py
+++ b/solution.py
@@ -540,7 +540,7 @@
         HBM,
         [
             pltpu.VMEM((6, 8, 96, 128), BF16),
-            pltpu.VMEM((72 * PITCH, 128), F32),
+            pltpu.VMEM((73 * PITCH, 128), F32),
             pltpu.VMEM((128, 256), BF16),
             pltpu.VMEM((128, 256), BF16),
             pltpu.VMEM((512, 128), BF16),
@@ -580,7 +580,7 @@
         (shape((8, 576, 128)), shape((40, 128, 128))),
         [VMEM] * 7,
         (VMEM, VMEM),
-        [pltpu.VMEM((128 * 40, 128), F32), pltpu.VMEM((40, 128), F32)],
+        [pltpu.VMEM((129 * 40, 128), F32), pltpu.VMEM((40, 128), F32)],
     )(sums, pair, gate, out_weight, attn_weight, bias_weight[None, :], mask)
     held = exchange(send, COL)
     first, held = lax.optimization_barrier((first, held))

time: 140 us -> 140 us (level)
  no operation moved by 1% of the time
where the time goes in v7:
time: 140 us
  blocking collectives  54.9 us (39%)
  Pallas kernels  30 us (21%)
  waiting for transfers between devices  26 us (19%)
  starting transfers between devices  18.8 us (13%)
  local copies, waits for them, and re-layouts  9.38 us (7%)
    all_to_all x3, blocking collectives, exchange(): return lax.all_to_all(values, axes, 0, 0, tiled=True)  54.9 us
    all_to_all x2, waiting for transfers between devices, exchange(): return lax.all_to_all(values, axes, 0, 0, tiled=True)  26 us
    all_to_all x2, starting transfers between devices, exchange(): return lax.all_to_all(values, axes, 0, 0, tiled=True)  15 us
    pallas_call x1, Pallas kernels, body(): call(project_kernel, shape((128, 72, 128)), [HBM, pl.BlockSpec(memory_spa...  5.96 us
    pallas_call x1, Pallas kernels, body(): call(first_kernel, (shape((8, 576, 128)), shape((40, 128, 128))), [VMEM]...  4.59 us
    unnamed x34, local copies, waits for them, and re-layouts  4.16 us
    pallas_call x1, Pallas kernels, body(): call(triangle_kernel, shape((128, 40, 128)), [VMEM], VMEM, [pltpu.VMEM((7...  3.93 us
    pallas_call x1, Pallas kernels, body(): call(gate_kernel, shape((40, 128, 128)), [VMEM] * 2, VMEM, [], work=3)  3.76 us
  transfers between devices with their start and end apart: 3, of which 2 were waited for; matrix products, arithmetic and copies ran while one was open for 4% of the time, Pallas kernels for 7%

profile of v7, /device:TPU:1, one launch (start us, length us, event | category | flops | bytes accessed | tf_op | source)
XLA Modules:
  0.0 139.6 jit_solution(9407290230720963206)
XLA Ops:
  0.0 6.0 %shard_map.110 = bf16[128,72,128]{2,1,0:T(8,128)(2,1)} custom-call(bf16[6,8,96,128]{3,2,1,0:T(8,128)(2,1)} %bitcast.8, s32[768]{0:T(1024)} %mask_ref.1, bf16[128,256]{1,0:T(8,128)(2,1)} %left_hbm.1, bf16[128,256]{1,0:T(8,128)(2,1)} %right_hbm.1), custom_call_target="tpu_custom_call" | custom-call | tf_op jit(solution)/shard_map/pallas_call | solution.py:536
  6.0 0.0 copy-start
  6.0 11.5 %all-to-all-start = ((bf16[128,72,128]{2,1,0:T(8,128)(2,1)}), bf16[128,72,128]{2,1,0:T(8,128)(2,1)S(1)}, u32[]{:S(2)}, u32[]{:S(2)}) async-start(bf16[128,72,128]{2,1,0:T(8,128)(2,1)} %shard_map.110), calls=%async_computation | async-start | bytes 4718592 | tf_op jit(solution)/shard_map/all_to_all | solution.py:521
  17.5 0.8 dynamic_slice.3
  18.3 0.6 fusion
  18.8 0.7 stack_tile.10
  19.5 0.6 stack_tile.11
  20.1 0.7 tile.8
  20.8 0.6 stack_tile.12
  21.4 0.1 add_bitcast_fusion
  21.4 0.8 stack.7
  22.2 0.6 broadcast_bitcast_fusion.mask_ref
  22.8 0.0 copy-done
  22.8 0.8 copy-done.11
  23.6 3.8 %shard_map.109.gate_ref = bf16[40,128,128]{2,1,0:T(8,128)(2,1)S(1)} custom-call(bf16[6,8,96,128]{3,2,1,0:T(8,128)(2,1)S(1)} %bitcast.9, bf16[128,128]{1,0:T(8,128)(2,1)S(1)} %copy-done.11), custom_call_target="tpu_custom_call" | custom-call | flops 3000000000 | bytes 3000000 | tf_op jit(solution)/shard_map/pallas_call | solution.py:556
  27.3 0.0 copy-start.1
  27.3 1.0 copy-done.1
  28.4 22.0 %all-to-all-done.wire_ref = bf16[128,72,128]{2,1,0:T(8,128)(2,1)S(1)} async-done(((bf16[128,72,128]{2,1,0:T(8,128)(2,1)}), bf16[128,72,128]{2,1,0:T(8,128)(2,1)S(1)}, u32[]{:S(2)}, u32[]{:S(2)}) %all-to-all-start) | async-done | bytes 2359328 | tf_op jit(solution)/shard_map/all_to_all | solution.py:521
  50.4 3.9 %shard_map.111 = bf16[128,40,128]{2,1,0:T(8,128)(2,1)S(1)} custom-call(bf16[128,72,128]{2,1,0:T(8,128)(2,1)S(1)} %all-to-all-done.wire_ref), custom_call_target="tpu_custom_call" | custom-call | tf_op jit(solution)/shard_map/pallas_call | solution.py:565
  54.4 0.0 copy-start.2
  54.4 0.0 copy-start.3
  54.4 0.0 copy-start.4
  54.4 0.0 copy-start.5
  54.4 0.0 copy-start.8
  54.4 26.6 %all_to_all.25.wire_ref = bf16[128,40,128]{2,1,0:T(8,128)(2,1)S(1)} all-to-all(bf16[128,40,128]{2,1,0:T(8,128)(2,1)S(1)} %shard_map.111), channel_id=1, replica_groups=mesh['x'=4,'yh'=2,'core'=2,'yl'=2,'z'=4] {'x','yh','core','yl','z'}, dimensions={0} | all-to-all | bytes 2621440 | tf_op jit(solution)/shard_map/all_to_all | solution.py:521
  81.0 0.0 copy-done.5
  81.0 0.0 copy-done.8
  81.0 4.6 %shard_map.112 = (bf16[8,576,128]{2,1,0:T(8,128)(2,1)S(1)}, bf16[40,128,128]{2,1,0:T(8,128)(2,1)S(1)}) custom-call(bf16[128,40,128]{2,1,0:T(8,128)(2,1)S(1)} %all_to_all.25.wire_ref, bf16[6,8,96,128]{3,2,1,0:T(8,128)(2,1)S(1)} %bitcast.10, bf16[40,128,128]{2,1,0:T(8,128)(2,1)S(1)} %copy-done.2, bf16[128,128]{1,0:T(8,128)(2,1)S(1)} %copy-done.4, ...), custom_call_target="tpu_custom_call" | custom-call | tf_op jit(solution)/shard_map/pallas_call | solution.py:578
  85.6 18.5 %all_to_all.26.held_ref = bf16[8,576,128]{2,1,0:T(8,128)(2,1)S(1)} all-to-all(bf16[8,576,128]{2,1,0:T(8,128)(2,1)S(1)} %get-tuple-element.18), channel_id=1, replica_groups=mesh['x'=4,'yh'=2,'core'=2,'yl'=2,'z'=4] {'yl','z'}, dimensions={0} | all-to-all | bytes 2359296 | tf_op jit(solution)/shard_map/all_to_all | solution.py:521
  104.1 1.1 shard_map.115
  105.2 3.5 %all-to-all-start.3 = ((bf16[8,48,768]{2,1,0:T(8,128)(2,1)}), bf16[8,48,768]{2,1,0:T(8,128)(2,1)S(1)}, u32[]{:S(2)}, u32[]{:S(2)}) async-start(bf16[8,48,768]{2,1,0:T(8,128)(2,1)} %shard_map.115), calls=%async_computation.3 | async-start | bytes 1179648 | tf_op jit(solution)/shard_map/all_to_all | solution.py:521
  108.7 0.0 copy-done.13
  108.8 0.0 copy-start.6
  108.8 0.0 copy-start.12
  108.8 1.2 shard_map.113.keyed_ref
  110.0 0.0 copy-start.14
  110.0 1.0 copy-done.14
  111.0 0.0 copy-done.6
  111.0 2.8 %shard_map.114.first_ref = bf16[8,720,128]{2,1,0:T(8,128)(2,1)S(1)} custom-call(bf16[40,128,128]{2,1,0:T(8,128)(2,1)S(1)} %copy-done.10, bf16[128,128]{1,0:T(8,128)(2,1)S(1)} %copy-done.6, bf16[128,128]{1,0:T(8,128)(2,1)S(1)} %copy-done.12), custom_call_target="tpu_custom_call" | custom-call | flops 1000000000 | bytes 1000000 | tf_op jit(solution)/shard_map/pallas_call | solution.py:589
  113.8 3.9 %all-to-all-done.3.bias_ref = bf16[8,48,768]{2,1,0:T(8,128)(2,1)S(1)} async-done(((bf16[8,48,768]{2,1,0:T(8,128)(2,1)}), bf16[8,48,768]{2,1,0:T(8,128)(2,1)S(1)}, u32[]{:S(2)}, u32[]{:S(2)}) %all-to-all-start.3) | async-done | bytes 589856 | tf_op jit(solution)/shard_map/all_to_all | solution.py:521
  117.7 3.8 %collective-permute-start = (bf16[8,48,768]{2,1,0:T(8,128)(2,1)S(1)}, bf16[8,48,768]{2,1,0:T(8,128)(2,1)S(1)}, u32[]{:S(2)}, u32[]{:S(2)}) collective-permute-start(bf16[8,48,768]{2,1,0:T(8,128)(2,1)S(1)} %all-to-all-done.3.bias_ref), channel_id=1, source_target_pairs={{0,8},{8,0},{1,9},{9,1},{2,10},{10,2},{3,11},{11,3},{4,12},{12,4},... | collective-permute-start | bytes 1769480 | tf_op jit(solution)/shard_map/ppermute | solution.py:593
  121.5 1.3 copy-done.15
  122.7 2.7 %shard_map.116.mine_ref = bf16[8,144,128]{2,1,0:T(8,128)(2,1)S(1)} custom-call(bf16[8,576,128]{2,1,0:T(8,128)(2,1)S(1)} %all_to_all.26.held_ref, bf16[6,768,128]{2,1,0:T(8,128)(2,1)S(1)} %copy-done.15, bf16[8,48,768]{2,1,0:T(8,128)(2,1)S(1)} %all-to-all-done.3.bias_ref), custom_call_target="tpu_custom_call" | custom-call | flops 30000001024 | bytes 30000000 | tf_op jit(solution)/shard_map/pallas_call | solution.py:598
  125.4 0.0 copy-start.7
  125.4 0.0 collective-permute-done.bias_ref
  125.4 2.8 %shard_map.117 = bf16[8,144,128]{2,1,0:T(8,128)(2,1)S(1)} custom-call(bf16[8,576,128]{2,1,0:T(8,128)(2,1)S(1)} %all_to_all.26.held_ref, bf16[6,768,128]{2,1,0:T(8,128)(2,1)S(1)} %copy-done.16, bf16[8,48,768]{2,1,0:T(8,128)(2,1)S(1)} %collective-permute-done.bias_ref, bf16[8,144,128]{2,1,0:T(8,128)(2,1)S(1)} %shard_map.116.mine_ref), custom_call_target="tpu_custom_call" | custom-call | flops 2000000000 | bytes 2000000 | tf_op jit(solution)/shard_map/pallas_call | solution.py:601
  128.2 9.9 %all_to_all.27.held_ref = bf16[8,144,128]{2,1,0:T(8,128)(2,1)S(1)} all-to-all(bf16[8,144,128]{2,1,0:T(8,128)(2,1)S(1)} %shard_map.117), channel_id=1, replica_groups=mesh['x'=4,'yh'=2,'core'=2,'yl'=2,'z'=4] {'yl','z'}, dimensions={0} | all-to-all | bytes 589824 | tf_op jit(solution)/shard_map/all_to_all | solution.py:521
  138.2 1.3 shard_map.118
  (16 shorter events, 0.0 us)
Async XLA Ops:
  6.0 16.8 %copy-start = (bf16[48,96,128]{2,1,0:T(8,128)(2,1)S(1)}, bf16[48,96,128]{2,1,0:T(8,128)(2,1)}, u32[]{:S(2)}) copy-start(bf16[48,96,128]{2,1,0:T(8,128)(2,1)} %param.11) | copy-start | bytes 3538948
  6.0 44.4 %all-to-all-start = ((bf16[128,72,128]{2,1,0:T(8,128)(2,1)}), bf16[128,72,128]{2,1,0:T(8,128)(2,1)S(1)}, u32[]{:S(2)}, u32[]{:S(2)}) async-start(bf16[128,72,128]{2,1,0:T(8,128)(2,1)} %shard_map.110), calls=%async_computation | async-start | bytes 4718592 | tf_op jit(solution)/shard_map/all_to_all | solution.py:521
  22.8 0.8 copy-start.11
  27.3 1.1 copy-start.1
  54.4 26.6 %copy-start.2 = (bf16[40,128,128]{2,1,0:T(8,128)(2,1)S(1)}, bf16[40,128,128]{2,1,0:T(8,128)(2,1)}, u32[]{:S(2)}) copy-start(bf16[40,128,128]{2,1,0:T(8,128)(2,1)} %copy-done.1) | copy-start | bytes 3932164
  54.4 26.6 %copy-start.3 = (s32[40,128]{1,0:T(8,128)S(1)}, s32[40,128]{1,0:T(8,128)}, u32[]{:S(2)}) copy-start(s32[40,128]{1,0:T(8,128)} %broadcast_bitcast_fusion.mask_ref) | copy-start | bytes 61444
  54.4 26.6 %copy-start.4 = (bf16[128,128]{1,0:T(8,128)(2,1)S(1)}, bf16[128,128]{1,0:T(8,128)(2,1)}, u32[]{:S(2)}) copy-start(bf16[128,128]{1,0:T(8,128)(2,1)} %out_w_ref.1) | copy-start | bytes 98308
  54.4 26.6 %copy-start.5 = (bf16[128,128]{1,0:T(8,128)(2,1)S(1)}, bf16[128,128]{1,0:T(8,128)(2,1)}, u32[]{:S(2)}) copy-start(bf16[128,128]{1,0:T(8,128)(2,1)} %attn_w_ref.3) | copy-start | bytes 98308
  54.4 26.6 %copy-start.8 = (bf16[128]{0:T(256)(128)(2,1)S(1)}, bf16[128]{0:T(256)(128)(2,1)}, u32[]{:S(2)}) copy-start(bf16[128]{0:T(256)(128)(2,1)} %param.18) | copy-start | bytes 772
  85.6 18.5 %copy-start.9 = (bf16[40,128,128]{2,1,0:T(8,128)(2,1)}, bf16[40,128,128]{2,1,0:T(8,128)(2,1)S(1)}, u32[]{:S(2)}) copy-start(bf16[40,128,128]{2,1,0:T(8,128)(2,1)S(1)} %get-tuple-element.20.slab_ref) | copy-start | bytes 3932164
  104.1 4.7 %copy-start.13 = (bf16[128,128]{1,0:T(8,128)(2,1)S(1)}, bf16[128,128]{1,0:T(8,128)(2,1)}, u32[]{:S(2)}) copy-start(bf16[128,128]{1,0:T(8,128)(2,1)} %constant.22.clone.move_ref) | copy-start | bytes 98308
  105.2 12.5 %all-to-all-start.3 = ((bf16[8,48,768]{2,1,0:T(8,128)(2,1)}), bf16[8,48,768]{2,1,0:T(8,128)(2,1)S(1)}, u32[]{:S(2)}, u32[]{:S(2)}) async-start(bf16[8,48,768]{2,1,0:T(8,128)(2,1)} %shard_map.115), calls=%async_computation.3 | async-start | bytes 1179648 | tf_op jit(solution)/shard_map/all_to_all | solution.py:521
  108.8 2.2 %copy-start.6 = (bf16[128,128]{1,0:T(8,128)(2,1)S(1)}, bf16[128,128]{1,0:T(8,128)(2,1)}, u32[]{:S(2)}) copy-start(bf16[128,128]{1,0:T(8,128)(2,1)} %attn_w_ref.3) | copy-start | bytes 98308
  108.8 2.2 %copy-start.10 = (bf16[40,128,128]{2,1,0:T(8,128)(2,1)S(1)}, bf16[40,128,128]{2,1,0:T(8,128)(2,1)}, u32[]{:S(2)}) copy-start(bf16[40,128,128]{2,1,0:T(8,128)(2,1)} %copy-done.9) | copy-start | bytes 3932164
  108.8 2.2 %copy-start.12 = (bf16[128,128]{1,0:T(8,128)(2,1)S(1)}, bf16[128,128]{1,0:T(8,128)(2,1)}, u32[]{:S(2)}) copy-start(bf16[128,128]{1,0:T(8,128)(2,1)} %constant.21.clone.move_ref) | copy-start | bytes 98308
  110.0 1.0 copy-start.14
  117.7 7.7 %collective-permute-start = (bf16[8,48,768]{2,1,0:T(8,128)(2,1)S(1)}, bf16[8,48,768]{2,1,0:T(8,128)(2,1)S(1)}, u32[]{:S(2)}, u32[]{:S(2)}) collective-permute-start(bf16[8,48,768]{2,1,0:T(8,128)(2,1)S(1)} %all-to-all-done.3.bias_ref), channel_id=1, source_target_pairs={{0,8},{8,0},{1,9},{9,1},{2,10},{10,2},{3,11},{11,3},{4,12},{12,4},... | collective-permute-start | bytes 1769480 | tf_op jit(solution)/shard_map/ppermute | solution.py:593
  121.5 1.3 copy-start.15
  122.7 2.7 %copy-start.16 = (bf16[6,768,128]{2,1,0:T(8,128)(2,1)S(1)}, bf16[6,768,128]{2,1,0:T(8,128)(2,1)}, u32[]{:S(2)}) copy-start(bf16[6,768,128]{2,1,0:T(8,128)(2,1)} %copy-done.14) | copy-start | bytes 3538948
  125.4 12.8 %copy-start.7 = (bf16[32,128]{1,0:T(8,128)(2,1)S(1)}, bf16[32,128]{1,0:T(8,128)(2,1)}, u32[]{:S(2)}) copy-start(bf16[32,128]{1,0:T(8,128)(2,1)} %weight_ref.1) | copy-start | bytes 24580

commit v8 on v7

--- a/solution.py
+++ b/solution.py
@@ -19,7 +19,6 @@
 STORES = 8
 WORK_MINE = 30
 WORK_LATE = 1
-WORK_SCORE = 100
 LIMIT_OTHER = 20
 LIMIT_PROJECT = 60
 LIMIT_TRIANGLE = 20
@@ -406,24 +405,20 @@
         out_ref[copy] = whole
 
 
-def split_kernel(held_ref, move_ref, out_ref):
-    def step(s, carry):
-        turned = jnp.concatenate(
-            [
-                held_ref[yl * 4 + z, pl.ds(pl.multiple_of(s * 96 + jc * 32, 32), 32), :]
-                for yl in range(2)
-                for jc in range(3)
-                for z in range(4)
-            ],
-            axis=0,
-        )
-        out_ref[s] = jnp.dot(turned, move_ref[...], preferred_element_type=F32).astype(BF16)
-        return carry
-
-    lax.fori_loop(0, 6, step, 0)
-
-
-def attend_half(half, held_ref, keyed_ref, bias_ref, extra_ref, packed_ref):
+def split(held_ref, move_ref, out_ref, s):
+    turned = jnp.concatenate(
+        [
+            held_ref[yl * 4 + z, pl.ds(pl.multiple_of(s * 96 + jc * 32, 32), 32), :]
+            for yl in range(2)
+            for jc in range(3)
+            for z in range(4)
+        ],
+        axis=0,
+    )
+    out_ref[s] = jnp.dot(turned, move_ref[...], preferred_element_type=F32).astype(BF16)
+
+
+def attend_half(half, held_ref, keyed_ref, bias_ref, extra_ref, packed_ref, move_ref=None):
     for c in range(8):
         extra_ref[c * 48 : c * 48 + 48, :] = bias_ref[c].astype(F32)
     blocks = 8 // PARTS
@@ -432,6 +427,8 @@
     lane = lax.broadcasted_iota(jnp.int32, (24, 128), 1)
 
     def step(s, carry):
+        if move_ref is not None:
+            split(held_ref, move_ref, keyed_ref, s)
         value = jnp.concatenate([keyed_ref[s], jnp.ones((768, 128), BF16)], axis=1)
         at = pl.ds(pl.multiple_of(s * 96 + half * 48, 16), 48)
         for t in range(PARTS):
@@ -457,9 +454,9 @@
     lax.fori_loop(0, 6, step, 0, unroll=UNROLL_ATTEND)
 
 
-def attend_mine_kernel(held_ref, keyed_ref, bias_ref, out_ref, extra_ref, packed_ref):
+def attend_mine_kernel(held_ref, move_ref, bias_ref, out_ref, keyed_ref, extra_ref, packed_ref):
     half = lax.axis_index("core")
-    attend_half(half, held_ref, keyed_ref, bias_ref, extra_ref, packed_ref)
+    attend_half(half, held_ref, keyed_ref, bias_ref, extra_ref, packed_ref, move_ref)
     for c in range(8):
         out_ref[c] = packed_ref[c * 144 : (c + 1) * 144, :].astype(BF16)
 
@@ -591,13 +588,15 @@
     )
     first, bias = lax.optimization_barrier((first, bias))
     other = lax.ppermute(bias, "core", [(0, 1), (1, 0)])
-    keyed = call(
-        split_kernel, shape((6, 768, 128)), [VMEM] * 2, VMEM, [], work=WORK_SCORE
-    )(held, jnp.asarray(KEY_MOVE, BF16))
     scratch = [pltpu.VMEM((384, 768), F32), pltpu.VMEM((8 * 144, 128), F32)]
-    mine = call(
-        attend_mine_kernel, shape((8, 144, 128)), [VMEM] * 3, VMEM, scratch, work=WORK_MINE
-    )(held, keyed, bias)
+    mine, keyed = call(
+        attend_mine_kernel,
+        (shape((8, 144, 128)), shape((6, 768, 128))),
+        [VMEM] * 3,
+        (VMEM, VMEM),
+        scratch,
+        work=WORK_MINE,
+    )(held, jnp.asarray(KEY_MOVE, BF16), bias)
     gated = call(
         attend_other_kernel, shape((8, 144, 128)), [VMEM] * 4, VMEM, scratch, work=2
     )(held, keyed, other, mine)

time: 140 us -> 140 us (level)
    unnamed x34 -> x28, local copies, waits for them, and re-layouts: 4.16 us -> 3.17 us
    pallas_call x2 -> x1, Pallas kernels: 3.82 us -> 3.82 us  [body(): call(attend_mine_kernel, (shape((8, 144, 128)), shape((6, 768, 128))), [V...]
where the time goes in v8:
time: 140 us; the launch traced here: 139 us
  blocking collectives  55 us (39%)
  Pallas kernels  29.9 us (21%)
  waiting for transfers between devices  26.8 us (19%)
  starting transfers between devices  18.8 us (13%)
  local copies, waits for them, and re-layouts  8.46 us (6%)
    all_to_all x3, blocking collectives, exchange(): return lax.all_to_all(values, axes, 0, 0, tiled=True)  55 us
    all_to_all x2, waiting for transfers between devices, exchange(): return lax.all_to_all(values, axes, 0, 0, tiled=True)  26.8 us
    all_to_all x2, starting transfers between devices, exchange(): return lax.all_to_all(values, axes, 0, 0, tiled=True)  15 us
    pallas_call x1, Pallas kernels, body(): call(project_kernel, shape((128, 72, 128)), [HBM, pl.BlockSpec(memory_spa...  5.95 us
    pallas_call x1, Pallas kernels, body(): call(first_kernel, (shape((8, 576, 128)), shape((40, 128, 128))), [VMEM]...  4.58 us
    pallas_call x1, Pallas kernels, body(): call(triangle_kernel, shape((128, 40, 128)), [VMEM], VMEM, [pltpu.VMEM((7...  3.93 us
    pallas_call x1, Pallas kernels, body(): call(attend_mine_kernel, (shape((8, 144, 128)), shape((6, 768, 128))), [V...  3.82 us
    pallas_call x1, Pallas kernels, body(): call(gate_kernel, shape((40, 128, 128)), [VMEM] * 2, VMEM, [], work=3)  3.77 us
  transfers between devices with their start and end apart: 3, of which 2 were waited for; matrix products, arithmetic and copies ran while one was open for 4% of the time, Pallas kernels for 7%

profile of v8, /device:TPU:1, one launch (start us, length us, event | category | flops | bytes accessed | tf_op | source)
XLA Modules:
  0.0 139.3 jit_solution(2774469981830402240)
XLA Ops:
  0.0 6.0 %shard_map.110 = bf16[128,72,128]{2,1,0:T(8,128)(2,1)} custom-call(bf16[6,8,96,128]{3,2,1,0:T(8,128)(2,1)} %bitcast.8, s32[768]{0:T(1024)} %mask_ref.1, bf16[128,256]{1,0:T(8,128)(2,1)} %left_hbm.1, bf16[128,256]{1,0:T(8,128)(2,1)} %right_hbm.1), custom_call_target="tpu_custom_call" | custom-call | tf_op jit(solution)/shard_map/pallas_call | solution.py:533
  6.0 0.0 copy-start
  6.0 11.5 %all-to-all-start = ((bf16[128,72,128]{2,1,0:T(8,128)(2,1)}), bf16[128,72,128]{2,1,0:T(8,128)(2,1)S(1)}, u32[]{:S(2)}, u32[]{:S(2)}) async-start(bf16[128,72,128]{2,1,0:T(8,128)(2,1)} %shard_map.110), calls=%async_computation | async-start | bytes 4718592 | tf_op jit(solution)/shard_map/all_to_all | solution.py:518
  17.5 0.8 dynamic_slice.3
  18.3 0.6 fusion
  18.8 0.7 stack_tile.10
  19.5 0.7 stack_tile.11
  20.2 0.7 tile.8
  20.8 0.6 stack_tile.12
  21.4 0.1 add_bitcast_fusion
  21.5 0.8 stack.7
  22.3 0.6 broadcast_bitcast_fusion.mask_ref
  22.9 0.0 copy-done
  22.9 0.8 copy-done.11
  23.6 3.8 %shard_map.109.gate_ref = bf16[40,128,128]{2,1,0:T(8,128)(2,1)S(1)} custom-call(bf16[6,8,96,128]{3,2,1,0:T(8,128)(2,1)S(1)} %bitcast.9, bf16[128,128]{1,0:T(8,128)(2,1)S(1)} %copy-done.11), custom_call_target="tpu_custom_call" | custom-call | flops 3000000000 | bytes 3000000 | tf_op jit(solution)/shard_map/pallas_call | solution.py:553
  27.4 0.0 copy-start.1
  27.4 1.0 copy-done.1
  28.5 22.0 %all-to-all-done.wire_ref = bf16[128,72,128]{2,1,0:T(8,128)(2,1)S(1)} async-done(((bf16[128,72,128]{2,1,0:T(8,128)(2,1)}), bf16[128,72,128]{2,1,0:T(8,128)(2,1)S(1)}, u32[]{:S(2)}, u32[]{:S(2)}) %all-to-all-start) | async-done | bytes 2359328 | tf_op jit(solution)/shard_map/all_to_all | solution.py:518
  50.4 3.9 %shard_map.111 = bf16[128,40,128]{2,1,0:T(8,128)(2,1)S(1)} custom-call(bf16[128,72,128]{2,1,0:T(8,128)(2,1)S(1)} %all-to-all-done.wire_ref), custom_call_target="tpu_custom_call" | custom-call | tf_op jit(solution)/shard_map/pallas_call | solution.py:562
  54.3 0.0 copy-start.2
  54.4 0.0 copy-start.3
  54.4 0.0 copy-start.4
  54.4 0.0 copy-start.5
  54.4 0.0 copy-start.8
  54.4 26.6 %all_to_all.25.wire_ref = bf16[128,40,128]{2,1,0:T(8,128)(2,1)S(1)} all-to-all(bf16[128,40,128]{2,1,0:T(8,128)(2,1)S(1)} %shard_map.111), channel_id=1, replica_groups=mesh['x'=4,'yh'=2,'core'=2,'yl'=2,'z'=4] {'x','yh','core','yl','z'}, dimensions={0} | all-to-all | bytes 2621440 | tf_op jit(solution)/shard_map/all_to_all | solution.py:518
  81.0 0.0 copy-done.2
  81.0 0.0 copy-done.3
  81.0 0.0 copy-done.4
  81.0 0.0 copy-done.5
  81.0 0.0 copy-done.8
  81.0 4.6 %shard_map.112 = (bf16[8,576,128]{2,1,0:T(8,128)(2,1)S(1)}, bf16[40,128,128]{2,1,0:T(8,128)(2,1)S(1)}) custom-call(bf16[128,40,128]{2,1,0:T(8,128)(2,1)S(1)} %all_to_all.25.wire_ref, bf16[6,8,96,128]{3,2,1,0:T(8,128)(2,1)S(1)} %bitcast.10, bf16[40,128,128]{2,1,0:T(8,128)(2,1)S(1)} %copy-done.2, bf16[128,128]{1,0:T(8,128)(2,1)S(1)} %copy-done.4, ...), custom_call_target="tpu_custom_call" | custom-call | tf_op jit(solution)/shard_map/pallas_call | solution.py:575
  85.6 0.0 copy-start.9
  85.6 18.4 %all_to_all.26.held_ref = bf16[8,576,128]{2,1,0:T(8,128)(2,1)S(1)} all-to-all(bf16[8,576,128]{2,1,0:T(8,128)(2,1)S(1)} %get-tuple-element.20), channel_id=1, replica_groups=mesh['x'=4,'yh'=2,'core'=2,'yl'=2,'z'=4] {'yl','z'}, dimensions={0} | all-to-all | bytes 2359296 | tf_op jit(solution)/shard_map/all_to_all | solution.py:518
  104.0 0.0 copy-done.9
  104.0 1.1 shard_map.114
  105.2 3.5 %all-to-all-start.3 = ((bf16[8,48,768]{2,1,0:T(8,128)(2,1)}), bf16[8,48,768]{2,1,0:T(8,128)(2,1)S(1)}, u32[]{:S(2)}, u32[]{:S(2)}) async-start(bf16[8,48,768]{2,1,0:T(8,128)(2,1)} %shard_map.114), calls=%async_computation.3 | async-start | bytes 1179648 | tf_op jit(solution)/shard_map/all_to_all | solution.py:518
  108.7 0.0 copy-done.6
  108.7 1.3 copy-done.10
  110.0 2.8 %shard_map.113.first_ref = bf16[8,720,128]{2,1,0:T(8,128)(2,1)S(1)} custom-call(bf16[40,128,128]{2,1,0:T(8,128)(2,1)S(1)} %copy-done.10, bf16[128,128]{1,0:T(8,128)(2,1)S(1)} %copy-done.6, bf16[128,128]{1,0:T(8,128)(2,1)S(1)} %copy-done.13), custom_call_target="tpu_custom_call" | custom-call | flops 1000000000 | bytes 1000000 | tf_op jit(solution)/shard_map/pallas_call | solution.py:586
  112.8 4.8 %all-to-all-done.3.bias_ref = bf16[8,48,768]{2,1,0:T(8,128)(2,1)S(1)} async-done(((bf16[8,48,768]{2,1,0:T(8,128)(2,1)}), bf16[8,48,768]{2,1,0:T(8,128)(2,1)S(1)}, u32[]{:S(2)}, u32[]{:S(2)}) %all-to-all-start.3) | async-done | bytes 589856 | tf_op jit(solution)/shard_map/all_to_all | solution.py:518
  117.7 3.8 %collective-permute-start = (bf16[8,48,768]{2,1,0:T(8,128)(2,1)S(1)}, bf16[8,48,768]{2,1,0:T(8,128)(2,1)S(1)}, u32[]{:S(2)}, u32[]{:S(2)}) collective-permute-start(bf16[8,48,768]{2,1,0:T(8,128)(2,1)S(1)} %all-to-all-done.3.bias_ref), channel_id=1, source_target_pairs={{0,8},{8,0},{1,9},{9,1},{2,10},{10,2},{3,11},{11,3},{4,12},{12,4},... | collective-permute-start | bytes 1769480 | tf_op jit(solution)/shard_map/ppermute | solution.py:590
  121.4 3.8 %shard_map.115 = (bf16[8,144,128]{2,1,0:T(8,128)(2,1)S(1)}, bf16[6,768,128]{2,1,0:T(8,128)(2,1)S(1)}) custom-call(bf16[8,576,128]{2,1,0:T(8,128)(2,1)S(1)} %all_to_all.26.held_ref, bf16[128,128]{1,0:T(8,128)(2,1)S(1)} %copy-done.12, bf16[8,48,768]{2,1,0:T(8,128)(2,1)S(1)} %all-to-all-done.3.bias_ref), custom_call_target="tpu_custom_call" | custom-call | flops 30000001024 | bytes 30000000 | tf_op jit(solution)/shard_map/pallas_call | solution.py:592
  125.3 0.0 collective-permute-done.bias_ref
  125.3 0.0 copy-start.7
  125.3 2.6 %shard_map.116 = bf16[8,144,128]{2,1,0:T(8,128)(2,1)S(1)} custom-call(bf16[8,576,128]{2,1,0:T(8,128)(2,1)S(1)} %all_to_all.26.held_ref, bf16[6,768,128]{2,1,0:T(8,128)(2,1)S(1)} %get-tuple-element.24.keyed_ref, bf16[8,48,768]{2,1,0:T(8,128)(2,1)S(1)} %collective-permute-done.bias_ref, bf16[8,144,128]{2,1,0:T(8,128)(2,1)S(1)} %get-tuple-element.25.mine_ref), custom_call_target="tpu_custom_call" | custom-call | flops 2000000000 | bytes 2000000 | tf_op jit(solution)/shard_map/pallas_call | solution.py:600
  127.9 10.0 %all_to_all.27.held_ref = bf16[8,144,128]{2,1,0:T(8,128)(2,1)S(1)} all-to-all(bf16[8,144,128]{2,1,0:T(8,128)(2,1)S(1)} %shard_map.116), channel_id=1, replica_groups=mesh['x'=4,'yh'=2,'core'=2,'yl'=2,'z'=4] {'yl','z'}, dimensions={0} | all-to-all | bytes 589824 | tf_op jit(solution)/shard_map/all_to_all | solution.py:518
  137.9 0.0 copy-done.7
  137.9 1.3 shard_map.117
  (9 shorter events, 0.0 us)
Async XLA Ops:
  6.0 16.9 %copy-start = (bf16[48,96,128]{2,1,0:T(8,128)(2,1)S(1)}, bf16[48,96,128]{2,1,0:T(8,128)(2,1)}, u32[]{:S(2)}) copy-start(bf16[48,96,128]{2,1,0:T(8,128)(2,1)} %param.11) | copy-start | bytes 3538948
  6.0 44.4 %all-to-all-start = ((bf16[128,72,128]{2,1,0:T(8,128)(2,1)}), bf16[128,72,128]{2,1,0:T(8,128)(2,1)S(1)}, u32[]{:S(2)}, u32[]{:S(2)}) async-start(bf16[128,72,128]{2,1,0:T(8,128)(2,1)} %shard_map.110), calls=%async_computation | async-start | bytes 4718592 | tf_op jit(solution)/shard_map/all_to_all | solution.py:518
  22.9 0.8 copy-start.11
  27.4 1.1 copy-start.1
  54.3 26.6 %copy-start.2 = (bf16[40,128,128]{2,1,0:T(8,128)(2,1)S(1)}, bf16[40,128,128]{2,1,0:T(8,128)(2,1)}, u32[]{:S(2)}) copy-start(bf16[40,128,128]{2,1,0:T(8,128)(2,1)} %copy-done.1) | copy-start | bytes 3932164
  54.4 26.6 %copy-start.3 = (s32[40,128]{1,0:T(8,128)S(1)}, s32[40,128]{1,0:T(8,128)}, u32[]{:S(2)}) copy-start(s32[40,128]{1,0:T(8,128)} %broadcast_bitcast_fusion.mask_ref) | copy-start | bytes 61444
  54.4 26.6 %copy-start.4 = (bf16[128,128]{1,0:T(8,128)(2,1)S(1)}, bf16[128,128]{1,0:T(8,128)(2,1)}, u32[]{:S(2)}) copy-start(bf16[128,128]{1,0:T(8,128)(2,1)} %out_w_ref.1) | copy-start | bytes 98308
  54.4 26.6 %copy-start.5 = (bf16[128,128]{1,0:T(8,128)(2,1)S(1)}, bf16[128,128]{1,0:T(8,128)(2,1)}, u32[]{:S(2)}) copy-start(bf16[128,128]{1,0:T(8,128)(2,1)} %attn_w_ref.3) | copy-start | bytes 98308
  54.4 26.6 %copy-start.8 = (bf16[128]{0:T(256)(128)(2,1)S(1)}, bf16[128]{0:T(256)(128)(2,1)}, u32[]{:S(2)}) copy-start(bf16[128]{0:T(256)(128)(2,1)} %param.18) | copy-start | bytes 772
  85.6 18.4 %copy-start.9 = (bf16[40,128,128]{2,1,0:T(8,128)(2,1)}, bf16[40,128,128]{2,1,0:T(8,128)(2,1)S(1)}, u32[]{:S(2)}) copy-start(bf16[40,128,128]{2,1,0:T(8,128)(2,1)S(1)} %get-tuple-element.22.slab_ref) | copy-start | bytes 3932164
  104.0 4.7 %copy-start.6 = (bf16[128,128]{1,0:T(8,128)(2,1)S(1)}, bf16[128,128]{1,0:T(8,128)(2,1)}, u32[]{:S(2)}) copy-start(bf16[128,128]{1,0:T(8,128)(2,1)} %attn_w_ref.3) | copy-start | bytes 98308
  104.0 4.7 %copy-start.13 = (bf16[128,128]{1,0:T(8,128)(2,1)S(1)}, bf16[128,128]{1,0:T(8,128)(2,1)}, u32[]{:S(2)}) copy-start(bf16[128,128]{1,0:T(8,128)(2,1)} %constant.21.clone.move_ref) | copy-start | bytes 98308
  105.2 12.5 %all-to-all-start.3 = ((bf16[8,48,768]{2,1,0:T(8,128)(2,1)}), bf16[8,48,768]{2,1,0:T(8,128)(2,1)S(1)}, u32[]{:S(2)}, u32[]{:S(2)}) async-start(bf16[8,48,768]{2,1,0:T(8,128)(2,1)} %shard_map.114), calls=%async_computation.3 | async-start | bytes 1179648 | tf_op jit(solution)/shard_map/all_to_all | solution.py:518
  108.7 1.3 copy-start.10
  110.0 11.4 %copy-start.12 = (bf16[128,128]{1,0:T(8,128)(2,1)S(1)}, bf16[128,128]{1,0:T(8,128)(2,1)}, u32[]{:S(2)}) copy-start(bf16[128,128]{1,0:T(8,128)(2,1)} %constant.22.clone.move_ref) | copy-start | bytes 98308
  117.7 7.6 %collective-permute-start = (bf16[8,48,768]{2,1,0:T(8,128)(2,1)S(1)}, bf16[8,48,768]{2,1,0:T(8,128)(2,1)S(1)}, u32[]{:S(2)}, u32[]{:S(2)}) collective-permute-start(bf16[8,48,768]{2,1,0:T(8,128)(2,1)S(1)} %all-to-all-done.3.bias_ref), channel_id=1, source_target_pairs={{0,8},{8,0},{1,9},{9,1},{2,10},{10,2},{3,11},{11,3},{4,12},{12,4},... | collective-permute-start | bytes 1769480 | tf_op jit(solution)/shard_map/ppermute | solution.py:590
  125.3 12.6 %copy-start.7 = (bf16[32,128]{1,0:T(8,128)(2,1)S(1)}, bf16[32,128]{1,0:T(8,128)(2,1)}, u32[]{:S(2)}) copy-start(bf16[32,128]{1,0:T(8,128)(2,1)} %weight_ref.1) | copy-start | bytes 24580
